TPU v7x, 128 devices: a whole 4x4x4 slice. The times are simulated.
128 devices in a mesh: replica: 4 (over x), shard: 32 (over z, y, core).
Axes of the slice: x: 4, y: 4, z: 4, core: 2. Of those that a mesh axis runs over, the one named last changes fastest.
Arguments:
- grads: bfloat16 [4, 62914560], P('replica', 'shard'), may hold values from -3 to 3
- slot_table: int32 [32, 3], replicated, may hold values from -1 to 59, as said below
- left_factor: float32 [32, 3, 1024, 1024], P('shard', None, 'replica'), may hold values from -6 to 6
- right_factor: float32 [32, 3, 1024, 1024], P('shard', None, 'replica'), may hold values from -6 to 6
- left_root: bfloat16 [32, 3, 1024, 1024], P('shard', None, 'replica')
- right_root: bfloat16 [32, 3, 1024, 1024], P('shard', None, 'replica')
Outputs:
- new_left: float32 [32, 3, 1024, 1024], P('shard', None, 'replica')
- new_right: float32 [32, 3, 1024, 1024], P('shard', None, 'replica')
- update: bfloat16 [4, 62914560], P('replica', 'shard')
Inputs may be any that keep to these rules, and one draw needn't show every extreme that they name: slot_table[h, k] is a block number or -1 (empty slot); every block stands in exactly one slot; slot k of shard index h holds only blocks of block row (h + k) mod 4; some shard index has all 3 slots filled.
All inputs are finite; a program needn't handle non-finite values.
Results may differ from a plain program's by a relative error of at most 0.018.
Values may be sent and summed in bfloat16 or wider, within the bound.
A program may use at most 128 MiB of HBM per device.

v0:
```python
import jax
import jax.numpy as jnp
from jax import lax
from jax.sharding import PartitionSpec as P

ROWS = 4096
COLS = 15360
BLK = 1024


EPSILON = 1e-06


def pick_pieces(source, columns, live):
    taken = jnp.take(source, columns.reshape(-1), axis=1)
    taken = taken.reshape(source.shape[0], columns.shape[0], columns.shape[1], source.shape[2])
    taken = jnp.transpose(taken, (1, 2, 0, 3))
    return jnp.where(live[:, :, None, None], taken, jnp.zeros_like(taken))


def assemble(received, holder, slot_count, row_count, per_block):
    slot_ids = jnp.arange(slot_count)
    block_rows = (holder + slot_ids) % row_count
    positions = slot_ids // row_count
    sources = block_rows[:, None] * per_block + jnp.arange(per_block)[None, :]
    blocks = received[sources, positions[:, None]]
    return blocks.reshape(slot_count, per_block * received.shape[2], received.shape[3])


def on_device(grads, slot_table, left_factor, right_factor, left_root, right_root):
    shards = lax.axis_size("shard")
    replica_id = lax.axis_index("replica")
    shard_id = lax.axis_index("shard")
    slot_count = left_factor.shape[1]
    quarter = left_factor.shape[2]
    row_count = ROWS // BLK
    col_count = COLS // BLK
    rows_dev = ROWS // shards
    per_block = BLK // rows_dev
    capacity = (slot_count + row_count - 1) // row_count
    local = grads.reshape(rows_dev, col_count, BLK)
    my_row = shard_id // per_block
    holders = jnp.arange(shards)[:, None]
    positions = jnp.arange(capacity)[None, :]
    slot_out = positions * row_count + (my_row - holders) % row_count
    slot_fit = jnp.minimum(slot_out, slot_count - 1)
    block_out = slot_table[holders, slot_fit]
    live_out = (slot_out < slot_count) & (block_out >= 0)
    column_out = jnp.where(live_out, block_out % col_count, 0)
    pieces = pick_pieces(local, column_out, live_out)
    received = lax.all_to_all(pieces, "shard", split_axis=0, concat_axis=0, tiled=True)
    partial_value = assemble(received, shard_id, slot_count, row_count, per_block).astype(
        jnp.float32
    )
    owned = lax.psum_scatter(
        partial_value.astype(jnp.bfloat16), "replica", scatter_dimension=1, tiled=True
    )
    gradient = lax.all_gather(owned, "replica", axis=1, tiled=True)
    begin = replica_id * quarter
    grad_rows = lax.dynamic_slice_in_dim(gradient, begin, quarter, 1)
    grad_cols = lax.dynamic_slice_in_dim(gradient, begin, quarter, 2)
    new_left = (
        left_factor[0]
        + jnp.einsum("sab,scb->sac", grad_rows, gradient, preferred_element_type=jnp.float32) / BLK
    )
    new_right = (
        right_factor[0]
        + jnp.einsum("saq,sab->sqb", grad_cols, gradient, preferred_element_type=jnp.float32) / BLK
    )
    precond = jnp.einsum(
        "sab,sqb->saq", gradient, right_root[0], preferred_element_type=jnp.float32
    ).astype(jnp.bfloat16)
    left_rows = left_root[0]
    direction = jnp.einsum(
        "sqa,sab->sqb",
        left_rows,
        lax.all_gather(precond, "replica", axis=2, tiled=True),
        preferred_element_type=jnp.float32,
    )
    grad_power = jnp.mean(jnp.square(gradient.astype(jnp.float32)), axis=(1, 2))
    direction_sum = lax.psum(jnp.sum(jnp.square(direction), axis=(1, 2)), "replica")
    direction_power = direction_sum / (BLK * BLK)
    factor = jnp.sqrt(grad_power) / jnp.sqrt(direction_power + EPSILON)
    grafted = (direction * factor[:, None, None]).astype(jnp.bfloat16)
    whole = lax.all_gather(grafted, "replica", axis=1, tiled=True)
    targets = jnp.arange(shards)[:, None]
    target_rows = targets // per_block
    target_sub = targets % per_block
    slot_back = positions * row_count + (target_rows - shard_id) % row_count
    back_fit = jnp.minimum(slot_back, slot_count - 1)
    block_back = slot_table[shard_id, back_fit]
    live_back = (slot_back < slot_count) & (block_back >= 0)
    divided = whole.reshape(slot_count, per_block, rows_dev, BLK)
    wanted = my_row * col_count + jnp.arange(col_count)
    match = slot_table.reshape(-1)[None, :] == wanted[:, None]
    cells = jnp.sum(jnp.where(match, jnp.arange(shards * slot_count)[None, :], 0), axis=1)
    from_holder = cells // slot_count
    from_place = cells % slot_count // row_count
    outgoing = divided[back_fit, target_sub]
    outgoing = jnp.where(live_back[:, :, None, None], outgoing, jnp.zeros_like(outgoing))
    incoming = lax.all_to_all(outgoing, "shard", split_axis=0, concat_axis=0, tiled=True)
    placed = incoming[from_holder, from_place]
    update = jnp.transpose(placed, (1, 0, 2)).reshape(1, rows_dev * col_count * BLK)
    return (new_left[None], new_right[None], update)


def solution(mesh):
    in_specs = (
        P("replica", "shard"),
        P(),
        P("shard", None, "replica", None),
        P("shard", None, "replica", None),
        P("shard", None, "replica", None),
        P("shard", None, "replica", None),
    )
    out_specs = (
        P("shard", None, "replica", None),
        P("shard", None, "replica", None),
        P("replica", "shard"),
    )
    return jax.shard_map(
        on_device, mesh=mesh, in_specs=in_specs, out_specs=out_specs, check_vma=False
    )
```

profile of v0, /device:TPU:0, one launch (start us, length us, event | category | flops | bytes accessed | tf_op | source)
XLA Modules:
  0.0 702.4 jit_solution(10935409090893214855)
XLA Ops:
  7.3 1.5 gather_fusion
  8.8 84.5 %reduce.1 = bf16[1966080]{0:T(1024)(128)(2,1)} reduce(bf16[1,1966080]{1,0:T(2,128)(2,1)} %param.6, bf16[]{:T(256)} %constant.247), dimensions={0}, to_apply=%param.6.reduce_sub_computation | reduce | bytes 7864322 | tf_op args[0]
  93.3 7.6 %reshape.622 = bf16[128,15,1024]{2,1,0:T(8,128)(2,1)} reshape(bf16[1966080]{0:T(1024)(128)(2,1)} %reduce.1) | data formatting | bytes 7864320 | tf_op jit(solution)/shard_map/reshape | solution.py:41
  100.9 6.4 copy.27
  107.3 7.0 %gather_fusion.1 = bf16[32,128,1024]{2,1,0:T(8,128)(2,1)} fusion(bf16[128,15,1024]{2,0,1:T(8,128)(2,1)} %copy.27, s32[1024]{0:T(1024)S(1)} %pad_clamp_fusion), kind=kCustom, calls=%fused_computation.1 | custom fusion | bytes 16777344 | tf_op jit(solution)/shard_map/jit(_take)/gather | solution.py:15
  114.3 7.6 %fusion.1 = bf16[32,1,128,1024]{3,2,1,0:T(8,128)(2,1)} fusion(bf16[32,128,1024]{2,1,0:T(8,128)(2,1)} %gather_fusion.1, pred[32]{0:T(512)(128)(4,1)S(1)} %get-tuple-element.3, pred[32]{0:T(512)(128)(4,1)S(1)} %get-tuple-element.4), kind=kLoop, calls=%fused_computation.9 | loop fusion | flops 8388608 | bytes 16777280 | tf_op jit(solution)/shard_map/jit(_where)/select_n | solution.py:18
  121.9 8.6 %all-to-all-start = ((bf16[32,1,128,1024]{3,2,1,0:T(8,128)(2,1)}), bf16[32,1,128,1024]{3,2,1,0:T(8,128)(2,1)}, u32[]{:S(2)}, u32[]{:S(2)}) async-start(bf16[32,1,128,1024]{3,2,1,0:T(8,128)(2,1)} %fusion.1), calls=%async_computation | async-start | bytes 16777216 | tf_op jit(solution)/shard_map/all_to_all | solution.py:51
  130.5 0.2 reduce-scatter.2.cloned.1.call-start
  130.9 105.5 %all-to-all-done = bf16[32,1,128,1024]{3,2,1,0:T(8,128)(2,1)} async-done(((bf16[32,1,128,1024]{3,2,1,0:T(8,128)(2,1)}), bf16[32,1,128,1024]{3,2,1,0:T(8,128)(2,1)}, u32[]{:S(2)}, u32[]{:S(2)}) %all-to-all-start) | async-done | bytes 8388640 | tf_op jit(solution)/shard_map/all_to_all | solution.py:51
  236.4 7.9 %gather_fusion.2 = bf16[24,128,1024]{2,1,0:T(8,128)(2,1)} fusion(bf16[32,1,128,1024]{3,2,1,0:T(8,128)(2,1)} %all-to-all-done, s32[24]{0:T(128)S(1)} %reshape.642), kind=kCustom, calls=%fused_computation.2 | custom fusion | bytes 12583104 | tf_op jit(solution)/shard_map/gather | solution.py:26
  244.3 60.7 %reduce-scatter.2.cloned.1.call-done = bf16[3,256,1024]{2,1,0:T(8,128)(2,1)} async-done(((bf16[3,1024,1024]{2,1,0:T(8,128)(2,1)}), bf16[3,256,1024]{2,1,0:T(8,128)(2,1)}) %reduce-scatter.2.cloned.1.call-update) | async-done | bytes 1572880 | tf_op jit(solution)/shard_map/reduce_scatter | solution.py:55
  305.1 67.0 %all-gather.4.cloned.1.call-done = bf16[3,1024,1024]{2,1,0:T(8,128)(2,1)} async-done(((bf16[3,256,1024]{2,1,0:T(8,128)(2,1)}), bf16[3,1024,1024]{2,1,0:T(8,128)(2,1)}) %all-gather.4.cloned.1.call-update) | async-done | bytes 6291472 | tf_op jit(solution)/shard_map/all_gather | solution.py:58
  372.1 5.8 convolution_convert_fusion
  377.9 4.4 multiply_reduce_fusion
  382.4 66.1 %all-gather.6.cloned.1.call-done = bf16[3,1024,1024]{2,1,0:T(8,128)(2,1)} async-done(((bf16[3,1024,256]{2,1,0:T(8,128)(2,1)}), bf16[3,1024,1024]{2,1,0:T(8,128)(2,1)}) %all-gather.6.cloned.1.call-update) | async-done | bytes 6291472 | tf_op jit(solution)/shard_map/all_gather | solution.py:77
  448.4 6.8 multiply_reduce_fusion.1
  455.2 9.7 %psum.7 = f32[3]{0:T(128)S(1)} all-reduce(f32[3]{0:T(128)S(1)} %get-tuple-element.7), channel_id=1, replica_groups=mesh['replica'=4,'shard'=32] {'replica'}, use_global_device_ids=true, to_apply=%region_3.4 | all-reduce | flops 3 | bytes 24 | tf_op jit(solution)/shard_map/psum | solution.py:81
  464.9 3.4 fusion.5
  468.4 0.8 gather_fusion.3
  469.2 68.1 %all-gather.8.cloned.1.call-done = bf16[3,1024,1024]{1,2,0:T(8,128)(2,1)} async-done(((bf16[3,256,1024]{1,2,0:T(8,128)(2,1)}), bf16[3,1024,1024]{1,2,0:T(8,128)(2,1)}) %all-gather.8.cloned.1.call-update) | async-done | bytes 6291472 | tf_op jit(solution)/shard_map/all_gather | solution.py:85
  537.3 8.6 %copy.37 = bf16[3,1024,1024]{2,1,0:T(8,128)(2,1)} copy(bf16[3,1024,1024]{1,2,0:T(8,128)(2,1)} %all-gather.8.cloned.1.call-done) | data formatting | bytes 12582912 | tf_op jit(solution)/shard_map/reshape | solution.py:93
  545.9 8.0 %gather_fusion.4 = bf16[32,128,1024]{2,1,0:T(8,128)(2,1)} fusion(bf16[3,8,128,1024]{3,2,1,0:T(8,128)(2,1)} %bitcast.98, s32[32]{0:T(128)S(1)} %or_bitcast_fusion), kind=kCustom, calls=%fused_computation.4 | custom fusion | bytes 16777472 | tf_op jit(solution)/shard_map/gather | solution.py:99
  553.9 7.2 %fusion.2 = bf16[32,1,128,1024]{3,2,1,0:T(8,128)(2,1)} fusion(bf16[32,128,1024]{2,1,0:T(8,128)(2,1)} %gather_fusion.4, pred[32]{0:T(512)(128)(4,1)S(1)} %compare_and_fusion), kind=kLoop, calls=%fused_computation.11 | loop fusion | flops 4194304 | bytes 16777248 | tf_op jit(solution)/shard_map/jit(_where)/select_n | solution.py:100
  561.1 7.6 %all-to-all-start.1 = ((bf16[32,1,128,1024]{3,2,1,0:T(8,128)(2,1)}), bf16[32,1,128,1024]{3,2,1,0:T(8,128)(2,1)}, u32[]{:S(2)}, u32[]{:S(2)}) async-start(bf16[32,1,128,1024]{3,2,1,0:T(8,128)(2,1)} %fusion.2), calls=%async_computation.2 | async-start | bytes 16777216 | tf_op jit(solution)/shard_map/all_to_all | solution.py:101
  568.8 0.1 eq.24
  568.9 0.2 select_reduce_fusion
  569.2 7.8 %fusion.4 = f32[1,3,256,1024]{3,2,1,0:T(8,128)} fusion(f32[1,3,256,1024]{3,2,1,0:T(8,128)} %param.8, bf16[3,1024,1024]{2,1,0:T(8,128)(2,1)} %all-gather.4.cloned.1.call-done, s32[]{:T(128)S(6)} %select_n.334), kind=kOutput, calls=%fused_computation.15 | convolution fusion | flops 1612185600 | bytes 14155780 | tf_op jit(solution)/shard_map/sab,scb->sac/dot_general | solution.py:64
  577.0 6.8 fusion.3
  583.8 90.6 %all-to-all-done.1 = bf16[32,1,128,1024]{3,2,1,0:T(8,128)(2,1)} async-done(((bf16[32,1,128,1024]{3,2,1,0:T(8,128)(2,1)}), bf16[32,1,128,1024]{3,2,1,0:T(8,128)(2,1)}, u32[]{:S(2)}, u32[]{:S(2)}) %all-to-all-start.1) | async-done | bytes 8388640 | tf_op jit(solution)/shard_map/all_to_all | solution.py:101
  674.4 6.1 gather_fusion.5
  680.5 6.3 copy.34
  686.9 9.0 %reshape.625 = bf16[1,1966080]{1,0:T(2,128)(2,1)} reshape(bf16[128,15,1024]{2,1,0:T(8,128)(2,1)} %copy.34) | data formatting | bytes 7864320 | tf_op jit(solution)/shard_map/reshape | solution.py:103
  (36 shorter events, 0.7 us)
Async XLA Ops:
  7.2 441.3 %copy-start = (bf16[1,3,256,1024]{3,2,1,0:T(8,128)(2,1)S(1)}, bf16[1,3,256,1024]{3,2,1,0:T(8,128)(2,1)}, u32[]{:S(2)}) copy-start(bf16[1,3,256,1024]{3,2,1,0:T(8,128)(2,1)} %param.10) | copy-start | bytes 4718596
  121.9 114.4 %all-to-all-start = ((bf16[32,1,128,1024]{3,2,1,0:T(8,128)(2,1)}), bf16[32,1,128,1024]{3,2,1,0:T(8,128)(2,1)}, u32[]{:S(2)}, u32[]{:S(2)}) async-start(bf16[32,1,128,1024]{3,2,1,0:T(8,128)(2,1)} %fusion.1), calls=%async_computation | async-start | bytes 16777216 | tf_op jit(solution)/shard_map/all_to_all | solution.py:51
  130.5 174.5 %reduce-scatter.2.cloned.1.call-start = ((), (), s32[]{:S(2)}) async-start(), calls=%async_computation.3 | async-start | bytes 7864320 | tf_op jit(solution)/shard_map/reduce_scatter | solution.py:55
  244.3 127.8 %copy-start.4 = (bf16[1,3,256,1024]{3,2,1,0:T(8,128)(2,1)S(1)}, bf16[1,3,256,1024]{3,2,1,0:T(8,128)(2,1)}, u32[]{:S(2)}) copy-start(bf16[1,3,256,1024]{3,2,1,0:T(8,128)(2,1)} %param.11) | copy-start | bytes 4718596
  244.3 127.8 %all-gather.4.cloned.1.call-start = ((), (), s32[]{:S(2)}) async-start(), calls=%async_computation.4 | async-start | bytes 7864320 | tf_op jit(solution)/shard_map/all_gather | solution.py:58
  305.1 143.4 %all-gather.6.cloned.1.call-start = ((), (), s32[]{:S(2)}) async-start(), calls=%async_computation.5 | async-start | bytes 7864320 | tf_op jit(solution)/shard_map/all_gather | solution.py:77
  377.9 159.4 %all-gather.8.cloned.1.call-start = ((), (), s32[]{:S(2)}) async-start(), calls=%async_computation.6 | async-start | bytes 7864320 | tf_op jit(solution)/shard_map/all_gather | solution.py:85
  382.4 86.0 %copy-start.2 = (s32[32,3]{0,1:T(4,128)S(1)}, s32[32,3]{0,1:T(4,128)}, u32[]{:S(2)}) copy-start(s32[32,3]{0,1:T(4,128)} %param.7) | copy-start | bytes 1156
  561.1 113.3 %all-to-all-start.1 = ((bf16[32,1,128,1024]{3,2,1,0:T(8,128)(2,1)}), bf16[32,1,128,1024]{3,2,1,0:T(8,128)(2,1)}, u32[]{:S(2)}, u32[]{:S(2)}) async-start(bf16[32,1,128,1024]{3,2,1,0:T(8,128)(2,1)} %fusion.2), calls=%async_computation.2 | async-start | bytes 16777216 | tf_op jit(solution)/shard_map/all_to_all | solution.py:101
  569.2 7.8 %copy-start.3 = (f32[1,3,256,1024]{3,2,1,0:T(8,128)S(1)}, f32[1,3,256,1024]{3,2,1,0:T(8,128)}, u32[]{:S(2)}) copy-start(f32[1,3,256,1024]{3,2,1,0:T(8,128)} %param.9) | copy-start | bytes 9437188
  680.5 15.4 %copy-start.1 = (bf16[1,3,256,1024]{3,2,1,0:T(8,128)(2,1)S(1)}, bf16[1,3,256,1024]{3,2,1,0:T(8,128)(2,1)}, u32[]{:S(2)}) copy-start(bf16[1,3,256,1024]{3,2,1,0:T(8,128)(2,1)} %param.10) | copy-start | bytes 4718596
Sparse Core Ops, SparseCore 0:
  244.4 60.5 reduce-scatter.1
  306.7 65.3 all-gather.3
  378.0 70.3 all-gather.5
  468.4 68.8 all-gather.7
where the time goes:
time: 703 us; the launch traced here: 702 us
  waiting for transfers between devices  458 us (65%)
  other arithmetic  108 us (15%)
  local copies, waits for them, and re-layouts  69.5 us (10%)
  matrix products  27.2 us (4%)
  starting transfers between devices  16.5 us (2%)
  between operations  13.9 us (2%)
  blocking collectives  9.72 us (1%)
    all_to_all x1, waiting for transfers between devices, on_device(): lax.all_to_all(pieces, 'shard', split_axis=0, concat_axis=0, tiled=True)  105 us
    all_to_all x1, waiting for transfers between devices, on_device(): lax.all_to_all(outgoing, 'shard', split_axis=0, concat_axis=0, tiled=True)  90.6 us
    unnamed x1, other arithmetic  84.5 us
    all_gather x1, waiting for transfers between devices, on_device(): whole = lax.all_gather(grafted, 'replica', axis=1, tiled=True)  68.1 us
    all_gather x1, waiting for transfers between devices, on_device(): gradient = lax.all_gather(owned, 'replica', axis=1, tiled=True)  67 us
    all_gather x1, waiting for transfers between devices, on_device(): lax.all_gather(precond, 'replica', axis=2, tiled=True)  66.1 us
    reduce_scatter x1, waiting for transfers between devices, on_device(): lax.psum_scatter(partial_value.astype(jnp.bfloat16), 'replica', scatter_d...  60.7 us
  transfers between devices with their start and end apart: 6, of which 6 were waited for; matrix products, arithmetic and copies ran while one was open for 3% of the time, Pallas kernels for 0%

commit v1 on v0

v1 whole, which is shorter than its diff:
```python
import functools

import jax
import jax.numpy as jnp
from jax import lax
from jax.experimental import pallas as pl
from jax.experimental.pallas import tpu as pltpu
from jax.sharding import PartitionSpec as P

ROWS = 4096
COLS = 15360
BLK = 1024
EPSILON = 1e-06

N_X = 4
N_S = 32
SLOTS = 3
NBR = 4
NBC = 15
SUBS = 8
CELLS = 24
QROWS = 32
CUT = 8
GROUPS = 4
MESH = pl.DeviceIdType.MESH
f32 = jnp.float32
bf16 = jnp.bfloat16
VMEM_BYTES = 56 * 1024 * 1024


def unpack(flat_ref, out_ref, mid):
    def step(col, carry):
        for row in range(16):
            at = pl.multiple_of(row * COLS + col * BLK, BLK)
            mid[row] = flat_ref[:, pl.ds(at, BLK)].astype(f32).reshape(8, 128)
        for lane in range(8):
            out_ref[0, col, :, lane * 128 : lane * 128 + 128] = mid[:, lane, :].astype(bf16)
        return carry

    lax.fori_loop(0, NBC, step, 0)


def pack(in_ref, out_ref, mid):
    def step(col, carry):
        for part in range(N_X):
            for half in range(2):
                mid[:, part * 2 + half, :] = in_ref[part, 0, col, :, half * 128 : half * 128 + 128].astype(f32)
        for row in range(16):
            at = pl.multiple_of(row * COLS + col * BLK, BLK)
            out_ref[:, pl.ds(at, BLK)] = mid[row].reshape(1, BLK).astype(bf16)
        return carry

    lax.fori_loop(0, NBC, step, 0)


def greet(me_x, me_s):
    barrier = pltpu.get_barrier_semaphore()

    def hail(step, carry):
        pl.semaphore_signal(
            barrier, inc=1, device_id=(me_x, lax.rem(me_s + step, N_S)), device_id_type=MESH
        )
        return carry

    lax.fori_loop(1, N_S, hail, 0)
    for far in range(1, N_X):
        pl.semaphore_signal(
            barrier, inc=1, device_id=(lax.rem(me_x + far, N_X), me_s), device_id_type=MESH
        )
    pl.semaphore_wait(barrier, N_S - 1 + N_X - 1)


def exchange(
    table, own, left, blocks, roots, fwd_a, fwd_b, part_a, part_b, from_p, from_m,
    sum_own, sum_down, sum_up, sum_over, outbox, send, recv, piece_send, piece_recv, local_sem,
):
    me_x, me_s = lax.axis_index("replica"), lax.axis_index("shard")
    row, sub = me_s // SUBS, lax.rem(me_s, SUBS)
    up, down, over = lax.rem(me_x + 1, N_X), lax.rem(me_x + 3, N_X), lax.rem(me_x + 2, N_X)

    def remote(src, dst, place, x):
        return pltpu.make_async_remote_copy(
            src_ref=src, dst_ref=dst, send_sem=send.at[place], recv_sem=recv.at[place],
            device_id=(x, me_s), device_id_type=MESH,
        )

    low, high = pl.ds(0, CUT), pl.ds(CUT, NBC - CUT)
    copies = [None] * 18
    copies[0] = remote(own.at[over, low], fwd_a, 0, down)
    copies[1] = remote(own.at[over, high], fwd_b, 1, up)
    copies[2] = remote(own.at[down, high], from_p.at[high], 2, down)
    copies[3] = remote(own.at[up, low], from_m.at[low], 3, up)
    copies[4] = remote(part_a, from_p.at[low], 4, down)
    copies[5] = remote(part_b, from_m.at[high], 5, up)
    copies[6] = remote(sum_own.at[low], sum_down.at[low], 6, up)
    copies[7] = remote(sum_own.at[high], sum_up.at[high], 7, down)
    copies[8] = remote(sum_own.at[high], sum_down.at[high], 8, up)
    copies[9] = remote(sum_own.at[low], sum_up.at[low], 9, down)
    copies[10] = remote(sum_down.at[low], sum_over.at[low], 10, up)
    copies[11] = remote(sum_up.at[high], sum_over.at[high], 11, down)
    upper, lower = pl.ds(0, 128), pl.ds(128, 128)
    copies[12] = remote(left.at[:, upper], roots.at[:, me_x, upper], 12, up)
    copies[13] = remote(left.at[:, lower], roots.at[:, me_x, lower], 13, down)
    copies[14] = remote(left.at[:, lower], roots.at[:, me_x, lower], 14, up)
    copies[15] = remote(left.at[:, upper], roots.at[:, me_x, upper], 15, down)
    copies[16] = remote(roots.at[:, down, upper], roots.at[:, down, upper], 16, up)
    copies[17] = remote(roots.at[:, up, lower], roots.at[:, up, lower], 17, down)
    keep = pltpu.make_async_copy(left, roots.at[:, me_x], local_sem)

    def piece(quarter, index):
        place = index % SLOTS
        holder = lax.rem(index // SLOTS + me_s // NBR, SUBS) * NBR + lax.rem(row + NBR - place, NBR)
        src = outbox.at[quarter, index]
        dst = blocks.at[place, sub, quarter]
        away = lambda: pltpu.make_async_remote_copy(
            src_ref=src, dst_ref=dst, send_sem=piece_send.at[quarter, index],
            recv_sem=piece_recv.at[place], device_id=(me_x, holder), device_id_type=MESH,
        )
        home = lambda: pltpu.make_async_copy(src, dst, piece_recv.at[place])
        return place, holder, away, home

    def spread(quarter, total):
        def step(index, carry):
            place, holder, away, home = piece(quarter, index)
            block = table[holder * SLOTS + place]
            outbox[quarter, index] = total[lax.rem(jnp.maximum(block, 0), NBC)]

            @pl.when(holder != me_s)
            def _():
                away().start()

            @pl.when(holder == me_s)
            def _():
                home().start()

            return carry

        lax.fori_loop(0, CELLS, step, 0)

    greet(me_x, me_s)
    for place in range(4):
        copies[place].start()
    keep.start()

    def add_a(col, carry):
        part_a[col] = (fwd_a[col].astype(f32) + own[down, col].astype(f32)).astype(bf16)
        return carry

    def add_b(col, carry):
        part_b[col] = (fwd_b[col].astype(f32) + own[up, CUT + col].astype(f32)).astype(bf16)
        return carry

    def add_all(col, carry):
        sum_own[col] = (
            own[me_x, col].astype(f32) + (from_p[col].astype(f32) + from_m[col].astype(f32))
        ).astype(bf16)
        return carry

    copies[0].wait_recv()
    lax.fori_loop(0, CUT, add_a, 0)
    copies[4].start()
    copies[1].wait_recv()
    lax.fori_loop(0, NBC - CUT, add_b, 0)
    copies[5].start()
    copies[3].wait_recv()
    copies[4].wait_recv()
    lax.fori_loop(0, CUT, add_all, 0)
    copies[6].start()
    copies[9].start()
    copies[2].wait_recv()
    copies[5].wait_recv()
    lax.fori_loop(CUT, NBC, add_all, 0)
    copies[7].start()
    copies[8].start()
    spread(me_x, sum_own)
    copies[6].wait_recv()
    copies[10].start()
    copies[7].wait_recv()
    copies[11].start()
    for place in range(12, 16):
        copies[place].start()
    copies[8].wait_recv()
    spread(down, sum_down)
    copies[9].wait_recv()
    spread(up, sum_up)
    copies[12].wait_recv()
    copies[16].start()
    copies[13].wait_recv()
    copies[17].start()
    copies[10].wait_recv()
    copies[11].wait_recv()
    spread(over, sum_over)
    for place in range(14, 18):
        copies[place].wait_recv()
    for place in range(18):
        copies[place].wait_send()
    keep.wait()

    def sent(index, carry):
        for quarter in range(N_X):
            place, holder, away, home = piece(quarter, index)

            @pl.when(holder != me_s)
            def _():
                away().wait_send()

        return carry

    lax.fori_loop(0, CELLS, sent, 0)
    for place in range(SLOTS):
        pltpu.make_async_copy(blocks.at[place], blocks.at[place], piece_recv.at[place]).wait()


def spread_back(
    table, direction, sums, powers, update, sum_box, scaled, inbox_0, inbox_1, inbox_2, inbox_3, own,
    sum_send, sum_recv, piece_send, piece_recv, send, recv, local_sem,
):
    me_x, me_s = lax.axis_index("replica"), lax.axis_index("shard")
    row, sub = me_s // SUBS, lax.rem(me_s, SUBS)
    up, down, over = lax.rem(me_x + 1, N_X), lax.rem(me_x + 3, N_X), lax.rem(me_x + 2, N_X)
    low, high = pl.ds(0, CUT), pl.ds(CUT, NBC - CUT)

    inbox = (inbox_0, inbox_1, inbox_2, inbox_3)

    greet(me_x, me_s)
    shares = []
    for index, x in enumerate((up, down, over)):
        shares.append(
            pltpu.make_async_remote_copy(
                src_ref=sums, dst_ref=sum_box.at[index], send_sem=sum_send.at[index],
                recv_sem=sum_recv.at[index], device_id=(x, me_s), device_id_type=MESH,
            )
        )
        shares[index].start()

    def piece(group, index):
        place, target_sub = index // SUBS, lax.rem(index + sub, SUBS)
        target = lax.rem(me_s + place, NBR) * SUBS + target_sub
        src = scaled.at[group, place, target_sub]
        dst = inbox[group].at[me_s // NBR * SLOTS + place]
        away = lambda: pltpu.make_async_remote_copy(
            src_ref=src, dst_ref=dst, send_sem=piece_send.at[group, index],
            recv_sem=piece_recv.at[group], device_id=(me_x, target), device_id_type=MESH,
        )
        home = lambda: pltpu.make_async_copy(src, dst, piece_recv.at[group])
        return place, target_sub, target, away, home

    for share in shares:
        share.wait_recv()
    all_sums = sums[...] + (sum_box[0] + sum_box[1] + sum_box[2])
    factor = jnp.sqrt(powers[...] / (BLK * BLK)) / jnp.sqrt(all_sums / (BLK * BLK) + EPSILON)

    for group in range(GROUPS):
        for place in range(SLOTS):
            scale = jnp.concatenate([factor[place : place + 1]] * 2, axis=1)

            def step(count, carry):
                target_sub = lax.rem(count + sub, SUBS)
                at = pl.multiple_of(target_sub * 128 + group * QROWS, QROWS)
                scaled[group, place, target_sub] = (
                    direction[place, pl.ds(at, QROWS)] * scale
                ).astype(bf16)
                _, _, target, away, home = piece(group, place * SUBS + count)

                @pl.when(target != me_s)
                def _():
                    away().start()

                @pl.when(target == me_s)
                def _():
                    home().start()

                return carry

            lax.fori_loop(0, SUBS, step, 0)

    def remote(src, dst, group, place, x):
        return pltpu.make_async_remote_copy(
            src_ref=src, dst_ref=dst, send_sem=send.at[group, place],
            recv_sem=recv.at[group, place], device_id=(x, me_s), device_id_type=MESH,
        )

    def links(group):
        mine = update.at[me_x, group]
        return [
            remote(own.at[group, low], mine.at[low], group, 0, up),
            remote(own.at[group, high], mine.at[high], group, 1, down),
            remote(own.at[group, high], mine.at[high], group, 2, up),
            remote(own.at[group, low], mine.at[low], group, 3, down),
            remote(update.at[down, group, low], update.at[down, group, low], group, 4, up),
            remote(update.at[up, group, high], update.at[up, group, high], group, 5, down),
            pltpu.make_async_copy(own.at[group], mine, local_sem.at[group]),
        ]

    every = [links(group) for group in range(GROUPS)]

    def find(col):
        wanted = row * NBC + col
        index = 0
        for cell in range(CELLS):
            place = cell % SLOTS
            holder = cell // SLOTS * NBR + lax.rem(row + NBR - place, NBR)
            index = jnp.where(table[holder * SLOTS + place] == wanted, cell, index)
        return index

    for group in range(GROUPS):
        pltpu.make_async_copy(inbox[group], inbox[group], piece_recv.at[group]).wait()

        def place_col(col, carry):
            own[group, col] = inbox[group][find(col)]
            return carry

        lax.fori_loop(0, NBC, place_col, 0)
        for place in (0, 1, 2, 3, 6):
            every[group][place].start()
        if group > 0:
            every[group - 1][0].wait_recv()
            every[group - 1][4].start()
            every[group - 1][1].wait_recv()
            every[group - 1][5].start()
    every[GROUPS - 1][0].wait_recv()
    every[GROUPS - 1][4].start()
    every[GROUPS - 1][1].wait_recv()
    every[GROUPS - 1][5].start()
    for group in range(GROUPS):
        for place in range(2, 6):
            every[group][place].wait_recv()
        for place in range(6):
            every[group][place].wait_send()
        every[group][6].wait()
    for share in shares:
        share.wait_send()

    def sent(index, carry):
        for group in range(GROUPS):
            _, _, target, away, home = piece(group, index)

            @pl.when(target != me_s)
            def _():
                away().wait_send()

        return carry

    lax.fori_loop(0, CELLS, sent, 0)


def contract_last(a, b):
    return lax.dot_general(a, b, (((1,), (1,)), ((), ())), preferred_element_type=f32)


def precondition(scalars, grad, left, right, left_fac, right_fac, new_left, new_right, direction, sums, powers):
    slot = pl.program_id(0)
    start = pl.multiple_of(scalars[0] * 256, 256)
    scale = jnp.where(scalars[1 + slot] >= 0, 1.0 / BLK, 0.0).astype(f32)
    whole = grad[0]
    rows = grad[0, pl.ds(start, 256), :]
    new_left[0] = left_fac[0] + contract_last(rows, whole) * scale
    cols = grad[0, :, pl.ds(start, 256)]
    new_right[0] = right_fac[0] + jnp.dot(cols.T, whole, preferred_element_type=f32) * scale
    precond = contract_last(whole, right[0]).astype(bf16)
    result = jnp.dot(left[0], precond, preferred_element_type=f32)
    direction[0] = result
    sums[0] = jnp.full((8, 128), jnp.sum(jnp.square(result)), f32)
    powers[0] = jnp.full((8, 128), jnp.sum(jnp.square(whole.astype(f32))), f32)


def on_device(grads, slot_table, left_factor, right_factor, left_root, right_root):
    me_x, me_s = lax.axis_index("replica"), lax.axis_index("shard")
    table = slot_table.reshape(N_S * SLOTS)
    vmem = pl.BlockSpec(memory_space=pltpu.VMEM)
    smem = pl.BlockSpec(memory_space=pltpu.SMEM)
    hbm = pl.BlockSpec(memory_space=pl.ANY)
    dma = pltpu.SemaphoreType.DMA

    own = pl.pallas_call(
        unpack,
        grid=(N_X, 2),
        in_specs=[pl.BlockSpec((1, 16 * COLS), lambda i, j: (0, i * 2 + j))],
        out_specs=pl.BlockSpec((1, NBC, 16, BLK), lambda i, j: (i, 0, j, 0)),
        out_shape=jax.ShapeDtypeStruct((N_X, NBC, QROWS, BLK), bf16),
        scratch_shapes=[pltpu.VMEM((16, 8, 128), f32)],
        compiler_params=pltpu.CompilerParams(vmem_limit_bytes=VMEM_BYTES),
        name="unpack",
    )(grads)

    blocks, roots = pl.pallas_call(
        exchange,
        in_specs=[smem, vmem, hbm],
        out_specs=[hbm, hbm],
        out_shape=[
            jax.ShapeDtypeStruct((SLOTS, SUBS, N_X, QROWS, BLK), bf16),
            jax.ShapeDtypeStruct((SLOTS, N_X, 256, BLK), bf16),
        ],
        scratch_shapes=[
            pltpu.VMEM((CUT, QROWS, BLK), bf16),
            pltpu.VMEM((NBC - CUT, QROWS, BLK), bf16),
            pltpu.VMEM((CUT, QROWS, BLK), bf16),
            pltpu.VMEM((NBC - CUT, QROWS, BLK), bf16),
            pltpu.VMEM((NBC, QROWS, BLK), bf16),
            pltpu.VMEM((NBC, QROWS, BLK), bf16),
            pltpu.VMEM((NBC, QROWS, BLK), bf16),
            pltpu.VMEM((NBC, QROWS, BLK), bf16),
            pltpu.VMEM((NBC, QROWS, BLK), bf16),
            pltpu.VMEM((NBC, QROWS, BLK), bf16),
            pltpu.VMEM((N_X, CELLS, QROWS, BLK), bf16),
            dma((18,)),
            dma((18,)),
            dma((N_X, CELLS)),
            dma((SLOTS,)),
            dma,
        ],
        compiler_params=pltpu.CompilerParams(
            collective_id=0, has_side_effects=True, vmem_limit_bytes=VMEM_BYTES
        ),
        name="exchange",
    )(table, own, left_root[0])

    mine = lax.dynamic_index_in_dim(slot_table, me_s, 0, keepdims=False)
    scalars = jnp.concatenate([me_x.astype(jnp.int32)[None], mine])

    def block(shape):
        return pl.BlockSpec((1,) + shape, lambda slot: (slot,) + (0,) * len(shape))

    new_left, new_right, direction, sums, powers = pl.pallas_call(
        precondition,
        grid=(SLOTS,),
        in_specs=[smem] + [block((BLK, BLK))] * 2 + [block((256, BLK))] * 3,
        out_specs=[block((256, BLK))] * 2 + [block((BLK, 256))] + [block((8, 128))] * 2,
        out_shape=[
            jax.ShapeDtypeStruct((SLOTS, 256, BLK), f32),
            jax.ShapeDtypeStruct((SLOTS, 256, BLK), f32),
            jax.ShapeDtypeStruct((SLOTS, BLK, 256), f32),
            jax.ShapeDtypeStruct((SLOTS, 8, 128), f32),
            jax.ShapeDtypeStruct((SLOTS, 8, 128), f32),
        ],
        compiler_params=pltpu.CompilerParams(vmem_limit_bytes=VMEM_BYTES),
        name="precondition",
    )(
        scalars,
        blocks.reshape(SLOTS, BLK, BLK),
        roots.reshape(SLOTS, BLK, BLK),
        right_root[0],
        left_factor[0],
        right_factor[0],
    )

    def lines(values):
        return jnp.pad(values[:, 0, :], ((0, 8 - SLOTS), (0, 0)))

    update = pl.pallas_call(
        spread_back,
        in_specs=[smem, vmem, vmem, vmem],
        out_specs=hbm,
        out_shape=jax.ShapeDtypeStruct((N_X, GROUPS, NBC, QROWS, 256), bf16),
        scratch_shapes=[
            pltpu.VMEM((3, 8, 128), f32),
            pltpu.VMEM((GROUPS, SLOTS, SUBS, QROWS, 256), bf16),
            pltpu.VMEM((CELLS, QROWS, 256), bf16),
            pltpu.VMEM((CELLS, QROWS, 256), bf16),
            pltpu.VMEM((CELLS, QROWS, 256), bf16),
            pltpu.VMEM((CELLS, QROWS, 256), bf16),
            pltpu.VMEM((GROUPS, NBC, QROWS, 256), bf16),
            dma((3,)),
            dma((3,)),
            dma((GROUPS, CELLS)),
            dma((GROUPS,)),
            dma((GROUPS, 6)),
            dma((GROUPS, 6)),
            dma((GROUPS,)),
        ],
        compiler_params=pltpu.CompilerParams(
            collective_id=1, has_side_effects=True, vmem_limit_bytes=VMEM_BYTES
        ),
        name="spread_back",
    )(table, direction, lines(sums), lines(powers))

    flat = pl.pallas_call(
        pack,
        grid=(GROUPS, 2),
        in_specs=[pl.BlockSpec((N_X, 1, NBC, 16, 256), lambda i, j: (0, i, 0, j, 0))],
        out_specs=pl.BlockSpec((1, 16 * COLS), lambda i, j: (0, i * 2 + j)),
        out_shape=jax.ShapeDtypeStruct((1, 128 * COLS), bf16),
        scratch_shapes=[pltpu.VMEM((16, 8, 128), f32)],
        compiler_params=pltpu.CompilerParams(vmem_limit_bytes=VMEM_BYTES),
        name="pack",
    )(update)
    return new_left[None], new_right[None], flat


def solution(mesh):
    rows = P("shard", None, "replica", None)
    flat = P("replica", "shard")
    return jax.shard_map(
        on_device,
        mesh=mesh,
        in_specs=(flat, P(), rows, rows, rows, rows),
        out_specs=(rows, rows, flat),
        check_vma=False,
    )
```

time: 703 us -> 256 us (0.36)
  waiting for transfers between devices: 458 us -> 0 us
  Pallas kernels: 0 us -> 245 us
  other arithmetic: 108 us -> 0.66 us
  local copies, waits for them, and re-layouts: 69.5 us -> 4.92 us
  matrix products: 27.2 us -> 0 us
  starting transfers between devices: 16.5 us -> 0 us
  between operations: 13.9 us -> 0.66 us
  blocking collectives: 9.72 us -> 0 us
    pallas_call x0 -> x5, Pallas kernels: none -> 245 us  [the longest x1 139 us: on_device(): pl.pallas_call(exchange, in_specs=[smem, vmem, hbm], out_specs=[hbm, hbm]...]
    all_gather x3 -> x0, waiting for transfers between devices: 201 us -> none  [the longest x1 68.1 us: on_device(): whole = lax.all_gather(grafted, 'replica', axis=1, tiled=True)]
    all_to_all x2 -> x0, waiting for transfers between devices: 196 us -> none  [the longest x1 105 us: on_device(): lax.all_to_all(pieces, 'shard', split_axis=0, concat_axis=0, tiled=True)]
    unnamed x1 -> x0, other arithmetic: 84.5 us -> none
    reduce_scatter x1 -> x0, waiting for transfers between devices: 60.7 us -> none  [on_device(): lax.psum_scatter(partial_value.astype(jnp.bfloat16), 'replica', scatter_d...]
    gather x6 -> x0, local copies, waits for them, and re-layouts: 31.3 us -> none  [the longest x1 7.95 us: on_device(): outgoing = divided[back_fit, target_sub]]
    reshape x4 -> x1, local copies, waits for them, and re-layouts: 31.6 us -> 0.68 us  [on_device(): table = slot_table.reshape(N_S * SLOTS)]
    dot_general x4 -> x0, matrix products: 27.2 us -> none  [the longest x1 7.82 us: on_device(): jnp.einsum('sab,scb->sac', grad_rows, gradient, preferred_element_type=jn...]
  transfers between devices with their start and end apart: 6 -> 0, of which waited for: 6 -> 0; matrix products, arithmetic and copies ran while one was open for 3% -> 0% of each run, Pallas kernels for 0% -> 0%
where the time goes in v1:
time: 256 us; the launch traced here: 252 us
  Pallas kernels  245 us (96%)
  local copies, waits for them, and re-layouts  4.92 us (2%)
    pallas_call x1, Pallas kernels, on_device(): pl.pallas_call(exchange, in_specs=[smem, vmem, hbm], out_specs=[hbm, hbm]...  139 us
    pallas_call x1, Pallas kernels, on_device(): pl.pallas_call(spread_back, in_specs=[smem, vmem, vmem, vmem], out_specs=...  59 us
    pallas_call x1, Pallas kernels, on_device(): pl.pallas_call(unpack, grid=(N_X, 2), in_specs=[pl.BlockSpec((1, 16 * COL...  16.2 us
    pallas_call x1, Pallas kernels, on_device(): pl.pallas_call(pack, grid=(GROUPS, 2), in_specs=[pl.BlockSpec((N_X, 1, NB...  16 us
    pallas_call x1, Pallas kernels, on_device(): pl.pallas_call(precondition, grid=(SLOTS,), in_specs=[smem] + [block((BLK...  15.6 us

profile of v1, /device:TPU:0, one launch (start us, length us, event | category | flops | bytes accessed | tf_op | source)
XLA Modules:
  0.0 251.7 jit_solution(17543161343804208709)
XLA Ops:
  0.6 0.9 dynamic-slice_reduce_fusion
  1.5 0.7 pad_add_fusion.scalars
  2.2 0.8 copy.12
  2.9 0.7 reshape.15.table
  3.6 16.2 %unpack.1.own = bf16[4,15,32,1024]{3,2,1,0:T(8,128)(2,1)} custom-call(bf16[1,1966080]{1,0:T(2,128)(2,1)} %flat_ref.1), custom_call_target="tpu_custom_call" | custom-call | tf_op jit(solution)/shard_map/unpack/pallas_call | solution.py:375
  19.8 138.8 %exchange.1 = (bf16[3,8,4,32,1024]{4,3,2,1,0:T(8,128)(2,1)}, bf16[3,4,256,1024]{3,2,1,0:T(8,128)(2,1)}) custom-call(s32[96]{0:T(128)} %reshape.15.table, bf16[4,15,32,1024]{3,2,1,0:T(8,128)(2,1)} %unpack.1.own, bf16[3,256,1024]{2,1,0:T(8,128)(2,1)} %bitcast.18), custom_call_target="tpu_custom_call" | custom-call | tf_op jit(solution)/shard_map/exchange/pallas_call | solution.py:386
  158.6 15.6 %precondition.1 = (f32[3,256,1024]{2,1,0:T(8,128)}, f32[3,256,1024]{2,1,0:T(8,128)}, f32[3,1024,256]{2,1,0:T(8,128)}, f32[3,8,128]{2,1,0:T(8,128)}, f32[3,8,128]{2,1,0:T(8,128)}) custom-call(s32[4]{0:T(128)} %pad_add_fusion.scalars, bf16[3,1024,1024]{2,1,0:T(8,128)(2,1)} %bitcast.13, bf16[3,1024,1024]{2,1,0:T(8,128)(2,1)} %bitcast.14, ...), custom_call_target="tpu_custom_call" | custom-call | tf_op jit(solution)/shard_map/precondition/pallas_call | solution.py:424
  174.1 0.7 copy.13
  174.9 0.6 pad.7.sums
  175.4 0.7 copy.14
  176.2 0.6 pad.8.powers
  176.7 59.0 %spread_back.1.in_ref = bf16[4,4,15,32,256]{4,3,2,1,0:T(8,128)(2,1)} custom-call(s32[96]{0:T(128)} %reshape.15.table, f32[3,1024,256]{2,1,0:T(8,128)} %get-tuple-element.14.direction, f32[8,128]{1,0:T(8,128)} %pad.7.sums, f32[8,128]{1,0:T(8,128)} %pad.8.powers), custom_call_target="tpu_custom_call" | custom-call | tf_op jit(solution)/shard_map/spread_back/pallas_call | solution.py:450
  235.7 16.0 %pack.1 = bf16[1,1966080]{1,0:T(2,128)(2,1)} custom-call(bf16[4,4,15,32,256]{4,3,2,1,0:T(8,128)(2,1)} %spread_back.1.in_ref), custom_call_target="tpu_custom_call" | custom-call | tf_op jit(solution)/shard_map/pack/pallas_call | solution.py:477
  (2 shorter events, 0.0 us)

commit v2 on v1

v2 whole, which is shorter than its diff:
```python
import functools

import jax
import jax.numpy as jnp
from jax import lax
from jax.experimental import pallas as pl
from jax.experimental.pallas import tpu as pltpu
from jax.sharding import PartitionSpec as P

ROWS = 4096
COLS = 15360
BLK = 1024
EPSILON = 1e-06

N_X = 4
N_S = 32
SLOTS = 3
NBR = 4
NBC = 15
SUBS = 8
CELLS = 24
QROWS = 32
CUT = 8
GROUPS = 4
MESH = pl.DeviceIdType.MESH
f32 = jnp.float32
bf16 = jnp.bfloat16
VMEM_BYTES = 56 * 1024 * 1024


STEP = 9


def pack(in_ref, out_ref, mid):
    def step(col, carry):
        for part in range(N_X):
            for half in range(2):
                mid[pl.ds(part * 2 + half, 16, STEP), :] = in_ref[part, 0, col, :, half * 128 : half * 128 + 128].astype(f32)
        for row in range(16):
            at = pl.multiple_of(row * COLS + col * BLK, BLK)
            out_ref[:, pl.ds(at, BLK)] = mid[row * STEP : row * STEP + 8, :].reshape(1, BLK).astype(bf16)
        return carry

    lax.fori_loop(0, NBC, step, 0)


def hail(me_x, me_s):
    barrier = pltpu.get_barrier_semaphore()

    def one(step, carry):
        pl.semaphore_signal(
            barrier, inc=1, device_id=(me_x, lax.rem(me_s + step, N_S)), device_id_type=MESH
        )
        return carry

    lax.fori_loop(1, N_S, one, 0)
    for far in range(1, N_X):
        pl.semaphore_signal(
            barrier, inc=1, device_id=(lax.rem(me_x + far, N_X), me_s), device_id_type=MESH
        )


def admitted():
    pl.semaphore_wait(pltpu.get_barrier_semaphore(), N_S - 1 + N_X - 1)


def shampoo(
    table, grads, left, right, blocks_out, update,
    flat, mid, tiles, fwd_a, fwd_b, part_a, part_b, from_p, from_m,
    sum_own, sum_down, sum_up, sum_over, outbox, blocks, roots, right_box, precond, direction,
    sums, sum_box, scaled, inbox_0, inbox_1, inbox_2, inbox_3, own,
    flat_sem, right_sem, keep_sem, out_sem, send, recv, root_send, root_recv,
    piece_send, piece_recv, sum_send, sum_recv, back_send, back_recv, ring_send, ring_recv, local_sem,
):
    me_x, me_s = lax.axis_index("replica"), lax.axis_index("shard")
    row, sub = me_s // SUBS, lax.rem(me_s, SUBS)
    up, down, over = lax.rem(me_x + 1, N_X), lax.rem(me_x + 3, N_X), lax.rem(me_x + 2, N_X)
    low, high = pl.ds(0, CUT), pl.ds(CUT, NBC - CUT)
    inbox = (inbox_0, inbox_1, inbox_2, inbox_3)
    OVER, DOWN, UP, OWN = range(4)

    def cross(src, dst, send_sem, recv_sem, x):
        return pltpu.make_async_remote_copy(
            src_ref=src, dst_ref=dst, send_sem=send_sem, recv_sem=recv_sem,
            device_id=(x, me_s), device_id_type=MESH,
        )

    def remote(src, dst, place, x):
        return cross(src, dst, send.at[place], recv.at[place], x)

    copies = [
        remote(tiles.at[OVER, low], fwd_a, 0, down),
        remote(tiles.at[OVER, high], fwd_b, 1, up),
        remote(tiles.at[DOWN, high], from_p.at[high], 2, down),
        remote(tiles.at[UP, low], from_m.at[low], 3, up),
        remote(part_a, from_p.at[low], 4, down),
        remote(part_b, from_m.at[high], 5, up),
        remote(sum_own.at[low], sum_down.at[low], 6, up),
        remote(sum_own.at[high], sum_up.at[high], 7, down),
        remote(sum_own.at[high], sum_down.at[high], 8, up),
        remote(sum_own.at[low], sum_up.at[low], 9, down),
        remote(sum_down.at[low], sum_over.at[low], 10, up),
        remote(sum_up.at[high], sum_over.at[high], 11, down),
    ]
    upper, lower = pl.ds(0, 128), pl.ds(128, 128)

    def root(slot, place, src, dst, x):
        return cross(src, dst, root_send.at[slot, place], root_recv.at[slot, place], x)

    root_copies = []
    for slot in range(SLOTS):
        mine, there = left.at[slot], roots.at[slot, me_x]
        below, above = roots.at[slot, down, upper], roots.at[slot, up, lower]
        root_copies.append([
            root(slot, 0, mine.at[upper], there.at[upper], up),
            root(slot, 1, mine.at[lower], there.at[lower], down),
            root(slot, 2, mine.at[lower], there.at[lower], up),
            root(slot, 3, mine.at[upper], there.at[upper], down),
            root(slot, 4, below, below, up),
            root(slot, 5, above, above, down),
        ])
    keep = pltpu.make_async_copy(left, roots.at[:, me_x], keep_sem)
    fetch_right = pltpu.make_async_copy(right, right_box, right_sem)
    size = QROWS * COLS
    quarters = (over, down, up, me_x)
    loads = [
        pltpu.make_async_copy(
            grads.at[:, pl.ds(pl.multiple_of(quarters[part] * size, size), size)],
            flat.at[part % 2], flat_sem.at[part % 2],
        )
        for part in range(N_X)
    ]

    def unpack(part, first, last):
        def step(col, carry):
            for half in range(2):
                for line in range(16):
                    at = pl.multiple_of((half * 16 + line) * COLS + col * BLK, BLK)
                    mid[line * STEP : line * STEP + 8, :] = (
                        flat[part % 2, :, pl.ds(at, BLK)].astype(f32).reshape(8, 128)
                    )
                for lane in range(8):
                    tiles[part, col, half * 16 : half * 16 + 16, lane * 128 : lane * 128 + 128] = (
                        mid[pl.ds(lane, 16, STEP), :].astype(bf16)
                    )
            return carry

        lax.fori_loop(first, last, step, 0)

    def piece(quarter, index):
        place = index % SLOTS
        holder = lax.rem(index // SLOTS + me_s // NBR, SUBS) * NBR + lax.rem(row + NBR - place, NBR)
        src = outbox.at[quarter, index]
        dst = blocks.at[place, sub, quarter]
        away = lambda: pltpu.make_async_remote_copy(
            src_ref=src, dst_ref=dst, send_sem=piece_send.at[quarter, index],
            recv_sem=piece_recv.at[place], device_id=(me_x, holder), device_id_type=MESH,
        )
        home = lambda: pltpu.make_async_copy(src, dst, piece_recv.at[place])
        return place, holder, away, home

    def spread(quarter, total):
        def step(index, carry):
            place, holder, away, home = piece(quarter, index)
            block = table[holder * SLOTS + place]
            outbox[quarter, index] = total[lax.rem(jnp.maximum(block, 0), NBC)]

            @pl.when(holder != me_s)
            def _():
                away().start()

            @pl.when(holder == me_s)
            def _():
                home().start()

            return carry

        lax.fori_loop(0, CELLS, step, 0)

    def add_a(col, carry):
        part_a[col] = (fwd_a[col].astype(f32) + tiles[DOWN, col].astype(f32)).astype(bf16)
        return carry

    def add_b(col, carry):
        part_b[col] = (fwd_b[col].astype(f32) + tiles[UP, CUT + col].astype(f32)).astype(bf16)
        return carry

    def add_all(col, carry):
        sum_own[col] = (
            tiles[OWN, col].astype(f32) + (from_p[col].astype(f32) + from_m[col].astype(f32))
        ).astype(bf16)
        return carry

    loads[0].start()
    loads[1].start()
    fetch_right.start()
    hail(me_x, me_s)
    loads[0].wait()
    unpack(OVER, 0, CUT)
    admitted()
    keep.start()
    copies[0].start()
    unpack(OVER, CUT, NBC)
    copies[1].start()
    loads[2].start()
    loads[1].wait()
    unpack(DOWN, 0, NBC)
    copies[2].start()
    loads[3].start()
    loads[2].wait()
    unpack(UP, 0, NBC)
    copies[3].start()
    copies[0].wait_recv()
    lax.fori_loop(0, CUT, add_a, 0)
    copies[4].start()
    copies[1].wait_recv()
    lax.fori_loop(0, NBC - CUT, add_b, 0)
    copies[5].start()
    loads[3].wait()
    unpack(OWN, 0, NBC)
    copies[3].wait_recv()
    copies[4].wait_recv()
    lax.fori_loop(0, CUT, add_all, 0)
    copies[6].start()
    copies[9].start()
    copies[2].wait_recv()
    copies[5].wait_recv()
    lax.fori_loop(CUT, NBC, add_all, 0)
    copies[7].start()
    copies[8].start()
    for place in range(4):
        for slot in range(SLOTS):
            root_copies[slot][place].start()
    spread(me_x, sum_own)
    copies[6].wait_recv()
    copies[10].start()
    copies[7].wait_recv()
    copies[11].start()
    copies[8].wait_recv()
    spread(down, sum_down)
    copies[9].wait_recv()
    spread(up, sum_up)
    copies[10].wait_recv()
    copies[11].wait_recv()
    spread(over, sum_over)
    for slot in range(SLOTS):
        root_copies[slot][0].wait_recv()
        root_copies[slot][4].start()
        root_copies[slot][1].wait_recv()
        root_copies[slot][5].start()

    fetch_right.wait()
    powers = []
    for slot in range(SLOTS):
        pltpu.make_async_copy(blocks.at[slot], blocks.at[slot], piece_recv.at[slot]).wait()
        pltpu.make_async_copy(blocks.at[slot], blocks_out.at[slot], out_sem.at[slot]).start()
        grad = blocks[slot].reshape(BLK, BLK)
        precond[slot] = contract_last(grad, right_box[slot]).astype(bf16)
        powers.append(jnp.sum(jnp.square(grad.astype(f32))) / (BLK * BLK))

    keep.wait()
    shares = []
    for slot in range(SLOTS):
        for place in range(2, 6):
            root_copies[slot][place].wait_recv()
        result = jnp.dot(
            roots[slot].reshape(BLK, BLK), precond[slot], preferred_element_type=f32
        )
        direction[slot] = result
        sums[slot] = jnp.full((8, 128), jnp.sum(jnp.square(result)), f32)
        for index, x in enumerate((up, down, over)):
            share = cross(
                sums.at[slot], sum_box.at[slot, index],
                sum_send.at[slot, index], sum_recv.at[slot, index], x,
            )
            share.start()
            shares.append(share)
    for share in shares:
        share.wait_recv()
    scales = []
    for slot in range(SLOTS):
        total = sums[slot] + (sum_box[slot, 0] + sum_box[slot, 1] + sum_box[slot, 2])
        factor = jnp.sqrt(powers[slot]) / jnp.sqrt(total[0:1] / (BLK * BLK) + EPSILON)
        scales.append(jnp.concatenate([factor, factor], axis=1))

    def back(group, index):
        place, target_sub = index // SUBS, lax.rem(index + sub, SUBS)
        target = lax.rem(me_s + place, NBR) * SUBS + target_sub
        src = scaled.at[group, place, target_sub]
        dst = inbox[group].at[me_s // NBR * SLOTS + place]
        away = lambda: pltpu.make_async_remote_copy(
            src_ref=src, dst_ref=dst, send_sem=back_send.at[group, index],
            recv_sem=back_recv.at[group], device_id=(me_x, target), device_id_type=MESH,
        )
        home = lambda: pltpu.make_async_copy(src, dst, back_recv.at[group])
        return target_sub, target, away, home

    for group in range(GROUPS):
        for place in range(SLOTS):

            def step(count, carry):
                target_sub, target, away, home = back(group, place * SUBS + count)
                at = pl.multiple_of(target_sub * 128 + group * QROWS, QROWS)
                scaled[group, place, target_sub] = (
                    direction[place, pl.ds(at, QROWS)] * scales[place]
                ).astype(bf16)

                @pl.when(target != me_s)
                def _():
                    away().start()

                @pl.when(target == me_s)
                def _():
                    home().start()

                return carry

            lax.fori_loop(0, SUBS, step, 0)

    def ring(src, dst, group, place, x):
        return cross(src, dst, ring_send.at[group, place], ring_recv.at[group, place], x)

    def links(group):
        mine = update.at[me_x, group]
        below, above = update.at[down, group, low], update.at[up, group, high]
        return [
            ring(own.at[group, low], mine.at[low], group, 0, up),
            ring(own.at[group, high], mine.at[high], group, 1, down),
            ring(own.at[group, high], mine.at[high], group, 2, up),
            ring(own.at[group, low], mine.at[low], group, 3, down),
            ring(below, below, group, 4, up),
            ring(above, above, group, 5, down),
            pltpu.make_async_copy(own.at[group], mine, local_sem.at[group]),
        ]

    every = [links(group) for group in range(GROUPS)]

    def find(col):
        wanted = row * NBC + col
        index = 0
        for cell in range(CELLS):
            place = cell % SLOTS
            holder = cell // SLOTS * NBR + lax.rem(row + NBR - place, NBR)
            index = jnp.where(table[holder * SLOTS + place] == wanted, cell, index)
        return index

    def forward(group):
        every[group][0].wait_recv()
        every[group][4].start()
        every[group][1].wait_recv()
        every[group][5].start()

    for group in range(GROUPS):
        pltpu.make_async_copy(inbox[group], inbox[group], back_recv.at[group]).wait()

        def place_col(col, carry):
            own[group, col] = inbox[group][find(col)]
            return carry

        lax.fori_loop(0, NBC, place_col, 0)
        for place in (0, 1, 2, 3, 6):
            every[group][place].start()
        if group > 0:
            forward(group - 1)
    forward(GROUPS - 1)
    for group in range(GROUPS):
        for place in range(2, 6):
            every[group][place].wait_recv()
        for place in range(6):
            every[group][place].wait_send()
        every[group][6].wait()
    for share in shares:
        share.wait_send()
    for copy in copies:
        copy.wait_send()
    for slot in range(SLOTS):
        for copy in root_copies[slot]:
            copy.wait_send()
        pltpu.make_async_copy(blocks.at[slot], blocks_out.at[slot], out_sem.at[slot]).wait()

    def sent(index, carry):
        for quarter in range(N_X):
            place, holder, away, home = piece(quarter, index)

            @pl.when(holder != me_s)
            def _():
                away().wait_send()

        for group in range(GROUPS):
            target_sub, target, back_away, back_home = back(group, index)

            @pl.when(target != me_s)
            def _():
                back_away().wait_send()

        return carry

    lax.fori_loop(0, CELLS, sent, 0)


def contract_last(a, b):
    return lax.dot_general(a, b, (((1,), (1,)), ((), ())), preferred_element_type=f32)


def statistics(scalars, grad, left_fac, right_fac, new_left, new_right):
    slot = pl.program_id(0)
    start = pl.multiple_of(scalars[0] * 256, 256)
    scale = jnp.where(scalars[1 + slot] >= 0, 1.0 / BLK, 0.0).astype(f32)
    whole = grad[0]
    rows = grad[0, pl.ds(start, 256), :]
    new_left[0] = left_fac[0] + contract_last(rows, whole) * scale
    cols = grad[0, :, pl.ds(start, 256)]
    new_right[0] = right_fac[0] + jnp.dot(cols.T, whole, preferred_element_type=f32) * scale


def on_device(grads, slot_table, left_factor, right_factor, left_root, right_root):
    me_x, me_s = lax.axis_index("replica"), lax.axis_index("shard")
    table = slot_table.reshape(N_S * SLOTS)
    smem = pl.BlockSpec(memory_space=pltpu.SMEM)
    hbm = pl.BlockSpec(memory_space=pl.ANY)
    dma = pltpu.SemaphoreType.DMA
    vmem = pltpu.VMEM

    blocks, update = pl.pallas_call(
        shampoo,
        in_specs=[smem, hbm, hbm, hbm],
        out_specs=[hbm, hbm],
        out_shape=[
            jax.ShapeDtypeStruct((SLOTS, SUBS, N_X, QROWS, BLK), bf16),
            jax.ShapeDtypeStruct((N_X, GROUPS, NBC, QROWS, 256), bf16),
        ],
        scratch_shapes=[
            vmem((2, 1, QROWS * COLS), bf16),
            vmem((16 * STEP, 128), f32),
            vmem((N_X, NBC, QROWS, BLK), bf16),
            vmem((CUT, QROWS, BLK), bf16),
            vmem((NBC - CUT, QROWS, BLK), bf16),
            vmem((CUT, QROWS, BLK), bf16),
            vmem((NBC - CUT, QROWS, BLK), bf16),
        ]
        + [vmem((NBC, QROWS, BLK), bf16)] * 6
        + [
            vmem((N_X, CELLS, QROWS, BLK), bf16),
            vmem((SLOTS, SUBS, N_X, QROWS, BLK), bf16),
            vmem((SLOTS, N_X, 256, BLK), bf16),
            vmem((SLOTS, 256, BLK), bf16),
            vmem((SLOTS, BLK, 256), bf16),
            vmem((SLOTS, BLK, 256), f32),
            vmem((SLOTS, 8, 128), f32),
            vmem((SLOTS, 3, 8, 128), f32),
            vmem((GROUPS, SLOTS, SUBS, QROWS, 256), bf16),
        ]
        + [vmem((CELLS, QROWS, 256), bf16)] * GROUPS
        + [
            vmem((GROUPS, NBC, QROWS, 256), bf16),
            dma((2,)),
            dma,
            dma,
            dma((SLOTS,)),
            dma((12,)),
            dma((12,)),
            dma((SLOTS, 6)),
            dma((SLOTS, 6)),
            dma((N_X, CELLS)),
            dma((SLOTS,)),
            dma((SLOTS, 3)),
            dma((SLOTS, 3)),
            dma((GROUPS, CELLS)),
            dma((GROUPS,)),
            dma((GROUPS, 6)),
            dma((GROUPS, 6)),
            dma((GROUPS,)),
        ],
        compiler_params=pltpu.CompilerParams(
            collective_id=0, has_side_effects=True, vmem_limit_bytes=VMEM_BYTES
        ),
        name="shampoo",
    )(table, grads, left_root[0], right_root[0])

    mine = lax.dynamic_index_in_dim(slot_table, me_s, 0, keepdims=False)
    scalars = jnp.concatenate([me_x.astype(jnp.int32)[None], mine])

    def block(shape):
        return pl.BlockSpec((1,) + shape, lambda slot: (slot,) + (0,) * len(shape))

    new_left, new_right = pl.pallas_call(
        statistics,
        grid=(SLOTS,),
        in_specs=[smem, block((BLK, BLK))] + [block((256, BLK))] * 2,
        out_specs=[block((256, BLK))] * 2,
        out_shape=[jax.ShapeDtypeStruct((SLOTS, 256, BLK), f32)] * 2,
        compiler_params=pltpu.CompilerParams(vmem_limit_bytes=VMEM_BYTES),
        name="statistics",
    )(scalars, blocks.reshape(SLOTS, BLK, BLK), left_factor[0], right_factor[0])

    flat = pl.pallas_call(
        pack,
        grid=(GROUPS, 2),
        in_specs=[pl.BlockSpec((N_X, 1, NBC, 16, 256), lambda i, j: (0, i, 0, j, 0))],
        out_specs=pl.BlockSpec((1, 16 * COLS), lambda i, j: (0, i * 2 + j)),
        out_shape=jax.ShapeDtypeStruct((1, 128 * COLS), bf16),
        scratch_shapes=[pltpu.VMEM((16 * STEP, 128), f32)],
        compiler_params=pltpu.CompilerParams(vmem_limit_bytes=VMEM_BYTES),
        name="pack",
    )(update)
    return new_left[None], new_right[None], flat


def solution(mesh):
    rows = P("shard", None, "replica", None)
    flat = P("replica", "shard")
    return jax.shard_map(
        on_device,
        mesh=mesh,
        in_specs=(flat, P(), rows, rows, rows, rows),
        out_specs=(rows, rows, flat),
        check_vma=False,
    )
```

time: 256 us -> 227 us (0.89); the launches traced: 252 us -> 226 us
  Pallas kernels: 245 us -> 222 us
  local copies, waits for them, and re-layouts: 4.92 us -> 2.25 us
    pallas_call x4 -> x2, Pallas kernels: 230 us -> 211 us  [the longest x1 202 us: on_device(): pl.pallas_call(shampoo, in_specs=[smem, hbm, hbm, hbm], out_specs=[hbm, h...]
    pallas_call x1, Pallas kernels: 16 us -> 11.4 us  [on_device(): pl.pallas_call(pack, grid=(GROUPS, 2), in_specs=[pl.BlockSpec((N_X, 1, NB...]
where the time goes in v2:
time: 227 us; the launch traced here: 226 us
  Pallas kernels  222 us (98%)
    pallas_call x1, Pallas kernels, on_device(): pl.pallas_call(shampoo, in_specs=[smem, hbm, hbm, hbm], out_specs=[hbm, h...  202 us
    pallas_call x1, Pallas kernels, on_device(): pl.pallas_call(pack, grid=(GROUPS, 2), in_specs=[pl.BlockSpec((N_X, 1, NB...  11.4 us
    pallas_call x1, Pallas kernels, on_device(): pl.pallas_call(statistics, grid=(SLOTS,), in_specs=[smem, block((BLK, BLK...  9.09 us

profile of v2, /device:TPU:0, one launch (start us, length us, event | category | flops | bytes accessed | tf_op | source)
XLA Modules:
  0.0 225.5 jit_solution(17317203735878205871)
XLA Ops:
  0.6 0.9 dynamic-slice_reduce_fusion
  1.5 0.6 pad_add_fusion.scalars
  2.1 0.8 copy.10
  2.9 0.6 reshape.12.table
  3.5 201.5 %shampoo.1 = (bf16[3,8,4,32,1024]{4,3,2,1,0:T(8,128)(2,1)}, bf16[4,4,15,32,256]{4,3,2,1,0:T(8,128)(2,1)}) custom-call(s32[96]{0:T(128)} %reshape.12.table, bf16[1,1966080]{1,0:T(2,128)(2,1)} %grads.1, bf16[3,256,1024]{2,1,0:T(8,128)(2,1)} %bitcast.11, bf16[3,256,1024]{2,1,0:T(8,128)(2,1)} %bitcast.12), custom_call_target="tpu_custom_call" | custom-call | tf_op jit(solution)/shard_map/shampoo/pallas_call | solution.py:424
  205.0 9.1 %statistics.1 = (f32[3,256,1024]{2,1,0:T(8,128)}, f32[3,256,1024]{2,1,0:T(8,128)}) custom-call(s32[4]{0:T(128)} %pad_add_fusion.scalars, bf16[3,1024,1024]{2,1,0:T(8,128)(2,1)} %bitcast.8, f32[3,256,1024]{2,1,0:T(8,128)} %bitcast.9, f32[3,256,1024]{2,1,0:T(8,128)} %bitcast.10), custom_call_target="tpu_custom_call" | custom-call | tf_op jit(solution)/shard_map/statistics/pallas_call | solution.py:486
  214.1 11.4 %pack.1 = bf16[1,1966080]{1,0:T(2,128)(2,1)} custom-call(bf16[4,4,15,32,256]{4,3,2,1,0:T(8,128)(2,1)} %get-tuple-element.10.in_ref), custom_call_target="tpu_custom_call" | custom-call | tf_op jit(solution)/shard_map/pack/pallas_call | solution.py:496

commit v3 on v2

--- a/solution.py
+++ b/solution.py
@@ -25,7 +25,7 @@
 MESH = pl.DeviceIdType.MESH
 f32 = jnp.float32
 bf16 = jnp.bfloat16
-VMEM_BYTES = 56 * 1024 * 1024
+VMEM_BYTES = 58 * 1024 * 1024
 
 
 STEP = 9
@@ -65,12 +65,12 @@
 
 
 def shampoo(
-    table, grads, left, right, blocks_out, update,
+    table, grads, left, right, left_fac, right_fac, new_left, new_right, update,
     flat, mid, tiles, fwd_a, fwd_b, part_a, part_b, from_p, from_m,
     sum_own, sum_down, sum_up, sum_over, outbox, blocks, roots, right_box, precond, direction,
-    sums, sum_box, scaled, inbox_0, inbox_1, inbox_2, inbox_3, own,
+    sums, sum_box, scaled, inbox_early, inbox_0, inbox_1, inbox_2, inbox_3, own, left_box, right_fac_box, places,
     flat_sem, right_sem, keep_sem, out_sem, send, recv, root_send, root_recv,
-    piece_send, piece_recv, sum_send, sum_recv, back_send, back_recv, ring_send, ring_recv, local_sem,
+    fac_sem, piece_send, piece_recv, sum_send, sum_recv, back_send, back_recv, early_recv, ring_send, ring_recv, local_sem,
 ):
     me_x, me_s = lax.axis_index("replica"), lax.axis_index("shard")
     row, sub = me_s // SUBS, lax.rem(me_s, SUBS)
@@ -121,6 +121,8 @@
         ])
     keep = pltpu.make_async_copy(left, roots.at[:, me_x], keep_sem)
     fetch_right = pltpu.make_async_copy(right, right_box, right_sem)
+    fetch_left_fac = pltpu.make_async_copy(left_fac, left_box, fac_sem.at[0])
+    fetch_right_fac = pltpu.make_async_copy(right_fac, right_fac_box, fac_sem.at[1])
     size = QROWS * COLS
     quarters = (over, down, up, me_x)
     loads = [
@@ -162,7 +164,7 @@
     def spread(quarter, total):
         def step(index, carry):
             place, holder, away, home = piece(quarter, index)
-            block = table[holder * SLOTS + place]
+            block = table[holder, place]
             outbox[quarter, index] = total[lax.rem(jnp.maximum(block, 0), NBC)]
 
             @pl.when(holder != me_s)
@@ -176,6 +178,23 @@
             return carry
 
         lax.fori_loop(0, CELLS, step, 0)
+
+    def locate(col, carry):
+        wanted = row * NBC + col
+        early, late, is_late = 0, 0, 0
+        for cell in range(CELLS):
+            block_of, place = cell // SLOTS, cell % SLOTS
+            holder = block_of * NBR + lax.rem(row + NBR - place, NBR)
+            found = table[holder, place] == wanted
+            if place == SLOTS - 1:
+                late = jnp.where(found, block_of, late)
+                is_late = jnp.where(found, 1, is_late)
+            else:
+                early = jnp.where(found, block_of * 2 + place, early)
+        places[0, col] = early
+        places[1, col] = late
+        places[2, col] = is_late
+        return carry
 
     def add_a(col, carry):
         part_a[col] = (fwd_a[col].astype(f32) + tiles[DOWN, col].astype(f32)).astype(bf16)
@@ -194,6 +213,8 @@
     loads[0].start()
     loads[1].start()
     fetch_right.start()
+    fetch_left_fac.start()
+    fetch_right_fac.start()
     hail(me_x, me_s)
     loads[0].wait()
     unpack(OVER, 0, CUT)
@@ -228,10 +249,11 @@
     lax.fori_loop(CUT, NBC, add_all, 0)
     copies[7].start()
     copies[8].start()
-    for place in range(4):
-        for slot in range(SLOTS):
+    for slot in range(SLOTS):
+        for place in range(4):
             root_copies[slot][place].start()
     spread(me_x, sum_own)
+    lax.fori_loop(0, NBC, locate, 0)
     copies[6].wait_recv()
     copies[10].start()
     copies[7].wait_recv()
@@ -253,14 +275,47 @@
     powers = []
     for slot in range(SLOTS):
         pltpu.make_async_copy(blocks.at[slot], blocks.at[slot], piece_recv.at[slot]).wait()
-        pltpu.make_async_copy(blocks.at[slot], blocks_out.at[slot], out_sem.at[slot]).start()
         grad = blocks[slot].reshape(BLK, BLK)
         precond[slot] = contract_last(grad, right_box[slot]).astype(bf16)
         powers.append(jnp.sum(jnp.square(grad.astype(f32))) / (BLK * BLK))
 
-    keep.wait()
+    def back(place, group, count):
+        target_sub = lax.rem(count + sub, SUBS)
+        target = lax.rem(me_s + place, NBR) * SUBS + target_sub
+        if group is None:
+            src = scaled.at[place, target_sub]
+            dst = inbox_early.at[me_s // NBR * 2 + place]
+            send_sem, recv_sem = back_send.at[place, count], early_recv
+        else:
+            src = scaled.at[place, target_sub, pl.ds(group * QROWS, QROWS)]
+            dst = inbox[group].at[me_s // NBR]
+            send_sem, recv_sem = back_send.at[place + group, count], back_recv.at[group]
+        away = lambda: pltpu.make_async_remote_copy(
+            src_ref=src, dst_ref=dst, send_sem=send_sem, recv_sem=recv_sem,
+            device_id=(me_x, target), device_id_type=MESH,
+        )
+        home = lambda: pltpu.make_async_copy(src, dst, recv_sem)
+        return target, away, home
+
+    def give_back(place, group):
+        def step(count, carry):
+            target, away, home = back(place, group, count)
+
+            @pl.when(target != me_s)
+            def _():
+                away().start()
+
+            @pl.when(target == me_s)
+            def _():
+                home().start()
+
+            return carry
+
+        lax.fori_loop(0, SUBS, step, 0)
+
     shares = []
-    for slot in range(SLOTS):
+
+    def direct(slot):
         for place in range(2, 6):
             root_copies[slot][place].wait_recv()
         result = jnp.dot(
@@ -268,54 +323,41 @@
         )
         direction[slot] = result
         sums[slot] = jnp.full((8, 128), jnp.sum(jnp.square(result)), f32)
+        shares.append([])
         for index, x in enumerate((up, down, over)):
             share = cross(
                 sums.at[slot], sum_box.at[slot, index],
                 sum_send.at[slot, index], sum_recv.at[slot, index], x,
             )
             share.start()
-            shares.append(share)
-    for share in shares:
-        share.wait_recv()
-    scales = []
-    for slot in range(SLOTS):
+            shares[slot].append(share)
+
+    def graft(slot):
+        for share in shares[slot]:
+            share.wait_recv()
         total = sums[slot] + (sum_box[slot, 0] + sum_box[slot, 1] + sum_box[slot, 2])
         factor = jnp.sqrt(powers[slot]) / jnp.sqrt(total[0:1] / (BLK * BLK) + EPSILON)
-        scales.append(jnp.concatenate([factor, factor], axis=1))
-
-    def back(group, index):
-        place, target_sub = index // SUBS, lax.rem(index + sub, SUBS)
-        target = lax.rem(me_s + place, NBR) * SUBS + target_sub
-        src = scaled.at[group, place, target_sub]
-        dst = inbox[group].at[me_s // NBR * SLOTS + place]
-        away = lambda: pltpu.make_async_remote_copy(
-            src_ref=src, dst_ref=dst, send_sem=back_send.at[group, index],
-            recv_sem=back_recv.at[group], device_id=(me_x, target), device_id_type=MESH,
-        )
-        home = lambda: pltpu.make_async_copy(src, dst, back_recv.at[group])
-        return target_sub, target, away, home
-
-    for group in range(GROUPS):
-        for place in range(SLOTS):
-
-            def step(count, carry):
-                target_sub, target, away, home = back(group, place * SUBS + count)
-                at = pl.multiple_of(target_sub * 128 + group * QROWS, QROWS)
-                scaled[group, place, target_sub] = (
-                    direction[place, pl.ds(at, QROWS)] * scales[place]
-                ).astype(bf16)
-
-                @pl.when(target != me_s)
-                def _():
-                    away().start()
-
-                @pl.when(target == me_s)
-                def _():
-                    home().start()
-
-                return carry
-
-            lax.fori_loop(0, SUBS, step, 0)
+        scale = jnp.concatenate([factor, factor], axis=1)
+
+        def step(part, carry):
+            scaled[slot, part] = (
+                direction[slot, pl.ds(pl.multiple_of(part * 128, 128), 128)] * scale
+            ).astype(bf16)
+            return carry
+
+        lax.fori_loop(0, SUBS, step, 0)
+
+    keep.wait()
+    direct(0)
+    direct(1)
+    graft(0)
+    give_back(0, None)
+    direct(2)
+    graft(1)
+    give_back(1, None)
+    graft(2)
+    give_back(2, 0)
+    give_back(2, 1)
 
     def ring(src, dst, group, place, x):
         return cross(src, dst, ring_send.at[group, place], ring_recv.at[group, place], x)
@@ -335,14 +377,24 @@
 
     every = [links(group) for group in range(GROUPS)]
 
-    def find(col):
-        wanted = row * NBC + col
-        index = 0
-        for cell in range(CELLS):
-            place = cell % SLOTS
-            holder = cell // SLOTS * NBR + lax.rem(row + NBR - place, NBR)
-            index = jnp.where(table[holder * SLOTS + place] == wanted, cell, index)
-        return index
+    def statistics(slot):
+        whole = blocks[slot].reshape(BLK, BLK)
+        scale = jnp.where(table[me_s, slot] >= 0, 1.0 / BLK, 0.0).astype(f32)
+        rows = blocks[slot, pl.ds(me_x * 2, 2)].reshape(256, BLK)
+        left_box[slot] = left_box[slot] + contract_last(rows, whole) * scale
+        start = pl.multiple_of(me_x * 256, 256)
+        cols = blocks[slot, :, :, :, pl.ds(start, 256)].reshape(BLK, 256)
+        right_fac_box[slot] = (
+            right_fac_box[slot] + jnp.dot(cols.T, whole, preferred_element_type=f32) * scale
+        )
+        for copy in leave(slot):
+            copy.start()
+
+    def leave(slot):
+        return [
+            pltpu.make_async_copy(left_box.at[slot], new_left.at[slot], out_sem.at[slot, 0]),
+            pltpu.make_async_copy(right_fac_box.at[slot], new_right.at[slot], out_sem.at[slot, 1]),
+        ]
 
     def forward(group):
         every[group][0].wait_recv()
@@ -350,18 +402,26 @@
         every[group][1].wait_recv()
         every[group][5].start()
 
+    fetch_left_fac.wait()
+    fetch_right_fac.wait()
+    pltpu.make_async_copy(inbox_early, inbox_early, early_recv).wait()
     for group in range(GROUPS):
         pltpu.make_async_copy(inbox[group], inbox[group], back_recv.at[group]).wait()
 
         def place_col(col, carry):
-            own[group, col] = inbox[group][find(col)]
+            early = inbox_early[places[0, col], pl.ds(group * QROWS, QROWS)]
+            late = inbox[group][places[1, col]]
+            own[group, col] = jnp.where(places[2, col] == 1, late, early)
             return carry
 
         lax.fori_loop(0, NBC, place_col, 0)
         for place in (0, 1, 2, 3, 6):
             every[group][place].start()
+        if group + 2 < GROUPS:
+            give_back(2, group + 2)
         if group > 0:
             forward(group - 1)
+            statistics(group - 1)
     forward(GROUPS - 1)
     for group in range(GROUPS):
         for place in range(2, 6):
@@ -369,14 +429,13 @@
         for place in range(6):
             every[group][place].wait_send()
         every[group][6].wait()
-    for share in shares:
-        share.wait_send()
+    for slot in range(SLOTS):
+        for copy in shares[slot] + root_copies[slot]:
+            copy.wait_send()
+        for copy in leave(slot):
+            copy.wait()
     for copy in copies:
         copy.wait_send()
-    for slot in range(SLOTS):
-        for copy in root_copies[slot]:
-            copy.wait_send()
-        pltpu.make_async_copy(blocks.at[slot], blocks_out.at[slot], out_sem.at[slot]).wait()
 
     def sent(index, carry):
         for quarter in range(N_X):
@@ -386,8 +445,13 @@
             def _():
                 away().wait_send()
 
-        for group in range(GROUPS):
-            target_sub, target, back_away, back_home = back(group, index)
+        return carry
+
+    lax.fori_loop(0, CELLS, sent, 0)
+
+    def sent_back(count, carry):
+        for place, group in ((0, None), (1, None), (2, 0), (2, 1), (2, 2), (2, 3)):
+            target, back_away, back_home = back(place, group, count)
 
             @pl.when(target != me_s)
             def _():
@@ -395,38 +459,26 @@
 
         return carry
 
-    lax.fori_loop(0, CELLS, sent, 0)
+    lax.fori_loop(0, SUBS, sent_back, 0)
 
 
 def contract_last(a, b):
     return lax.dot_general(a, b, (((1,), (1,)), ((), ())), preferred_element_type=f32)
 
 
-def statistics(scalars, grad, left_fac, right_fac, new_left, new_right):
-    slot = pl.program_id(0)
-    start = pl.multiple_of(scalars[0] * 256, 256)
-    scale = jnp.where(scalars[1 + slot] >= 0, 1.0 / BLK, 0.0).astype(f32)
-    whole = grad[0]
-    rows = grad[0, pl.ds(start, 256), :]
-    new_left[0] = left_fac[0] + contract_last(rows, whole) * scale
-    cols = grad[0, :, pl.ds(start, 256)]
-    new_right[0] = right_fac[0] + jnp.dot(cols.T, whole, preferred_element_type=f32) * scale
-
-
 def on_device(grads, slot_table, left_factor, right_factor, left_root, right_root):
-    me_x, me_s = lax.axis_index("replica"), lax.axis_index("shard")
-    table = slot_table.reshape(N_S * SLOTS)
     smem = pl.BlockSpec(memory_space=pltpu.SMEM)
     hbm = pl.BlockSpec(memory_space=pl.ANY)
     dma = pltpu.SemaphoreType.DMA
     vmem = pltpu.VMEM
 
-    blocks, update = pl.pallas_call(
+    new_left, new_right, update = pl.pallas_call(
         shampoo,
-        in_specs=[smem, hbm, hbm, hbm],
-        out_specs=[hbm, hbm],
+        in_specs=[smem] + [hbm] * 5,
+        out_specs=[hbm] * 3,
         out_shape=[
-            jax.ShapeDtypeStruct((SLOTS, SUBS, N_X, QROWS, BLK), bf16),
+            jax.ShapeDtypeStruct((SLOTS, 256, BLK), f32),
+            jax.ShapeDtypeStruct((SLOTS, 256, BLK), f32),
             jax.ShapeDtypeStruct((N_X, GROUPS, NBC, QROWS, 256), bf16),
         ],
         scratch_shapes=[
@@ -448,25 +500,31 @@
             vmem((SLOTS, BLK, 256), f32),
             vmem((SLOTS, 8, 128), f32),
             vmem((SLOTS, 3, 8, 128), f32),
-            vmem((GROUPS, SLOTS, SUBS, QROWS, 256), bf16),
+            vmem((SLOTS, SUBS, 128, 256), bf16),
+            vmem((2 * SUBS, 128, 256), bf16),
         ]
-        + [vmem((CELLS, QROWS, 256), bf16)] * GROUPS
+        + [vmem((SUBS, QROWS, 256), bf16)] * GROUPS
         + [
             vmem((GROUPS, NBC, QROWS, 256), bf16),
+            vmem((SLOTS, 256, BLK), f32),
+            vmem((SLOTS, 256, BLK), f32),
+            pltpu.SMEM((3, NBC), jnp.int32),
             dma((2,)),
             dma,
             dma,
-            dma((SLOTS,)),
+            dma((SLOTS, 2)),
             dma((12,)),
             dma((12,)),
             dma((SLOTS, 6)),
             dma((SLOTS, 6)),
+            dma((2,)),
             dma((N_X, CELLS)),
             dma((SLOTS,)),
             dma((SLOTS, 3)),
             dma((SLOTS, 3)),
-            dma((GROUPS, CELLS)),
+            dma((2 + GROUPS, SUBS)),
             dma((GROUPS,)),
+            dma,
             dma((GROUPS, 6)),
             dma((GROUPS, 6)),
             dma((GROUPS,)),
@@ -475,23 +533,7 @@
             collective_id=0, has_side_effects=True, vmem_limit_bytes=VMEM_BYTES
         ),
         name="shampoo",
-    )(table, grads, left_root[0], right_root[0])
-
-    mine = lax.dynamic_index_in_dim(slot_table, me_s, 0, keepdims=False)
-    scalars = jnp.concatenate([me_x.astype(jnp.int32)[None], mine])
-
-    def block(shape):
-        return pl.BlockSpec((1,) + shape, lambda slot: (slot,) + (0,) * len(shape))
-
-    new_left, new_right = pl.pallas_call(
-        statistics,
-        grid=(SLOTS,),
-        in_specs=[smem, block((BLK, BLK))] + [block((256, BLK))] * 2,
-        out_specs=[block((256, BLK))] * 2,
-        out_shape=[jax.ShapeDtypeStruct((SLOTS, 256, BLK), f32)] * 2,
-        compiler_params=pltpu.CompilerParams(vmem_limit_bytes=VMEM_BYTES),
-        name="statistics",
-    )(scalars, blocks.reshape(SLOTS, BLK, BLK), left_factor[0], right_factor[0])
+    )(slot_table, grads, left_root[0], right_root[0], left_factor[0], right_factor[0])
 
     flat = pl.pallas_call(
         pack,

time: 227 us -> 224 us (0.987)
  Pallas kernels: 222 us -> 214 us
  local copies, waits for them, and re-layouts: 2.25 us -> 6.06 us
    pallas_call x2 -> x1, Pallas kernels: 211 us -> 203 us  [on_device(): pl.pallas_call(shampoo, in_specs=[smem] + [hbm] * 5, out_specs=[hbm] * 3,...]
    unnamed x1 -> x7, local copies, waits for them, and re-layouts: 0.76 us -> 6.06 us
where the time goes in v3:
time: 224 us; the launch traced here: 221 us
  Pallas kernels  214 us (96%)
  local copies, waits for them, and re-layouts  6.06 us (3%)
    pallas_call x1, Pallas kernels, on_device(): pl.pallas_call(shampoo, in_specs=[smem] + [hbm] * 5, out_specs=[hbm] * 3,...  203 us
    pallas_call x1, Pallas kernels, on_device(): pl.pallas_call(pack, grid=(GROUPS, 2), in_specs=[pl.BlockSpec((N_X, 1, NB...  11.6 us
    unnamed x7, local copies, waits for them, and re-layouts  6.06 us

profile of v3, /device:TPU:0, one launch (start us, length us, event | category | flops | bytes accessed | tf_op | source)
XLA Modules:
  0.0 221.1 jit_solution(10141221535034913867)
XLA Ops:
  0.6 1.4 copy.9.table
  2.0 202.8 %shampoo.1 = (f32[3,256,1024]{2,1,0:T(8,128)}, f32[3,256,1024]{2,1,0:T(8,128)}, bf16[4,4,15,32,256]{4,3,2,1,0:T(8,128)(2,1)}) custom-call(s32[32,3]{1,0:T(8,128)} %copy.9.table, bf16[1,1966080]{1,0:T(2,128)(2,1)} %grads.1, bf16[3,256,1024]{2,1,0:T(8,128)(2,1)} %bitcast.10, bf16[3,256,1024]{2,1,0:T(8,128)(2,1)} %bitcast.11, f32[3,256,1024]{2,1,0:T(8,128)} %bitcast.6, ...), custom_call_target="tpu_custom_call" | custom-call | tf_op jit(solution)/shard_map/shampoo/pallas_call | solution.py:475
  204.8 0.0 copy-start.1
  204.8 11.6 %pack.1 = bf16[1,1966080]{1,0:T(2,128)(2,1)} custom-call(bf16[4,4,15,32,256]{4,3,2,1,0:T(8,128)(2,1)} %get-tuple-element.8.in_ref), custom_call_target="tpu_custom_call" | custom-call | tf_op jit(solution)/shard_map/pack/pallas_call | solution.py:538
  216.4 0.0 copy-done.1
  216.4 0.0 copy-start
  216.4 1.7 copy.12
  218.1 1.4 copy-done
  219.4 1.7 copy.13
Async XLA Ops:
  204.8 11.6 %copy-start.1 = (f32[3,256,1024]{2,1,0:T(8,128)S(1)}, f32[3,256,1024]{2,1,0:T(8,128)}, u32[]{:S(2)}) copy-start(f32[3,256,1024]{2,1,0:T(8,128)} %get-tuple-element.6) | copy-start | bytes 9437188
  216.4 3.0 %copy-start = (f32[3,256,1024]{2,1,0:T(8,128)S(1)}, f32[3,256,1024]{2,1,0:T(8,128)}, u32[]{:S(2)}) copy-start(f32[3,256,1024]{2,1,0:T(8,128)} %get-tuple-element.7) | copy-start | bytes 9437188

commit v4 on v3

--- a/solution.py
+++ b/solution.py
@@ -29,19 +29,28 @@
 
 
 STEP = 9
+WIDE = 3
 
 
 def pack(in_ref, out_ref, mid):
-    def step(col, carry):
-        for part in range(N_X):
-            for half in range(2):
-                mid[pl.ds(part * 2 + half, 16, STEP), :] = in_ref[part, 0, col, :, half * 128 : half * 128 + 128].astype(f32)
-        for row in range(16):
-            at = pl.multiple_of(row * COLS + col * BLK, BLK)
-            out_ref[:, pl.ds(at, BLK)] = mid[row * STEP : row * STEP + 8, :].reshape(1, BLK).astype(bf16)
-        return carry
-
-    lax.fori_loop(0, NBC, step, 0)
+    def step(count, carry):
+        for lane in range(WIDE):
+            col, work = count * WIDE + lane, mid.at[lane]
+            for part in range(N_X):
+                for half in range(2):
+                    work[pl.ds(part * 2 + half, 16, STEP), :] = in_ref[
+                        part, 0, col, :, half * 128 : half * 128 + 128
+                    ].astype(f32)
+        for lane in range(WIDE):
+            col, work = count * WIDE + lane, mid.at[lane]
+            for row in range(16):
+                at = pl.multiple_of(row * COLS + col * BLK, BLK)
+                out_ref[:, pl.ds(at, BLK)] = (
+                    work[row * STEP : row * STEP + 8, :].reshape(1, BLK).astype(bf16)
+                )
+        return carry
+
+    lax.fori_loop(0, NBC // WIDE, step, 0)
 
 
 def hail(me_x, me_s):
@@ -138,12 +147,13 @@
             for half in range(2):
                 for line in range(16):
                     at = pl.multiple_of((half * 16 + line) * COLS + col * BLK, BLK)
-                    mid[line * STEP : line * STEP + 8, :] = (
+                    mid[half, line * STEP : line * STEP + 8, :] = (
                         flat[part % 2, :, pl.ds(at, BLK)].astype(f32).reshape(8, 128)
                     )
+            for half in range(2):
                 for lane in range(8):
                     tiles[part, col, half * 16 : half * 16 + 16, lane * 128 : lane * 128 + 128] = (
-                        mid[pl.ds(lane, 16, STEP), :].astype(bf16)
+                        mid[half, pl.ds(lane, 16, STEP), :].astype(bf16)
                     )
             return carry
 
@@ -161,10 +171,10 @@
         home = lambda: pltpu.make_async_copy(src, dst, piece_recv.at[place])
         return place, holder, away, home
 
-    def spread(quarter, total):
+    def spread(quarter, total, between=()):
         def step(index, carry):
             place, holder, away, home = piece(quarter, index)
-            block = table[holder, place]
+            block = table[place, holder]
             outbox[quarter, index] = total[lax.rem(jnp.maximum(block, 0), NBC)]
 
             @pl.when(holder != me_s)
@@ -177,7 +187,11 @@
 
             return carry
 
-        lax.fori_loop(0, CELLS, step, 0)
+        run = CELLS // max(len(between), 1)
+        for part in range(CELLS // run):
+            for copy in between[part : part + 1]:
+                copy.start()
+            lax.fori_loop(part * run, part * run + run, step, 0)
 
     def locate(col, carry):
         wanted = row * NBC + col
@@ -185,7 +199,7 @@
         for cell in range(CELLS):
             block_of, place = cell // SLOTS, cell % SLOTS
             holder = block_of * NBR + lax.rem(row + NBR - place, NBR)
-            found = table[holder, place] == wanted
+            found = table[place, holder] == wanted
             if place == SLOTS - 1:
                 late = jnp.where(found, block_of, late)
                 is_late = jnp.where(found, 1, is_late)
@@ -247,24 +261,19 @@
     copies[2].wait_recv()
     copies[5].wait_recv()
     lax.fori_loop(CUT, NBC, add_all, 0)
-    copies[7].start()
-    copies[8].start()
-    for slot in range(SLOTS):
-        for place in range(4):
-            root_copies[slot][place].start()
-    spread(me_x, sum_own)
+    spread(me_x, sum_own, copies[7:9])
     lax.fori_loop(0, NBC, locate, 0)
     copies[6].wait_recv()
     copies[10].start()
     copies[7].wait_recv()
     copies[11].start()
     copies[8].wait_recv()
-    spread(down, sum_down)
+    spread(down, sum_down, root_copies[0][:4])
     copies[9].wait_recv()
-    spread(up, sum_up)
+    spread(up, sum_up, root_copies[1][:4])
     copies[10].wait_recv()
     copies[11].wait_recv()
-    spread(over, sum_over)
+    spread(over, sum_over, root_copies[2][:4])
     for slot in range(SLOTS):
         root_copies[slot][0].wait_recv()
         root_copies[slot][4].start()
@@ -379,7 +388,7 @@
 
     def statistics(slot):
         whole = blocks[slot].reshape(BLK, BLK)
-        scale = jnp.where(table[me_s, slot] >= 0, 1.0 / BLK, 0.0).astype(f32)
+        scale = jnp.where(table[slot, me_s] >= 0, 1.0 / BLK, 0.0).astype(f32)
         rows = blocks[slot, pl.ds(me_x * 2, 2)].reshape(256, BLK)
         left_box[slot] = left_box[slot] + contract_last(rows, whole) * scale
         start = pl.multiple_of(me_x * 256, 256)
@@ -483,7 +492,7 @@
         ],
         scratch_shapes=[
             vmem((2, 1, QROWS * COLS), bf16),
-            vmem((16 * STEP, 128), f32),
+            vmem((2, 16 * STEP, 128), f32),
             vmem((N_X, NBC, QROWS, BLK), bf16),
             vmem((CUT, QROWS, BLK), bf16),
             vmem((NBC - CUT, QROWS, BLK), bf16),
@@ -533,7 +542,7 @@
             collective_id=0, has_side_effects=True, vmem_limit_bytes=VMEM_BYTES
         ),
         name="shampoo",
-    )(slot_table, grads, left_root[0], right_root[0], left_factor[0], right_factor[0])
+    )(slot_table.T, grads, left_root[0], right_root[0], left_factor[0], right_factor[0])
 
     flat = pl.pallas_call(
         pack,
@@ -541,7 +550,7 @@
         in_specs=[pl.BlockSpec((N_X, 1, NBC, 16, 256), lambda i, j: (0, i, 0, j, 0))],
         out_specs=pl.BlockSpec((1, 16 * COLS), lambda i, j: (0, i * 2 + j)),
         out_shape=jax.ShapeDtypeStruct((1, 128 * COLS), bf16),
-        scratch_shapes=[pltpu.VMEM((16 * STEP, 128), f32)],
+        scratch_shapes=[pltpu.VMEM((WIDE, 16 * STEP, 128), f32)],
         compiler_params=pltpu.CompilerParams(vmem_limit_bytes=VMEM_BYTES),
         name="pack",
     )(update)

time: 224 us -> 219 us (0.978); the launches traced: 221 us -> 218 us
    unnamed x7 -> x6, local copies, waits for them, and re-layouts: 6.06 us -> 4.69 us
where the time goes in v4:
time: 219 us; the launch traced here: 218 us
  Pallas kernels  213 us (97%)
  local copies, waits for them, and re-layouts  4.69 us (2%)
    pallas_call x1, Pallas kernels, on_device(): pl.pallas_call(shampoo, in_specs=[smem] + [hbm] * 5, out_specs=[hbm] * 3,...  202 us
    pallas_call x1, Pallas kernels, on_device(): pl.pallas_call(pack, grid=(GROUPS, 2), in_specs=[pl.BlockSpec((N_X, 1, NB...  10.8 us
    unnamed x6, local copies, waits for them, and re-layouts  4.69 us

profile of v4, /device:TPU:0, one launch (start us, length us, event | category | flops | bytes accessed | tf_op | source)
XLA Modules:
  0.0 218.5 jit_solution(6525697121222149095)
XLA Ops:
  0.6 202.3 %shampoo.1 = (f32[3,256,1024]{2,1,0:T(8,128)}, f32[3,256,1024]{2,1,0:T(8,128)}, bf16[4,4,15,32,256]{4,3,2,1,0:T(8,128)(2,1)}) custom-call(s32[3,32]{1,0:T(4,128)} %bitcast.13, bf16[1,1966080]{1,0:T(2,128)(2,1)} %grads.1, bf16[3,256,1024]{2,1,0:T(8,128)(2,1)} %bitcast.11, bf16[3,256,1024]{2,1,0:T(8,128)(2,1)} %bitcast.12, f32[3,256,1024]{2,1,0:T(8,128)} %bitcast.7, ...), custom_call_target="tpu_custom_call" | custom-call | tf_op jit(solution)/shard_map/shampoo/pallas_call | solution.py:484
  203.0 0.0 copy-start.1
  203.0 10.8 %pack.1 = bf16[1,1966080]{1,0:T(2,128)(2,1)} custom-call(bf16[4,4,15,32,256]{4,3,2,1,0:T(8,128)(2,1)} %get-tuple-element.8.in_ref), custom_call_target="tpu_custom_call" | custom-call | tf_op jit(solution)/shard_map/pack/pallas_call | solution.py:547
  213.8 0.0 copy-done.1
  213.8 0.0 copy-start
  213.8 1.7 copy.11
  215.5 1.4 copy-done
  216.8 1.7 copy.12
Async XLA Ops:
  203.0 10.8 %copy-start.1 = (f32[3,256,1024]{2,1,0:T(8,128)S(1)}, f32[3,256,1024]{2,1,0:T(8,128)}, u32[]{:S(2)}) copy-start(f32[3,256,1024]{2,1,0:T(8,128)} %get-tuple-element.6) | copy-start | bytes 9437188
  213.8 3.0 %copy-start = (f32[3,256,1024]{2,1,0:T(8,128)S(1)}, f32[3,256,1024]{2,1,0:T(8,128)}, u32[]{:S(2)}) copy-start(f32[3,256,1024]{2,1,0:T(8,128)} %get-tuple-element.7) | copy-start | bytes 9437188

commit v5 on v4

v5 whole, which is shorter than its diff:
```python
import functools

import jax
import jax.numpy as jnp
from jax import lax
from jax.experimental import pallas as pl
from jax.experimental.pallas import tpu as pltpu
from jax.sharding import PartitionSpec as P

ROWS = 4096
COLS = 15360
BLK = 1024
EPSILON = 1e-06

N_X = 4
N_S = 32
SLOTS = 3
NBR = 4
NBC = 15
SUBS = 8
CELLS = 24
QROWS = 32
CUT = 8
GROUPS = 4
MESH = pl.DeviceIdType.MESH
f32 = jnp.float32
bf16 = jnp.bfloat16
VMEM_BYTES = 58 * 1024 * 1024


STEP = 9
HALVES = 2
HROWS = 64
LINES = NBC * 8


def finish(flat_ref, left_ref, right_ref, out_ref, left_out, right_out, sems):
    step = pl.program_id(0)
    copies = (
        pltpu.make_async_copy(left_ref, left_out, sems.at[0]),
        pltpu.make_async_copy(right_ref, right_out, sems.at[1]),
    )

    @pl.when(step == 0)
    def _():
        for copy in copies:
            copy.start()

    def part(count, carry):
        at = pl.ds(pl.multiple_of(count * COLS, COLS), COLS)
        out_ref[:, at] = flat_ref[:, at].astype(bf16)
        return carry

    lax.fori_loop(0, 16, part, 0)

    @pl.when(step == pl.num_programs(0) - 1)
    def _():
        for copy in copies:
            copy.wait()


def hail(me_x, me_s):
    barrier = pltpu.get_barrier_semaphore()

    def one(step, carry):
        pl.semaphore_signal(
            barrier, inc=1, device_id=(me_x, lax.rem(me_s + step, N_S)), device_id_type=MESH
        )
        return carry

    lax.fori_loop(1, N_S, one, 0)
    for far in range(1, N_X):
        pl.semaphore_signal(
            barrier, inc=1, device_id=(lax.rem(me_x + far, N_X), me_s), device_id_type=MESH
        )


def admitted():
    pl.semaphore_wait(pltpu.get_barrier_semaphore(), N_S - 1 + N_X - 1)


def shampoo(
    table, grads, left, right, left_fac, right_fac, new_left, new_right, update,
    flat, mid, tiles, fwd_a, fwd_b, part_a, part_b, from_p, from_m,
    sum_own, sum_down, sum_up, sum_over, outbox, blocks, roots, right_box, precond,
    sums, sum_box, factors, factor_box, raw, inbox_0, inbox_1, gathered, lines, left_box, right_fac_box, places,
    flat_sem, right_sem, keep_sem, out_sem, send, recv, root_send, root_recv,
    fac_sem, piece_send, piece_recv, sum_send, sum_recv, factor_send, factor_recv,
    back_send, back_recv, ring_send, ring_recv, line_sem,
):
    me_x, me_s = lax.axis_index("replica"), lax.axis_index("shard")
    row, sub = me_s // SUBS, lax.rem(me_s, SUBS)
    up, down, over = lax.rem(me_x + 1, N_X), lax.rem(me_x + 3, N_X), lax.rem(me_x + 2, N_X)
    low, high = pl.ds(0, CUT), pl.ds(CUT, NBC - CUT)
    inbox = (inbox_0, inbox_1)
    OVER, DOWN, UP, OWN = range(4)

    def cross(src, dst, send_sem, recv_sem, x):
        return pltpu.make_async_remote_copy(
            src_ref=src, dst_ref=dst, send_sem=send_sem, recv_sem=recv_sem,
            device_id=(x, me_s), device_id_type=MESH,
        )

    def remote(src, dst, place, x):
        return cross(src, dst, send.at[place], recv.at[place], x)

    copies = [
        remote(tiles.at[OVER, low], fwd_a, 0, down),
        remote(tiles.at[OVER, high], fwd_b, 1, up),
        remote(tiles.at[DOWN, high], from_p.at[high], 2, down),
        remote(tiles.at[UP, low], from_m.at[low], 3, up),
        remote(part_a, from_p.at[low], 4, down),
        remote(part_b, from_m.at[high], 5, up),
        remote(sum_own.at[low], sum_down.at[low], 6, up),
        remote(sum_own.at[high], sum_up.at[high], 7, down),
        remote(sum_own.at[high], sum_down.at[high], 8, up),
        remote(sum_own.at[low], sum_up.at[low], 9, down),
        remote(sum_down.at[low], sum_over.at[low], 10, up),
        remote(sum_up.at[high], sum_over.at[high], 11, down),
    ]
    def root(slot, half):
        mine, there = left.at[slot], roots.at[slot, me_x]
        below, above = roots.at[slot, down, 0, half], roots.at[slot, up, 1, half]

        def one(place, src, dst, x):
            return cross(
                src, dst, root_send.at[slot, half, place], root_recv.at[slot, half, place], x
            )

        return [
            one(0, mine.at[0, half], there.at[0, half], up),
            one(1, mine.at[1, half], there.at[1, half], down),
            one(2, mine.at[1, half], there.at[1, half], up),
            one(3, mine.at[0, half], there.at[0, half], down),
            one(4, below, below, up),
            one(5, above, above, down),
        ]

    root_copies = [[root(slot, half) for slot in range(SLOTS)] for half in range(HALVES)]

    def pass_root(half, slot):
        for place in range(2):
            root_copies[half][slot][place].wait_recv()
            root_copies[half][slot][place + 4].start()

    keep = pltpu.make_async_copy(left, roots.at[:, me_x], keep_sem)
    fetch_right = pltpu.make_async_copy(right, right_box, right_sem)
    fetch_left_fac = pltpu.make_async_copy(left_fac, left_box, fac_sem.at[0])
    fetch_right_fac = pltpu.make_async_copy(right_fac, right_fac_box, fac_sem.at[1])
    size = QROWS * COLS
    quarters = (over, down, up, me_x)
    loads = [
        pltpu.make_async_copy(
            grads.at[:, pl.ds(pl.multiple_of(quarters[part] * size, size), size)],
            flat.at[part % 2], flat_sem.at[part % 2],
        )
        for part in range(N_X)
    ]

    def unpack(part, first, last):
        def step(col, carry):
            for half in range(2):
                for line in range(16):
                    at = pl.multiple_of((half * 16 + line) * COLS + col * BLK, BLK)
                    mid[half, line * STEP : line * STEP + 8, :] = (
                        flat[part % 2, :, pl.ds(at, BLK)].astype(f32).reshape(8, 128)
                    )
            for half in range(2):
                for lane in range(8):
                    tiles[part, col, half * 16 : half * 16 + 16, lane * 128 : lane * 128 + 128] = (
                        mid[half, pl.ds(lane, 16, STEP), :].astype(bf16)
                    )
            return carry

        lax.fori_loop(first, last, step, 0)

    def piece(quarter, index):
        place = index % SLOTS
        holder = lax.rem(index // SLOTS + me_s // NBR, SUBS) * NBR + lax.rem(row + NBR - place, NBR)
        src = outbox.at[quarter, index]
        dst = blocks.at[place, sub, quarter]
        away = lambda: pltpu.make_async_remote_copy(
            src_ref=src, dst_ref=dst, send_sem=piece_send.at[quarter, index],
            recv_sem=piece_recv.at[place], device_id=(me_x, holder), device_id_type=MESH,
        )
        home = lambda: pltpu.make_async_copy(src, dst, piece_recv.at[place])
        return place, holder, away, home

    def spread(quarter, total, between=()):
        def step(index, carry):
            place, holder, away, home = piece(quarter, index)
            block = table[place, holder]
            outbox[quarter, index] = total[lax.rem(jnp.maximum(block, 0), NBC)]

            @pl.when(holder != me_s)
            def _():
                away().start()

            @pl.when(holder == me_s)
            def _():
                home().start()

            return carry

        run = CELLS // max(len(between), 1)
        for part in range(CELLS // run):
            for copy in between[part : part + 1]:
                copy.start()
            lax.fori_loop(part * run, part * run + run, step, 0)

    def locate(col, carry):
        wanted = row * NBC + col
        index = 0
        for cell in range(CELLS):
            place = cell % SLOTS
            holder = cell // SLOTS * NBR + lax.rem(row + NBR - place, NBR)
            index = jnp.where(table[place, holder] == wanted, cell, index)
        places[col] = index
        return carry

    def add_a(col, carry):
        part_a[col] = (fwd_a[col].astype(f32) + tiles[DOWN, col].astype(f32)).astype(bf16)
        return carry

    def add_b(col, carry):
        part_b[col] = (fwd_b[col].astype(f32) + tiles[UP, CUT + col].astype(f32)).astype(bf16)
        return carry

    def add_all(col, carry):
        sum_own[col] = (
            tiles[OWN, col].astype(f32) + (from_p[col].astype(f32) + from_m[col].astype(f32))
        ).astype(bf16)
        return carry

    loads[0].start()
    loads[1].start()
    fetch_right.start()
    fetch_left_fac.start()
    fetch_right_fac.start()
    hail(me_x, me_s)
    loads[0].wait()
    unpack(OVER, 0, CUT)
    admitted()
    keep.start()
    copies[0].start()
    for copy in root_copies[0][0][:4]:
        copy.start()
    unpack(OVER, CUT, NBC)
    copies[1].start()
    loads[2].start()
    loads[1].wait()
    unpack(DOWN, 0, NBC)
    copies[2].start()
    loads[3].start()
    loads[2].wait()
    unpack(UP, 0, NBC)
    copies[3].start()
    copies[0].wait_recv()
    lax.fori_loop(0, CUT, add_a, 0)
    copies[4].start()
    copies[1].wait_recv()
    lax.fori_loop(0, NBC - CUT, add_b, 0)
    copies[5].start()
    for copy in root_copies[0][1][:4]:
        copy.start()
    loads[3].wait()
    unpack(OWN, 0, NBC)
    copies[3].wait_recv()
    copies[4].wait_recv()
    lax.fori_loop(0, CUT, add_all, 0)
    copies[6].start()
    copies[9].start()
    copies[2].wait_recv()
    copies[5].wait_recv()
    lax.fori_loop(CUT, NBC, add_all, 0)
    spread(me_x, sum_own, copies[7:9])
    lax.fori_loop(0, NBC, locate, 0)
    copies[6].wait_recv()
    copies[10].start()
    copies[7].wait_recv()
    copies[11].start()
    pass_root(0, 0)
    pass_root(0, 1)
    copies[8].wait_recv()
    spread(down, sum_down, root_copies[0][2][:4])
    copies[9].wait_recv()
    spread(up, sum_up, root_copies[1][0][:4])
    copies[10].wait_recv()
    copies[11].wait_recv()
    spread(over, sum_over, root_copies[1][1][:4] + root_copies[1][2][:4])
    pass_root(0, 2)
    for slot in range(SLOTS):
        pass_root(1, slot)

    fetch_right.wait()
    powers = []
    for slot in range(SLOTS):
        pltpu.make_async_copy(blocks.at[slot], blocks.at[slot], piece_recv.at[slot]).wait()
        grad = blocks[slot].reshape(BLK, BLK)
        precond[slot] = contract_last(grad, right_box[slot]).astype(bf16)
        powers.append(jnp.sum(jnp.square(grad.astype(f32))) / (BLK * BLK))

    def target_of(place, count):
        target_sub = lax.rem(count + sub, SUBS)
        return target_sub, lax.rem(me_s + place, NBR) * SUBS + target_sub

    def sender(src, dst, send_sem, recv_sem, target):
        away = lambda: pltpu.make_async_remote_copy(
            src_ref=src, dst_ref=dst, send_sem=send_sem, recv_sem=recv_sem,
            device_id=(me_x, target), device_id_type=MESH,
        )
        home = lambda: pltpu.make_async_copy(src, dst, recv_sem)
        return target, away, home

    def back(place, half, count):
        target_sub, target = target_of(place, count)
        return sender(
            raw.at[half, place, target_sub], inbox[half].at[me_s // NBR * SLOTS + place],
            back_send.at[half, place, count], back_recv.at[half], target,
        )

    def tell(place, count):
        target_sub, target = target_of(place, count)
        return sender(
            factors.at[place], factor_box.at[me_s // NBR * SLOTS + place],
            factor_send.at[place, count], factor_recv, target,
        )

    def start_all(describe):
        def step(count, carry):
            target, away, home = describe(count)

            @pl.when(target != me_s)
            def _():
                away().start()

            @pl.when(target == me_s)
            def _():
                home().start()

            return carry

        lax.fori_loop(0, SUBS, step, 0)

    def finish_all(describe):
        def step(count, carry):
            target, away, home = describe(count)

            @pl.when(target != me_s)
            def _():
                away().wait_send()

            return carry

        lax.fori_loop(0, SUBS, step, 0)

    squares = [[] for slot in range(SLOTS)]

    def direct(half, slot):
        for copy in root_copies[half][slot][2:]:
            copy.wait_recv()
        result = jnp.dot(
            roots[slot, :, :, half].reshape(BLK // HALVES, BLK), precond[slot],
            preferred_element_type=f32,
        )
        raw[half, slot] = result.astype(bf16).reshape(SUBS, HROWS, 256)
        start_all(functools.partial(back, slot, half))
        squares[slot].append(jnp.sum(jnp.square(result)))

    shares = []

    def share(slot):
        sums[slot] = jnp.full((8, 128), squares[slot][0] + squares[slot][1], f32)
        for index, x in enumerate((up, down, over)):
            copy = cross(
                sums.at[slot], sum_box.at[slot, index],
                sum_send.at[slot, index], sum_recv.at[slot, index], x,
            )
            copy.start()
            shares.append(copy)

    def graft(slot):
        total = sums[slot] + (sum_box[slot, 0] + sum_box[slot, 1] + sum_box[slot, 2])
        factors[slot] = jnp.sqrt(powers[slot]) / jnp.sqrt(total / (BLK * BLK) + EPSILON)
        start_all(functools.partial(tell, slot))

    def ring(src, dst, group, place, x):
        return cross(src, dst, ring_send.at[group, place], ring_recv.at[group, place], x)

    def links(group):
        mine = gathered.at[me_x, group]
        below, above = gathered.at[down, group, low], gathered.at[up, group, high]
        return [
            ring(mine.at[low], mine.at[low], group, 0, up),
            ring(mine.at[high], mine.at[high], group, 1, down),
            ring(mine.at[high], mine.at[high], group, 2, up),
            ring(mine.at[low], mine.at[low], group, 3, down),
            ring(below, below, group, 4, up),
            ring(above, above, group, 5, down),
        ]

    every = [links(group) for group in range(GROUPS)]

    def statistics(slot):
        whole = blocks[slot].reshape(BLK, BLK)
        scale = jnp.where(table[slot, me_s] >= 0, 1.0 / BLK, 0.0).astype(f32)
        rows = blocks[slot, pl.ds(me_x * 2, 2)].reshape(256, BLK)
        left_box[slot] = left_box[slot] + contract_last(rows, whole) * scale
        start = pl.multiple_of(me_x * 256, 256)
        cols = blocks[slot, :, :, :, pl.ds(start, 256)].reshape(BLK, 256)
        right_fac_box[slot] = (
            right_fac_box[slot] + jnp.dot(cols.T, whole, preferred_element_type=f32) * scale
        )
        for copy in leave(slot):
            copy.start()

    def leave(slot):
        return [
            pltpu.make_async_copy(left_box.at[slot], new_left.at[slot], out_sem.at[slot, 0]),
            pltpu.make_async_copy(right_fac_box.at[slot], new_right.at[slot], out_sem.at[slot, 1]),
        ]

    def forward(group):
        every[group][0].wait_recv()
        every[group][4].start()
        every[group][1].wait_recv()
        every[group][5].start()

    def place_group(group):
        half, first = group // 2, group % 2 * QROWS

        def step(col, carry):
            gathered[me_x, group, col] = inbox[half][places[col], pl.ds(first, QROWS)]
            return carry

        lax.fori_loop(0, NBC, step, 0)

    def ring_group(group):
        for copy in every[group][:4]:
            copy.start()

    def line_copy(group):
        count = QROWS * LINES
        return pltpu.make_async_copy(
            lines.at[group % 2], update.at[pl.ds(group * count, count)], line_sem.at[group % 2]
        )

    def flatten(group):
        for copy in every[group][2:]:
            copy.wait_recv()
        if group >= 2:
            line_copy(group - 2).wait()

        def step(col, carry):
            factor = factor_box[places[col]][0:1, :]
            for part in range(N_X):
                for rows in range(2):
                    for lane in range(2):
                        value = gathered[
                            part, group, col, rows * 16 : rows * 16 + 16, lane * 128 : lane * 128 + 128
                        ].astype(f32)
                        at = rows * 16 * LINES + col * 8 + part * 2 + lane
                        lines[group % 2, pl.ds(at, 16, LINES), :] = value * factor
            return carry

        lax.fori_loop(0, NBC, step, 0)
        line_copy(group).start()

    keep.wait()
    for slot in range(SLOTS):
        direct(0, slot)
    pltpu.make_async_copy(inbox_0, inbox_0, back_recv.at[0]).wait()
    place_group(0)
    ring_group(0)
    place_group(1)
    for slot in range(SLOTS):
        direct(1, slot)
    ring_group(1)
    for slot in range(SLOTS):
        share(slot)
    forward(0)
    pltpu.make_async_copy(inbox_1, inbox_1, back_recv.at[1]).wait()
    place_group(2)
    ring_group(2)
    place_group(3)
    ring_group(3)
    for copy in shares:
        copy.wait_recv()
    for slot in range(SLOTS):
        graft(slot)
    forward(1)
    fetch_left_fac.wait()
    fetch_right_fac.wait()
    statistics(0)
    forward(2)
    statistics(1)
    pltpu.make_async_copy(factor_box, factor_box, factor_recv).wait()
    flatten(0)
    flatten(1)
    forward(3)
    statistics(2)
    flatten(2)
    flatten(3)
    line_copy(2).wait()
    line_copy(3).wait()
    for group in range(GROUPS):
        for copy in every[group]:
            copy.wait_send()
    for copy in shares + copies:
        copy.wait_send()
    for slot in range(SLOTS):
        for half in range(HALVES):
            for copy in root_copies[half][slot]:
                copy.wait_send()
            finish_all(functools.partial(back, slot, half))
        finish_all(functools.partial(tell, slot))
        for copy in leave(slot):
            copy.wait()

    def sent(index, carry):
        for quarter in range(N_X):
            place, holder, away, home = piece(quarter, index)

            @pl.when(holder != me_s)
            def _():
                away().wait_send()

        return carry

    lax.fori_loop(0, CELLS, sent, 0)


def contract_last(a, b):
    return lax.dot_general(a, b, (((1,), (1,)), ((), ())), preferred_element_type=f32)


def on_device(grads, slot_table, left_factor, right_factor, left_root, right_root):
    smem = pl.BlockSpec(memory_space=pltpu.SMEM)
    hbm = pl.BlockSpec(memory_space=pl.ANY)
    dma = pltpu.SemaphoreType.DMA
    vmem = pltpu.VMEM

    new_left, new_right, update = pl.pallas_call(
        shampoo,
        in_specs=[smem] + [hbm] * 5,
        out_specs=[hbm] * 3,
        out_shape=[
            jax.ShapeDtypeStruct((SLOTS, 256, BLK), f32),
            jax.ShapeDtypeStruct((SLOTS, 256, BLK), f32),
            jax.ShapeDtypeStruct((128 * LINES, 128), f32),
        ],
        scratch_shapes=[
            vmem((2, 1, QROWS * COLS), bf16),
            vmem((2, 16 * STEP, 128), f32),
            vmem((N_X, NBC, QROWS, BLK), bf16),
            vmem((CUT, QROWS, BLK), bf16),
            vmem((NBC - CUT, QROWS, BLK), bf16),
            vmem((CUT, QROWS, BLK), bf16),
            vmem((NBC - CUT, QROWS, BLK), bf16),
        ]
        + [vmem((NBC, QROWS, BLK), bf16)] * 6
        + [
            vmem((N_X, CELLS, QROWS, BLK), bf16),
            vmem((SLOTS, SUBS, N_X, QROWS, BLK), bf16),
            vmem((SLOTS, N_X, 2, HALVES, HROWS, BLK), bf16),
            vmem((SLOTS, 256, BLK), bf16),
            vmem((SLOTS, BLK, 256), bf16),
            vmem((SLOTS, 8, 128), f32),
            vmem((SLOTS, 3, 8, 128), f32),
            vmem((SLOTS, 8, 128), f32),
            vmem((CELLS, 8, 128), f32),
            vmem((HALVES, SLOTS, SUBS, HROWS, 256), bf16),
            vmem((CELLS, HROWS, 256), bf16),
            vmem((CELLS, HROWS, 256), bf16),
            vmem((N_X, GROUPS, NBC, QROWS, 256), bf16),
            vmem((2, QROWS * LINES, 128), f32),
            vmem((SLOTS, 256, BLK), f32),
            vmem((SLOTS, 256, BLK), f32),
            pltpu.SMEM((NBC,), jnp.int32),
            dma((2,)),
            dma,
            dma,
            dma((SLOTS, 2)),
            dma((12,)),
            dma((12,)),
            dma((SLOTS, HALVES, 6)),
            dma((SLOTS, HALVES, 6)),
            dma((2,)),
            dma((N_X, CELLS)),
            dma((SLOTS,)),
            dma((SLOTS, 3)),
            dma((SLOTS, 3)),
            dma((SLOTS, SUBS)),
            dma,
            dma((HALVES, SLOTS, SUBS)),
            dma((HALVES,)),
            dma((GROUPS, 6)),
            dma((GROUPS, 6)),
            dma((2,)),
        ],
        compiler_params=pltpu.CompilerParams(
            collective_id=0, has_side_effects=True, vmem_limit_bytes=VMEM_BYTES
        ),
        name="shampoo",
    )(slot_table.T, grads, left_root.reshape(SLOTS, 2, HALVES, HROWS, BLK), right_root[0], left_factor[0], right_factor[0])

    piece = 16 * COLS
    flat, new_left, new_right = pl.pallas_call(
        finish,
        grid=(8,),
        in_specs=[pl.BlockSpec((1, piece), lambda i: (0, i)), hbm, hbm],
        out_specs=[pl.BlockSpec((1, piece), lambda i: (0, i)), hbm, hbm],
        out_shape=[
            jax.ShapeDtypeStruct((1, 128 * COLS), bf16),
            jax.ShapeDtypeStruct((SLOTS, 256, BLK), f32),
            jax.ShapeDtypeStruct((SLOTS, 256, BLK), f32),
        ],
        scratch_shapes=[dma((2,))],
        compiler_params=pltpu.CompilerParams(vmem_limit_bytes=VMEM_BYTES),
        name="finish",
    )(update.reshape(1, 128 * COLS), new_left, new_right)
    return new_left[None], new_right[None], flat


def solution(mesh):
    rows = P("shard", None, "replica", None)
    flat = P("replica", "shard")
    return jax.shard_map(
        on_device,
        mesh=mesh,
        in_specs=(flat, P(), rows, rows, rows, rows),
        out_specs=(rows, rows, flat),
        check_vma=False,
    )
```

time: 219 us -> 400 us (1.83)
  Pallas kernels: 213 us -> 399 us
  local copies, waits for them, and re-layouts: 4.69 us -> 0 us
    pallas_call x1, Pallas kernels: 10.8 us -> 194 us  [on_device(): pl.pallas_call(finish, grid=(8,), in_specs=[pl.BlockSpec((1, piece), lamb...]
    unnamed x6 -> x0, local copies, waits for them, and re-layouts: 4.69 us -> none
where the time goes in v5:
time: 400 us
  Pallas kernels  399 us (100%)
    pallas_call x1, Pallas kernels, on_device(): pl.pallas_call(shampoo, in_specs=[smem] + [hbm] * 5, out_specs=[hbm] * 3,...  205 us
    pallas_call x1, Pallas kernels, on_device(): pl.pallas_call(finish, grid=(8,), in_specs=[pl.BlockSpec((1, piece), lamb...  194 us

profile of v5, /device:TPU:0, one launch (start us, length us, event | category | flops | bytes accessed | tf_op | source)
XLA Modules:
  0.0 399.7 jit_solution(6970281933741620353)
XLA Ops:
  0.6 205.2 %shampoo.1 = (f32[3,256,1024]{2,1,0:T(8,128)}, f32[3,256,1024]{2,1,0:T(8,128)}, f32[15360,128]{1,0:T(8,128)}) custom-call(s32[3,32]{1,0:T(4,128)} %bitcast.13, bf16[1,1966080]{1,0:T(2,128)(2,1)} %grads.1, bf16[3,2,2,64,1024]{4,3,2,1,0:T(8,128)(2,1)} %bitcast.11, bf16[3,256,1024]{2,1,0:T(8,128)(2,1)} %bitcast.12, f32[3,256,1024]{2,1,0:T(8,128)} %bitcast.9, ...), custom_call_target="tpu_custom_call" | custom-call | tf_op jit(solution)/shard_map/shampoo/pallas_call | solution.py:543
  205.9 193.9 %finish.1 = (bf16[1,1966080]{1,0:T(2,128)(2,1)}, f32[3,256,1024]{2,1,0:T(8,128)}, f32[3,256,1024]{2,1,0:T(8,128)}) custom-call(f32[1,1966080]{1,0:T(1,128)} %bitcast.8, f32[3,256,1024]{2,1,0:T(8,128)} %get-tuple-element.10.left_ref, f32[3,256,1024]{2,1,0:T(8,128)} %get-tuple-element.11.right_ref), custom_call_target="tpu_custom_call" | custom-call | tf_op jit(solution)/shard_map/finish/pallas_call | solution.py:608

commit v6 on v5

--- a/solution.py
+++ b/solution.py
@@ -34,29 +34,18 @@
 LINES = NBC * 8
 
 
-def finish(flat_ref, left_ref, right_ref, out_ref, left_out, right_out, sems):
-    step = pl.program_id(0)
-    copies = (
-        pltpu.make_async_copy(left_ref, left_out, sems.at[0]),
-        pltpu.make_async_copy(right_ref, right_out, sems.at[1]),
-    )
-
-    @pl.when(step == 0)
-    def _():
-        for copy in copies:
-            copy.start()
+def finish(lines_ref, left_ref, right_ref, out_ref, left_out, right_out):
+    left_out[...] = left_ref[...]
+    right_out[...] = right_ref[...]
 
     def part(count, carry):
-        at = pl.ds(pl.multiple_of(count * COLS, COLS), COLS)
-        out_ref[:, at] = flat_ref[:, at].astype(bf16)
+        for line in range(NBC):
+            at = count * NBC + line
+            rows = lines_ref[pl.ds(pl.multiple_of(at * 8, 8), 8), :]
+            out_ref[:, pl.ds(pl.multiple_of(at * BLK, BLK), BLK)] = rows.reshape(1, BLK).astype(bf16)
         return carry
 
     lax.fori_loop(0, 16, part, 0)
-
-    @pl.when(step == pl.num_programs(0) - 1)
-    def _():
-        for copy in copies:
-            copy.wait()
 
 
 def hail(me_x, me_s):
@@ -82,10 +71,10 @@
 def shampoo(
     table, grads, left, right, left_fac, right_fac, new_left, new_right, update,
     flat, mid, tiles, fwd_a, fwd_b, part_a, part_b, from_p, from_m,
-    sum_own, sum_down, sum_up, sum_over, outbox, blocks, roots, right_box, precond,
+    sum_own, outbox, blocks, roots, right_box, precond,
     sums, sum_box, factors, factor_box, raw, inbox_0, inbox_1, gathered, lines, left_box, right_fac_box, places,
     flat_sem, right_sem, keep_sem, out_sem, send, recv, root_send, root_recv,
-    fac_sem, piece_send, piece_recv, sum_send, sum_recv, factor_send, factor_recv,
+    fac_sem, piece_send, piece_recv, block_send, block_recv, sum_send, sum_recv, factor_send, factor_recv,
     back_send, back_recv, ring_send, ring_recv, line_sem,
 ):
     me_x, me_s = lax.axis_index("replica"), lax.axis_index("shard")
@@ -111,12 +100,6 @@
         remote(tiles.at[UP, low], from_m.at[low], 3, up),
         remote(part_a, from_p.at[low], 4, down),
         remote(part_b, from_m.at[high], 5, up),
-        remote(sum_own.at[low], sum_down.at[low], 6, up),
-        remote(sum_own.at[high], sum_up.at[high], 7, down),
-        remote(sum_own.at[high], sum_down.at[high], 8, up),
-        remote(sum_own.at[low], sum_up.at[low], 9, down),
-        remote(sum_down.at[low], sum_over.at[low], 10, up),
-        remote(sum_up.at[high], sum_over.at[high], 11, down),
     ]
     def root(slot, half):
         mine, there = left.at[slot], roots.at[slot, me_x]
@@ -174,23 +157,27 @@
 
         lax.fori_loop(first, last, step, 0)
 
-    def piece(quarter, index):
-        place = index % SLOTS
-        holder = lax.rem(index // SLOTS + me_s // NBR, SUBS) * NBR + lax.rem(row + NBR - place, NBR)
-        src = outbox.at[quarter, index]
-        dst = blocks.at[place, sub, quarter]
+    def sender(src, dst, send_sem, recv_sem, target):
         away = lambda: pltpu.make_async_remote_copy(
-            src_ref=src, dst_ref=dst, send_sem=piece_send.at[quarter, index],
-            recv_sem=piece_recv.at[place], device_id=(me_x, holder), device_id_type=MESH,
-        )
-        home = lambda: pltpu.make_async_copy(src, dst, piece_recv.at[place])
-        return place, holder, away, home
-
-    def spread(quarter, total, between=()):
-        def step(index, carry):
-            place, holder, away, home = piece(quarter, index)
+            src_ref=src, dst_ref=dst, send_sem=send_sem, recv_sem=recv_sem,
+            device_id=(me_x, target), device_id_type=MESH,
+        )
+        home = lambda: pltpu.make_async_copy(src, dst, recv_sem)
+        return target, away, home
+
+    def piece(place, count):
+        holder = lax.rem(count + me_s // NBR, SUBS) * NBR + lax.rem(row + NBR - place, NBR)
+        src, dst = outbox.at[place, count], blocks.at[place, sub, me_x]
+        target, away, home = sender(
+            src, dst, piece_send.at[place, count], piece_recv.at[place], holder
+        )
+        return target, away, home
+
+    def spread(place):
+        def step(count, carry):
+            holder, away, home = piece(place, count)
             block = table[place, holder]
-            outbox[quarter, index] = total[lax.rem(jnp.maximum(block, 0), NBC)]
+            outbox[place, count] = sum_own[lax.rem(jnp.maximum(block, 0), NBC)]
 
             @pl.when(holder != me_s)
             def _():
@@ -202,11 +189,30 @@
 
             return carry
 
-        run = CELLS // max(len(between), 1)
-        for part in range(CELLS // run):
-            for copy in between[part : part + 1]:
-                copy.start()
-            lax.fori_loop(part * run, part * run + run, step, 0)
+        lax.fori_loop(0, SUBS, step, 0)
+
+    def gather_block(slot):
+        first, second = pl.ds(0, 4), pl.ds(4, 4)
+
+        def one(place, subs, x_from, x):
+            ref = blocks.at[slot, subs, x_from]
+            return cross(ref, ref, block_send.at[slot, place], block_recv.at[slot, place], x)
+
+        return [
+            one(0, first, me_x, up),
+            one(1, second, me_x, down),
+            one(2, second, me_x, up),
+            one(3, first, me_x, down),
+            one(4, first, down, up),
+            one(5, second, up, down),
+        ]
+
+    block_copies = [gather_block(slot) for slot in range(SLOTS)]
+
+    def pass_block(slot):
+        for place in range(2):
+            block_copies[slot][place].wait_recv()
+            block_copies[slot][place + 4].start()
 
     def locate(col, carry):
         wanted = row * NBC + col
@@ -261,41 +267,40 @@
     copies[1].wait_recv()
     lax.fori_loop(0, NBC - CUT, add_b, 0)
     copies[5].start()
-    for copy in root_copies[0][1][:4]:
-        copy.start()
     loads[3].wait()
     unpack(OWN, 0, NBC)
     copies[3].wait_recv()
     copies[4].wait_recv()
     lax.fori_loop(0, CUT, add_all, 0)
-    copies[6].start()
-    copies[9].start()
     copies[2].wait_recv()
     copies[5].wait_recv()
     lax.fori_loop(CUT, NBC, add_all, 0)
-    spread(me_x, sum_own, copies[7:9])
+    for slot in range(SLOTS):
+        spread(slot)
+    for half, slot in ((0, 1), (0, 2), (1, 0)):
+        for copy in root_copies[half][slot][:4]:
+            copy.start()
     lax.fori_loop(0, NBC, locate, 0)
-    copies[6].wait_recv()
-    copies[10].start()
-    copies[7].wait_recv()
-    copies[11].start()
     pass_root(0, 0)
+    for slot in range(SLOTS):
+        arrived = blocks.at[slot, :, me_x]
+        pltpu.make_async_copy(arrived, arrived, piece_recv.at[slot]).wait()
+        for copy in block_copies[slot][:4]:
+            copy.start()
     pass_root(0, 1)
-    copies[8].wait_recv()
-    spread(down, sum_down, root_copies[0][2][:4])
-    copies[9].wait_recv()
-    spread(up, sum_up, root_copies[1][0][:4])
-    copies[10].wait_recv()
-    copies[11].wait_recv()
-    spread(over, sum_over, root_copies[1][1][:4] + root_copies[1][2][:4])
     pass_root(0, 2)
-    for slot in range(SLOTS):
-        pass_root(1, slot)
+    pass_root(1, 0)
+    for slot in range(1, SLOTS):
+        for copy in root_copies[1][slot][:4]:
+            copy.start()
+    for slot in range(SLOTS):
+        pass_block(slot)
 
     fetch_right.wait()
     powers = []
     for slot in range(SLOTS):
-        pltpu.make_async_copy(blocks.at[slot], blocks.at[slot], piece_recv.at[slot]).wait()
+        for copy in block_copies[slot][2:]:
+            copy.wait_recv()
         grad = blocks[slot].reshape(BLK, BLK)
         precond[slot] = contract_last(grad, right_box[slot]).astype(bf16)
         powers.append(jnp.sum(jnp.square(grad.astype(f32))) / (BLK * BLK))
@@ -303,14 +308,6 @@
     def target_of(place, count):
         target_sub = lax.rem(count + sub, SUBS)
         return target_sub, lax.rem(me_s + place, NBR) * SUBS + target_sub
-
-    def sender(src, dst, send_sem, recv_sem, target):
-        away = lambda: pltpu.make_async_remote_copy(
-            src_ref=src, dst_ref=dst, send_sem=send_sem, recv_sem=recv_sem,
-            device_id=(me_x, target), device_id_type=MESH,
-        )
-        home = lambda: pltpu.make_async_copy(src, dst, recv_sem)
-        return target, away, home
 
     def back(place, half, count):
         target_sub, target = target_of(place, count)
@@ -469,6 +466,8 @@
     keep.wait()
     for slot in range(SLOTS):
         direct(0, slot)
+    for slot in range(1, SLOTS):
+        pass_root(1, slot)
     pltpu.make_async_copy(inbox_0, inbox_0, back_recv.at[0]).wait()
     place_group(0)
     ring_group(0)
@@ -514,20 +513,11 @@
                 copy.wait_send()
             finish_all(functools.partial(back, slot, half))
         finish_all(functools.partial(tell, slot))
+        finish_all(functools.partial(piece, slot))
+        for copy in block_copies[slot]:
+            copy.wait_send()
         for copy in leave(slot):
             copy.wait()
-
-    def sent(index, carry):
-        for quarter in range(N_X):
-            place, holder, away, home = piece(quarter, index)
-
-            @pl.when(holder != me_s)
-            def _():
-                away().wait_send()
-
-        return carry
-
-    lax.fori_loop(0, CELLS, sent, 0)
 
 
 def contract_last(a, b):
@@ -558,9 +548,9 @@
             vmem((CUT, QROWS, BLK), bf16),
             vmem((NBC - CUT, QROWS, BLK), bf16),
         ]
-        + [vmem((NBC, QROWS, BLK), bf16)] * 6
+        + [vmem((NBC, QROWS, BLK), bf16)] * 3
         + [
-            vmem((N_X, CELLS, QROWS, BLK), bf16),
+            vmem((SLOTS, SUBS, QROWS, BLK), bf16),
             vmem((SLOTS, SUBS, N_X, QROWS, BLK), bf16),
             vmem((SLOTS, N_X, 2, HALVES, HROWS, BLK), bf16),
             vmem((SLOTS, 256, BLK), bf16),
@@ -581,13 +571,15 @@
             dma,
             dma,
             dma((SLOTS, 2)),
-            dma((12,)),
-            dma((12,)),
+            dma((6,)),
+            dma((6,)),
             dma((SLOTS, HALVES, 6)),
             dma((SLOTS, HALVES, 6)),
             dma((2,)),
-            dma((N_X, CELLS)),
+            dma((SLOTS, SUBS)),
             dma((SLOTS,)),
+            dma((SLOTS, 6)),
+            dma((SLOTS, 6)),
             dma((SLOTS, 3)),
             dma((SLOTS, 3)),
             dma((SLOTS, SUBS)),
@@ -605,20 +597,22 @@
     )(slot_table.T, grads, left_root.reshape(SLOTS, 2, HALVES, HROWS, BLK), right_root[0], left_factor[0], right_factor[0])
 
     piece = 16 * COLS
+    lines_in = pl.BlockSpec((16 * LINES, 128), lambda i: (i, 0))
+    flat_out = pl.BlockSpec((1, piece), lambda i: (0, i))
+    table_block = pl.BlockSpec((SLOTS, 32, BLK), lambda i: (0, i, 0))
     flat, new_left, new_right = pl.pallas_call(
         finish,
         grid=(8,),
-        in_specs=[pl.BlockSpec((1, piece), lambda i: (0, i)), hbm, hbm],
-        out_specs=[pl.BlockSpec((1, piece), lambda i: (0, i)), hbm, hbm],
+        in_specs=[lines_in, table_block, table_block],
+        out_specs=[flat_out, table_block, table_block],
         out_shape=[
             jax.ShapeDtypeStruct((1, 128 * COLS), bf16),
             jax.ShapeDtypeStruct((SLOTS, 256, BLK), f32),
             jax.ShapeDtypeStruct((SLOTS, 256, BLK), f32),
         ],
-        scratch_shapes=[dma((2,))],
         compiler_params=pltpu.CompilerParams(vmem_limit_bytes=VMEM_BYTES),
         name="finish",
-    )(update.reshape(1, 128 * COLS), new_left, new_right)
+    )(update, new_left, new_right)
     return new_left[None], new_right[None], flat
 
 

time: 400 us -> 213 us (0.53)
  Pallas kernels: 399 us -> 211 us
    pallas_call x1, Pallas kernels: 194 us -> 14.9 us  [on_device(): pl.pallas_call(finish, grid=(8,), in_specs=[lines_in, table_block, table_...]
    pallas_call x1, Pallas kernels: 205 us -> 196 us  [on_device(): pl.pallas_call(shampoo, in_specs=[smem] + [hbm] * 5, out_specs=[hbm] * 3,...]
where the time goes in v6:
time: 213 us; the launch traced here: 212 us
  Pallas kernels  211 us (99%)
    pallas_call x1, Pallas kernels, on_device(): pl.pallas_call(shampoo, in_specs=[smem] + [hbm] * 5, out_specs=[hbm] * 3,...  196 us
    pallas_call x1, Pallas kernels, on_device(): pl.pallas_call(finish, grid=(8,), in_specs=[lines_in, table_block, table_...  14.9 us

profile of v6, /device:TPU:0, one launch (start us, length us, event | category | flops | bytes accessed | tf_op | source)
XLA Modules:
  0.0 212.0 jit_solution(6999056808543105413)
XLA Ops:
  0.6 196.5 %shampoo.1 = (f32[3,256,1024]{2,1,0:T(8,128)}, f32[3,256,1024]{2,1,0:T(8,128)}, f32[15360,128]{1,0:T(8,128)}) custom-call(s32[3,32]{1,0:T(4,128)} %bitcast.11, bf16[1,1966080]{1,0:T(2,128)(2,1)} %grads.1, bf16[3,2,2,64,1024]{4,3,2,1,0:T(8,128)(2,1)} %bitcast.9, bf16[3,256,1024]{2,1,0:T(8,128)(2,1)} %bitcast.10, f32[3,256,1024]{2,1,0:T(8,128)} %bitcast.7, ...), custom_call_target="tpu_custom_call" | custom-call | tf_op jit(solution)/shard_map/shampoo/pallas_call | solution.py:533
  197.1 14.9 %finish.1 = (bf16[1,1966080]{1,0:T(2,128)(2,1)}, f32[3,256,1024]{2,1,0:T(8,128)}, f32[3,256,1024]{2,1,0:T(8,128)}) custom-call(f32[15360,128]{1,0:T(8,128)} %get-tuple-element.9.lines_ref, f32[3,256,1024]{2,1,0:T(8,128)} %get-tuple-element.10.left_ref, f32[3,256,1024]{2,1,0:T(8,128)} %get-tuple-element.11.right_ref), custom_call_target="tpu_custom_call" | custom-call | tf_op jit(solution)/shard_map/finish/pallas_call | solution.py:603

commit v7 on v5

--- a/solution.py
+++ b/solution.py
@@ -31,32 +31,6 @@
 STEP = 9
 HALVES = 2
 HROWS = 64
-LINES = NBC * 8
-
-
-def finish(flat_ref, left_ref, right_ref, out_ref, left_out, right_out, sems):
-    step = pl.program_id(0)
-    copies = (
-        pltpu.make_async_copy(left_ref, left_out, sems.at[0]),
-        pltpu.make_async_copy(right_ref, right_out, sems.at[1]),
-    )
-
-    @pl.when(step == 0)
-    def _():
-        for copy in copies:
-            copy.start()
-
-    def part(count, carry):
-        at = pl.ds(pl.multiple_of(count * COLS, COLS), COLS)
-        out_ref[:, at] = flat_ref[:, at].astype(bf16)
-        return carry
-
-    lax.fori_loop(0, 16, part, 0)
-
-    @pl.when(step == pl.num_programs(0) - 1)
-    def _():
-        for copy in copies:
-            copy.wait()
 
 
 def hail(me_x, me_s):
@@ -83,10 +57,10 @@
     table, grads, left, right, left_fac, right_fac, new_left, new_right, update,
     flat, mid, tiles, fwd_a, fwd_b, part_a, part_b, from_p, from_m,
     sum_own, sum_down, sum_up, sum_over, outbox, blocks, roots, right_box, precond,
-    sums, sum_box, factors, factor_box, raw, inbox_0, inbox_1, gathered, lines, left_box, right_fac_box, places,
+    sums, sum_box, factors, factor_box, raw, inbox_0, inbox_1, gathered, left_box, right_fac_box, places,
     flat_sem, right_sem, keep_sem, out_sem, send, recv, root_send, root_recv,
     fac_sem, piece_send, piece_recv, sum_send, sum_recv, factor_send, factor_recv,
-    back_send, back_recv, ring_send, ring_recv, line_sem,
+    back_send, back_recv, ring_send, ring_recv,
 ):
     me_x, me_s = lax.axis_index("replica"), lax.axis_index("shard")
     row, sub = me_s // SUBS, lax.rem(me_s, SUBS)
@@ -187,7 +161,8 @@
         return place, holder, away, home
 
     def spread(quarter, total, between=()):
-        def step(index, carry):
+        def step(count, carry):
+            index = lax.rem(count * 7 + me_s * 5, CELLS)
             place, holder, away, home = piece(quarter, index)
             block = table[place, holder]
             outbox[quarter, index] = total[lax.rem(jnp.maximum(block, 0), NBC)]
@@ -301,7 +276,7 @@
         powers.append(jnp.sum(jnp.square(grad.astype(f32))) / (BLK * BLK))
 
     def target_of(place, count):
-        target_sub = lax.rem(count + sub, SUBS)
+        target_sub = lax.rem(3 * count + 3 * sub + 2 * row, SUBS)
         return target_sub, lax.rem(me_s + place, NBR) * SUBS + target_sub
 
     def sender(src, dst, send_sem, recv_sem, target):
@@ -439,32 +414,35 @@
         for copy in every[group][:4]:
             copy.start()
 
-    def line_copy(group):
-        count = QROWS * LINES
-        return pltpu.make_async_copy(
-            lines.at[group % 2], update.at[pl.ds(group * count, count)], line_sem.at[group % 2]
-        )
+    def flat_copy(group):
+        at = pl.ds(group * size, size)
+        return pltpu.make_async_copy(flat.at[group % 2], update.at[:, at], flat_sem.at[group % 2])
 
     def flatten(group):
         for copy in every[group][2:]:
             copy.wait_recv()
         if group >= 2:
-            line_copy(group - 2).wait()
+            flat_copy(group - 2).wait()
 
         def step(col, carry):
             factor = factor_box[places[col]][0:1, :]
-            for part in range(N_X):
-                for rows in range(2):
+            for rows in range(2):
+                for part in range(N_X):
                     for lane in range(2):
                         value = gathered[
                             part, group, col, rows * 16 : rows * 16 + 16, lane * 128 : lane * 128 + 128
                         ].astype(f32)
-                        at = rows * 16 * LINES + col * 8 + part * 2 + lane
-                        lines[group % 2, pl.ds(at, 16, LINES), :] = value * factor
+                        mid[rows, pl.ds(part * 2 + lane, 16, STEP), :] = value * factor
+            for rows in range(2):
+                for line in range(16):
+                    at = pl.multiple_of((rows * 16 + line) * COLS + col * BLK, BLK)
+                    flat[group % 2, :, pl.ds(at, BLK)] = (
+                        mid[rows, line * STEP : line * STEP + 8, :].reshape(1, BLK).astype(bf16)
+                    )
             return carry
 
         lax.fori_loop(0, NBC, step, 0)
-        line_copy(group).start()
+        flat_copy(group).start()
 
     keep.wait()
     for slot in range(SLOTS):
@@ -501,8 +479,8 @@
     statistics(2)
     flatten(2)
     flatten(3)
-    line_copy(2).wait()
-    line_copy(3).wait()
+    flat_copy(2).wait()
+    flat_copy(3).wait()
     for group in range(GROUPS):
         for copy in every[group]:
             copy.wait_send()
@@ -547,7 +525,7 @@
         out_shape=[
             jax.ShapeDtypeStruct((SLOTS, 256, BLK), f32),
             jax.ShapeDtypeStruct((SLOTS, 256, BLK), f32),
-            jax.ShapeDtypeStruct((128 * LINES, 128), f32),
+            jax.ShapeDtypeStruct((1, 128 * COLS), bf16),
         ],
         scratch_shapes=[
             vmem((2, 1, QROWS * COLS), bf16),
@@ -573,7 +551,6 @@
             vmem((CELLS, HROWS, 256), bf16),
             vmem((CELLS, HROWS, 256), bf16),
             vmem((N_X, GROUPS, NBC, QROWS, 256), bf16),
-            vmem((2, QROWS * LINES, 128), f32),
             vmem((SLOTS, 256, BLK), f32),
             vmem((SLOTS, 256, BLK), f32),
             pltpu.SMEM((NBC,), jnp.int32),
@@ -596,7 +573,6 @@
             dma((HALVES,)),
             dma((GROUPS, 6)),
             dma((GROUPS, 6)),
-            dma((2,)),
         ],
         compiler_params=pltpu.CompilerParams(
             collective_id=0, has_side_effects=True, vmem_limit_bytes=VMEM_BYTES
@@ -604,22 +580,7 @@
         name="shampoo",
     )(slot_table.T, grads, left_root.reshape(SLOTS, 2, HALVES, HROWS, BLK), right_root[0], left_factor[0], right_factor[0])
 
-    piece = 16 * COLS
-    flat, new_left, new_right = pl.pallas_call(
-        finish,
-        grid=(8,),
-        in_specs=[pl.BlockSpec((1, piece), lambda i: (0, i)), hbm, hbm],
-        out_specs=[pl.BlockSpec((1, piece), lambda i: (0, i)), hbm, hbm],
-        out_shape=[
-            jax.ShapeDtypeStruct((1, 128 * COLS), bf16),
-            jax.ShapeDtypeStruct((SLOTS, 256, BLK), f32),
-            jax.ShapeDtypeStruct((SLOTS, 256, BLK), f32),
-        ],
-        scratch_shapes=[dma((2,))],
-        compiler_params=pltpu.CompilerParams(vmem_limit_bytes=VMEM_BYTES),
-        name="finish",
-    )(update.reshape(1, 128 * COLS), new_left, new_right)
-    return new_left[None], new_right[None], flat
+    return new_left[None], new_right[None], update
 
 
 def solution(mesh):

time: 400 us -> 217 us (0.54)
  Pallas kernels: 399 us -> 205 us
  local copies, waits for them, and re-layouts: 0 us -> 11.5 us
    pallas_call x1 -> x0, Pallas kernels: 194 us -> none  [on_device(): pl.pallas_call(finish, grid=(8,), in_specs=[pl.BlockSpec((1, piece), lamb...]
    unnamed x0 -> x5, local copies, waits for them, and re-layouts: none -> 11.5 us
where the time goes in v7:
time: 217 us
  Pallas kernels  205 us (94%)
  local copies, waits for them, and re-layouts  11.5 us (5%)
    pallas_call x1, Pallas kernels, on_device(): pl.pallas_call(shampoo, in_specs=[smem] + [hbm] * 5, out_specs=[hbm] * 3,...  205 us
    unnamed x5, local copies, waits for them, and re-layouts  11.5 us

profile of v7, /device:TPU:0, one launch (start us, length us, event | category | flops | bytes accessed | tf_op | source)
XLA Modules:
  0.0 216.7 jit_solution(16172118884939666209)
XLA Ops:
  0.6 204.5 %shampoo.1 = (f32[3,256,1024]{2,1,0:T(8,128)}, f32[3,256,1024]{2,1,0:T(8,128)}, bf16[1,1966080]{1,0:T(2,128)(2,1)}) custom-call(s32[3,32]{1,0:T(4,128)} %bitcast.13, bf16[1,1966080]{1,0:T(2,128)(2,1)} %grads.1, bf16[3,2,2,64,1024]{4,3,2,1,0:T(8,128)(2,1)} %bitcast.11, bf16[3,256,1024]{2,1,0:T(8,128)(2,1)} %bitcast.12, f32[3,256,1024]{2,1,0:T(8,128)} %bitcast.7, ...), custom_call_target="tpu_custom_call" | custom-call | tf_op jit(solution)/shard_map/shampoo/pallas_call | solution.py:521
  205.2 0.0 copy-start
  205.2 4.1 %copy.12 = f32[1,3,256,1024]{3,2,1,0:T(8,128)} copy(f32[1,3,256,1024]{3,2,1,0:T(8,128)} %bitcast.10) | data formatting | bytes 6291456
  209.3 4.2 %copy.13 = f32[1,3,256,1024]{3,2,1,0:T(8,128)} copy(f32[1,3,256,1024]{3,2,1,0:T(8,128)} %bitcast.9) | data formatting | bytes 6291456
  213.5 0.0 copy-done
  213.5 3.2 %copy.14 = bf16[1,1966080]{1,0:T(2,128)(2,1)} copy(bf16[1,1966080]{1,0:T(2,128)(2,1)S(1)} %copy-done) | data formatting | bytes 7864320
Async XLA Ops:
  205.2 8.3 %copy-start = (bf16[1,1966080]{1,0:T(2,128)(2,1)S(1)}, bf16[1,1966080]{1,0:T(2,128)(2,1)}, u32[]{:S(2)}) copy-start(bf16[1,1966080]{1,0:T(2,128)(2,1)} %get-tuple-element.14) | copy-start | bytes 11796484

commit v8 on v6

--- a/solution.py
+++ b/solution.py
@@ -31,21 +31,31 @@
 STEP = 9
 HALVES = 2
 HROWS = 64
-LINES = NBC * 8
-
-
-def finish(lines_ref, left_ref, right_ref, out_ref, left_out, right_out):
-    left_out[...] = left_ref[...]
-    right_out[...] = right_ref[...]
-
-    def part(count, carry):
-        for line in range(NBC):
-            at = count * NBC + line
-            rows = lines_ref[pl.ds(pl.multiple_of(at * 8, 8), 8), :]
-            out_ref[:, pl.ds(pl.multiple_of(at * BLK, BLK), BLK)] = rows.reshape(1, BLK).astype(bf16)
-        return carry
-
-    lax.fori_loop(0, 16, part, 0)
+PARTS = 4
+
+
+def deliver(*refs):
+    sources, targets, boxes = refs[:3], refs[3:6], refs[6:9]
+    read_sem, write_sem = refs[9:]
+    reads, writes = [], []
+    for index in range(3):
+        for part in range(PARTS):
+            if index == 0:
+                count = 128 * COLS // PARTS
+                at = (slice(None), pl.ds(part * count, count))
+            else:
+                count = SLOTS * 256 // PARTS
+                at = (pl.ds(part * count, count),)
+            box = boxes[index].at[at]
+            reads.append(pltpu.make_async_copy(sources[index].at[at], box, read_sem.at[index, part]))
+            writes.append(pltpu.make_async_copy(box, targets[index].at[at], write_sem.at[index, part]))
+    for read in reads:
+        read.start()
+    for read, write in zip(reads, writes):
+        read.wait()
+        write.start()
+    for write in writes:
+        write.wait()
 
 
 def hail(me_x, me_s):
@@ -72,10 +82,10 @@
     table, grads, left, right, left_fac, right_fac, new_left, new_right, update,
     flat, mid, tiles, fwd_a, fwd_b, part_a, part_b, from_p, from_m,
     sum_own, outbox, blocks, roots, right_box, precond,
-    sums, sum_box, factors, factor_box, raw, inbox_0, inbox_1, gathered, lines, left_box, right_fac_box, places,
+    sums, sum_box, factors, factor_box, raw, inbox_0, inbox_1, gathered, left_box, right_fac_box, places,
     flat_sem, right_sem, keep_sem, out_sem, send, recv, root_send, root_recv,
     fac_sem, piece_send, piece_recv, block_send, block_recv, sum_send, sum_recv, factor_send, factor_recv,
-    back_send, back_recv, ring_send, ring_recv, line_sem,
+    back_send, back_recv, ring_send, ring_recv,
 ):
     me_x, me_s = lax.axis_index("replica"), lax.axis_index("shard")
     row, sub = me_s // SUBS, lax.rem(me_s, SUBS)
@@ -277,7 +287,7 @@
     lax.fori_loop(CUT, NBC, add_all, 0)
     for slot in range(SLOTS):
         spread(slot)
-    for half, slot in ((0, 1), (0, 2), (1, 0)):
+    for half, slot in ((0, 1), (0, 2), (1, 0), (1, 1)):
         for copy in root_copies[half][slot][:4]:
             copy.start()
     lax.fori_loop(0, NBC, locate, 0)
@@ -287,26 +297,17 @@
         pltpu.make_async_copy(arrived, arrived, piece_recv.at[slot]).wait()
         for copy in block_copies[slot][:4]:
             copy.start()
+    for copy in root_copies[1][2][:4]:
+        copy.start()
     pass_root(0, 1)
     pass_root(0, 2)
-    pass_root(1, 0)
-    for slot in range(1, SLOTS):
-        for copy in root_copies[1][slot][:4]:
-            copy.start()
     for slot in range(SLOTS):
         pass_block(slot)
-
-    fetch_right.wait()
-    powers = []
-    for slot in range(SLOTS):
-        for copy in block_copies[slot][2:]:
-            copy.wait_recv()
-        grad = blocks[slot].reshape(BLK, BLK)
-        precond[slot] = contract_last(grad, right_box[slot]).astype(bf16)
-        powers.append(jnp.sum(jnp.square(grad.astype(f32))) / (BLK * BLK))
+    for slot in range(SLOTS):
+        pass_root(1, slot)
 
     def target_of(place, count):
-        target_sub = lax.rem(count + sub, SUBS)
+        target_sub = lax.rem(3 * count + 3 * sub + 2 * row, SUBS)
         return target_sub, lax.rem(me_s + place, NBR) * SUBS + target_sub
 
     def back(place, half, count):
@@ -436,38 +437,45 @@
         for copy in every[group][:4]:
             copy.start()
 
-    def line_copy(group):
-        count = QROWS * LINES
-        return pltpu.make_async_copy(
-            lines.at[group % 2], update.at[pl.ds(group * count, count)], line_sem.at[group % 2]
-        )
+    def flat_copy(group):
+        at = pl.ds(group * size, size)
+        return pltpu.make_async_copy(flat.at[group % 2], update.at[:, at], flat_sem.at[group % 2])
 
     def flatten(group):
         for copy in every[group][2:]:
             copy.wait_recv()
         if group >= 2:
-            line_copy(group - 2).wait()
+            flat_copy(group - 2).wait()
 
         def step(col, carry):
             factor = factor_box[places[col]][0:1, :]
-            for part in range(N_X):
-                for rows in range(2):
+            for rows in range(2):
+                for part in range(N_X):
                     for lane in range(2):
                         value = gathered[
                             part, group, col, rows * 16 : rows * 16 + 16, lane * 128 : lane * 128 + 128
                         ].astype(f32)
-                        at = rows * 16 * LINES + col * 8 + part * 2 + lane
-                        lines[group % 2, pl.ds(at, 16, LINES), :] = value * factor
+                        mid[rows, pl.ds(part * 2 + lane, 16, STEP), :] = value * factor
+            for rows in range(2):
+                for line in range(16):
+                    at = pl.multiple_of((rows * 16 + line) * COLS + col * BLK, BLK)
+                    flat[group % 2, :, pl.ds(at, BLK)] = (
+                        mid[rows, line * STEP : line * STEP + 8, :].reshape(1, BLK).astype(bf16)
+                    )
             return carry
 
         lax.fori_loop(0, NBC, step, 0)
-        line_copy(group).start()
+        flat_copy(group).start()
 
     keep.wait()
-    for slot in range(SLOTS):
+    fetch_right.wait()
+    powers = []
+    for slot in range(SLOTS):
+        for copy in block_copies[slot][2:]:
+            copy.wait_recv()
+        grad = blocks[slot].reshape(BLK, BLK)
+        precond[slot] = contract_last(grad, right_box[slot]).astype(bf16)
         direct(0, slot)
-    for slot in range(1, SLOTS):
-        pass_root(1, slot)
     pltpu.make_async_copy(inbox_0, inbox_0, back_recv.at[0]).wait()
     place_group(0)
     ring_group(0)
@@ -483,6 +491,9 @@
     ring_group(2)
     place_group(3)
     ring_group(3)
+    for slot in range(SLOTS):
+        grad = blocks[slot].reshape(BLK, BLK)
+        powers.append(jnp.sum(jnp.square(grad.astype(f32))) / (BLK * BLK))
     for copy in shares:
         copy.wait_recv()
     for slot in range(SLOTS):
@@ -500,8 +511,8 @@
     statistics(2)
     flatten(2)
     flatten(3)
-    line_copy(2).wait()
-    line_copy(3).wait()
+    flat_copy(2).wait()
+    flat_copy(3).wait()
     for group in range(GROUPS):
         for copy in every[group]:
             copy.wait_send()
@@ -537,7 +548,7 @@
         out_shape=[
             jax.ShapeDtypeStruct((SLOTS, 256, BLK), f32),
             jax.ShapeDtypeStruct((SLOTS, 256, BLK), f32),
-            jax.ShapeDtypeStruct((128 * LINES, 128), f32),
+            jax.ShapeDtypeStruct((1, 128 * COLS), bf16),
         ],
         scratch_shapes=[
             vmem((2, 1, QROWS * COLS), bf16),
@@ -563,7 +574,6 @@
             vmem((CELLS, HROWS, 256), bf16),
             vmem((CELLS, HROWS, 256), bf16),
             vmem((N_X, GROUPS, NBC, QROWS, 256), bf16),
-            vmem((2, QROWS * LINES, 128), f32),
             vmem((SLOTS, 256, BLK), f32),
             vmem((SLOTS, 256, BLK), f32),
             pltpu.SMEM((NBC,), jnp.int32),
@@ -588,7 +598,6 @@
             dma((HALVES,)),
             dma((GROUPS, 6)),
             dma((GROUPS, 6)),
-            dma((2,)),
         ],
         compiler_params=pltpu.CompilerParams(
             collective_id=0, has_side_effects=True, vmem_limit_bytes=VMEM_BYTES
@@ -596,24 +605,22 @@
         name="shampoo",
     )(slot_table.T, grads, left_root.reshape(SLOTS, 2, HALVES, HROWS, BLK), right_root[0], left_factor[0], right_factor[0])
 
-    piece = 16 * COLS
-    lines_in = pl.BlockSpec((16 * LINES, 128), lambda i: (i, 0))
-    flat_out = pl.BlockSpec((1, piece), lambda i: (0, i))
-    table_block = pl.BlockSpec((SLOTS, 32, BLK), lambda i: (0, i, 0))
+    shapes = [
+        jax.ShapeDtypeStruct((1, 128 * COLS), bf16),
+        jax.ShapeDtypeStruct((SLOTS * 256, BLK), f32),
+        jax.ShapeDtypeStruct((SLOTS * 256, BLK), f32),
+    ]
     flat, new_left, new_right = pl.pallas_call(
-        finish,
-        grid=(8,),
-        in_specs=[lines_in, table_block, table_block],
-        out_specs=[flat_out, table_block, table_block],
-        out_shape=[
-            jax.ShapeDtypeStruct((1, 128 * COLS), bf16),
-            jax.ShapeDtypeStruct((SLOTS, 256, BLK), f32),
-            jax.ShapeDtypeStruct((SLOTS, 256, BLK), f32),
-        ],
+        deliver,
+        in_specs=[hbm] * 3,
+        out_specs=[hbm] * 3,
+        out_shape=shapes,
+        scratch_shapes=[vmem(shape.shape, shape.dtype) for shape in shapes] + [dma((3, PARTS))] * 2,
         compiler_params=pltpu.CompilerParams(vmem_limit_bytes=VMEM_BYTES),
-        name="finish",
-    )(update, new_left, new_right)
-    return new_left[None], new_right[None], flat
+        name="deliver",
+    )(update, new_left.reshape(SLOTS * 256, BLK), new_right.reshape(SLOTS * 256, BLK))
+    rows = (1, SLOTS, 256, BLK)
+    return new_left.reshape(rows), new_right.reshape(rows), flat
 
 
 def solution(mesh):

time: 213 us -> 204 us (0.958)
  Pallas kernels: 211 us -> 203 us
    pallas_call x1, Pallas kernels: 14.9 us -> 10.6 us  [on_device(): pl.pallas_call(deliver, in_specs=[hbm] * 3, out_specs=[hbm] * 3, out_shap...]
    pallas_call x1, Pallas kernels: 196 us -> 192 us  [on_device(): pl.pallas_call(shampoo, in_specs=[smem] + [hbm] * 5, out_specs=[hbm] * 3,...]
where the time goes in v8:
time: 204 us; the launch traced here: 203 us
  Pallas kernels  203 us (100%)
    pallas_call x1, Pallas kernels, on_device(): pl.pallas_call(shampoo, in_specs=[smem] + [hbm] * 5, out_specs=[hbm] * 3,...  192 us
    pallas_call x1, Pallas kernels, on_device(): pl.pallas_call(deliver, in_specs=[hbm] * 3, out_specs=[hbm] * 3, out_shap...  10.6 us

profile of v8, /device:TPU:0, one launch (start us, length us, event | category | flops | bytes accessed | tf_op | source)
XLA Modules:
  0.0 203.5 jit_solution(12316706639278025758)
XLA Ops:
  0.6 192.3 %shampoo.1 = (f32[3,256,1024]{2,1,0:T(8,128)}, f32[3,256,1024]{2,1,0:T(8,128)}, bf16[1,1966080]{1,0:T(2,128)(2,1)}) custom-call(s32[3,32]{1,0:T(4,128)} %bitcast.15, bf16[1,1966080]{1,0:T(2,128)(2,1)} %grads.1, bf16[3,2,2,64,1024]{4,3,2,1,0:T(8,128)(2,1)} %bitcast.13, bf16[3,256,1024]{2,1,0:T(8,128)(2,1)} %bitcast.14, f32[3,256,1024]{2,1,0:T(8,128)} %bitcast.9, ...), custom_call_target="tpu_custom_call" | custom-call | tf_op jit(solution)/shard_map/shampoo/pallas_call | solution.py:544
  192.9 10.6 %deliver.1 = (bf16[1,1966080]{1,0:T(2,128)(2,1)}, f32[768,1024]{1,0:T(8,128)}, f32[768,1024]{1,0:T(8,128)}) custom-call(bf16[1,1966080]{1,0:T(2,128)(2,1)} %get-tuple-element.9.refs_0_, f32[768,1024]{1,0:T(8,128)} %bitcast.11, f32[768,1024]{1,0:T(8,128)} %bitcast.12), custom_call_target="tpu_custom_call" | custom-call | tf_op jit(solution)/shard_map/deliver/pallas_call | solution.py:613

commit v9 on v8

--- a/solution.py
+++ b/solution.py
@@ -81,7 +81,7 @@
 def shampoo(
     table, grads, left, right, left_fac, right_fac, new_left, new_right, update,
     flat, mid, tiles, fwd_a, fwd_b, part_a, part_b, from_p, from_m,
-    sum_own, outbox, blocks, roots, right_box, precond,
+    sum_own, sum_down, sum_up, outbox, blocks, roots, right_box, precond,
     sums, sum_box, factors, factor_box, raw, inbox_0, inbox_1, gathered, left_box, right_fac_box, places,
     flat_sem, right_sem, keep_sem, out_sem, send, recv, root_send, root_recv,
     fac_sem, piece_send, piece_recv, block_send, block_recv, sum_send, sum_recv, factor_send, factor_recv,
@@ -110,6 +110,10 @@
         remote(tiles.at[UP, low], from_m.at[low], 3, up),
         remote(part_a, from_p.at[low], 4, down),
         remote(part_b, from_m.at[high], 5, up),
+        remote(sum_own.at[low], sum_down.at[low], 6, up),
+        remote(sum_own.at[high], sum_up.at[high], 7, down),
+        remote(sum_own.at[high], sum_down.at[high], 8, up),
+        remote(sum_own.at[low], sum_up.at[low], 9, down),
     ]
     def root(slot, half):
         mine, there = left.at[slot], roots.at[slot, me_x]
@@ -130,6 +134,10 @@
         ]
 
     root_copies = [[root(slot, half) for slot in range(SLOTS)] for half in range(HALVES)]
+
+    def start_root(half, slot):
+        for copy in root_copies[half][slot][:4]:
+            copy.start()
 
     def pass_root(half, slot):
         for place in range(2):
@@ -175,54 +183,48 @@
         home = lambda: pltpu.make_async_copy(src, dst, recv_sem)
         return target, away, home
 
-    def piece(place, count):
+    sums_of = (sum_own, sum_down, sum_up)
+    from_of = (me_x, down, up)
+
+    def piece(origin, place, count):
         holder = lax.rem(count + me_s // NBR, SUBS) * NBR + lax.rem(row + NBR - place, NBR)
-        src, dst = outbox.at[place, count], blocks.at[place, sub, me_x]
-        target, away, home = sender(
-            src, dst, piece_send.at[place, count], piece_recv.at[place], holder
-        )
-        return target, away, home
-
-    def spread(place):
-        def step(count, carry):
-            holder, away, home = piece(place, count)
-            block = table[place, holder]
-            outbox[place, count] = sum_own[lax.rem(jnp.maximum(block, 0), NBC)]
-
-            @pl.when(holder != me_s)
-            def _():
-                away().start()
-
-            @pl.when(holder == me_s)
-            def _():
-                home().start()
-
-            return carry
-
-        lax.fori_loop(0, SUBS, step, 0)
+        src, dst = outbox.at[origin, place, count], blocks.at[place, sub, from_of[origin]]
+        return sender(
+            src, dst, piece_send.at[origin, place, count], piece_recv.at[origin, place], holder
+        )
+
+    def spread(origin):
+        for place in range(SLOTS):
+
+            def step(count, carry):
+                holder, away, home = piece(origin, place, count)
+                block = table[place, holder]
+                outbox[origin, place, count] = sums_of[origin][lax.rem(jnp.maximum(block, 0), NBC)]
+
+                @pl.when(holder != me_s)
+                def _():
+                    away().start()
+
+                @pl.when(holder == me_s)
+                def _():
+                    home().start()
+
+                return carry
+
+            lax.fori_loop(0, SUBS, step, 0)
 
     def gather_block(slot):
-        first, second = pl.ds(0, 4), pl.ds(4, 4)
-
         def one(place, subs, x_from, x):
             ref = blocks.at[slot, subs, x_from]
             return cross(ref, ref, block_send.at[slot, place], block_recv.at[slot, place], x)
 
-        return [
-            one(0, first, me_x, up),
-            one(1, second, me_x, down),
-            one(2, second, me_x, up),
-            one(3, first, me_x, down),
-            one(4, first, down, up),
-            one(5, second, up, down),
-        ]
+        return [one(0, pl.ds(0, 4), down, up), one(1, pl.ds(4, 4), up, down)]
 
     block_copies = [gather_block(slot) for slot in range(SLOTS)]
 
-    def pass_block(slot):
-        for place in range(2):
-            block_copies[slot][place].wait_recv()
-            block_copies[slot][place + 4].start()
+    def arrive(origin, slot):
+        pieces = blocks.at[slot, :, from_of[origin]]
+        pltpu.make_async_copy(pieces, pieces, piece_recv.at[origin, slot]).wait()
 
     def locate(col, carry):
         wanted = row * NBC + col
@@ -259,8 +261,7 @@
     admitted()
     keep.start()
     copies[0].start()
-    for copy in root_copies[0][0][:4]:
-        copy.start()
+    start_root(0, 0)
     unpack(OVER, CUT, NBC)
     copies[1].start()
     loads[2].start()
@@ -282,27 +283,34 @@
     copies[3].wait_recv()
     copies[4].wait_recv()
     lax.fori_loop(0, CUT, add_all, 0)
+    copies[6].start()
+    copies[9].start()
     copies[2].wait_recv()
     copies[5].wait_recv()
     lax.fori_loop(CUT, NBC, add_all, 0)
-    for slot in range(SLOTS):
-        spread(slot)
-    for half, slot in ((0, 1), (0, 2), (1, 0), (1, 1)):
-        for copy in root_copies[half][slot][:4]:
-            copy.start()
+    copies[7].start()
+    copies[8].start()
+    spread(0)
+    start_root(0, 1)
+    start_root(0, 2)
     lax.fori_loop(0, NBC, locate, 0)
     pass_root(0, 0)
-    for slot in range(SLOTS):
-        arrived = blocks.at[slot, :, me_x]
-        pltpu.make_async_copy(arrived, arrived, piece_recv.at[slot]).wait()
-        for copy in block_copies[slot][:4]:
-            copy.start()
-    for copy in root_copies[1][2][:4]:
-        copy.start()
+    copies[6].wait_recv()
+    copies[8].wait_recv()
+    spread(1)
+    start_root(1, 0)
+    copies[7].wait_recv()
+    copies[9].wait_recv()
+    spread(2)
+    start_root(1, 1)
     pass_root(0, 1)
     pass_root(0, 2)
-    for slot in range(SLOTS):
-        pass_block(slot)
+    start_root(1, 2)
+    for slot in range(SLOTS):
+        arrive(1, slot)
+        block_copies[slot][0].start()
+        arrive(2, slot)
+        block_copies[slot][1].start()
     for slot in range(SLOTS):
         pass_root(1, slot)
 
@@ -471,7 +479,8 @@
     fetch_right.wait()
     powers = []
     for slot in range(SLOTS):
-        for copy in block_copies[slot][2:]:
+        arrive(0, slot)
+        for copy in block_copies[slot]:
             copy.wait_recv()
         grad = blocks[slot].reshape(BLK, BLK)
         precond[slot] = contract_last(grad, right_box[slot]).astype(bf16)
@@ -524,7 +533,8 @@
                 copy.wait_send()
             finish_all(functools.partial(back, slot, half))
         finish_all(functools.partial(tell, slot))
-        finish_all(functools.partial(piece, slot))
+        for origin in range(3):
+            finish_all(functools.partial(piece, origin, slot))
         for copy in block_copies[slot]:
             copy.wait_send()
         for copy in leave(slot):
@@ -559,9 +569,9 @@
             vmem((CUT, QROWS, BLK), bf16),
             vmem((NBC - CUT, QROWS, BLK), bf16),
         ]
-        + [vmem((NBC, QROWS, BLK), bf16)] * 3
+        + [vmem((NBC, QROWS, BLK), bf16)] * 5
         + [
-            vmem((SLOTS, SUBS, QROWS, BLK), bf16),
+            vmem((3, SLOTS, SUBS, QROWS, BLK), bf16),
             vmem((SLOTS, SUBS, N_X, QROWS, BLK), bf16),
             vmem((SLOTS, N_X, 2, HALVES, HROWS, BLK), bf16),
             vmem((SLOTS, 256, BLK), bf16),
@@ -581,15 +591,15 @@
             dma,
             dma,
             dma((SLOTS, 2)),
-            dma((6,)),
-            dma((6,)),
+            dma((10,)),
+            dma((10,)),
             dma((SLOTS, HALVES, 6)),
             dma((SLOTS, HALVES, 6)),
             dma((2,)),
-            dma((SLOTS, SUBS)),
-            dma((SLOTS,)),
-            dma((SLOTS, 6)),
-            dma((SLOTS, 6)),
+            dma((3, SLOTS, SUBS)),
+            dma((3, SLOTS)),
+            dma((SLOTS, 2)),
+            dma((SLOTS, 2)),
             dma((SLOTS, 3)),
             dma((SLOTS, 3)),
             dma((SLOTS, SUBS)),

time: 204 us -> 198 us (0.971)
  Pallas kernels: 203 us -> 197 us
    pallas_call x1, Pallas kernels: 192 us -> 186 us  [on_device(): pl.pallas_call(shampoo, in_specs=[smem] + [hbm] * 5, out_specs=[hbm] * 3,...]
where the time goes in v9:
time: 198 us; the launch traced here: 197 us
  Pallas kernels  197 us (99%)
    pallas_call x1, Pallas kernels, on_device(): pl.pallas_call(shampoo, in_specs=[smem] + [hbm] * 5, out_specs=[hbm] * 3,...  186 us
    pallas_call x1, Pallas kernels, on_device(): pl.pallas_call(deliver, in_specs=[hbm] * 3, out_specs=[hbm] * 3, out_shap...  10.6 us

profile of v9, /device:TPU:0, one launch (start us, length us, event | category | flops | bytes accessed | tf_op | source)
XLA Modules:
  0.0 197.5 jit_solution(11432701557062378177)
XLA Ops:
  0.6 186.2 %shampoo.1 = (f32[3,256,1024]{2,1,0:T(8,128)}, f32[3,256,1024]{2,1,0:T(8,128)}, bf16[1,1966080]{1,0:T(2,128)(2,1)}) custom-call(s32[3,32]{1,0:T(4,128)} %bitcast.15, bf16[1,1966080]{1,0:T(2,128)(2,1)} %grads.1, bf16[3,2,2,64,1024]{4,3,2,1,0:T(8,128)(2,1)} %bitcast.13, bf16[3,256,1024]{2,1,0:T(8,128)(2,1)} %bitcast.14, f32[3,256,1024]{2,1,0:T(8,128)} %bitcast.9, ...), custom_call_target="tpu_custom_call" | custom-call | tf_op jit(solution)/shard_map/shampoo/pallas_call | solution.py:554
  186.9 10.6 %deliver.1 = (bf16[1,1966080]{1,0:T(2,128)(2,1)}, f32[768,1024]{1,0:T(8,128)}, f32[768,1024]{1,0:T(8,128)}) custom-call(bf16[1,1966080]{1,0:T(2,128)(2,1)} %get-tuple-element.9.refs_0_, f32[768,1024]{1,0:T(8,128)} %bitcast.11, f32[768,1024]{1,0:T(8,128)} %bitcast.12), custom_call_target="tpu_custom_call" | custom-call | tf_op jit(solution)/shard_map/deliver/pallas_call | solution.py:623

commit v10 on v9

--- a/solution.py
+++ b/solution.py
@@ -261,7 +261,6 @@
     admitted()
     keep.start()
     copies[0].start()
-    start_root(0, 0)
     unpack(OVER, CUT, NBC)
     copies[1].start()
     loads[2].start()
@@ -291,28 +290,26 @@
     copies[7].start()
     copies[8].start()
     spread(0)
-    start_root(0, 1)
-    start_root(0, 2)
     lax.fori_loop(0, NBC, locate, 0)
-    pass_root(0, 0)
     copies[6].wait_recv()
     copies[8].wait_recv()
+    start_root(0, 0)
     spread(1)
-    start_root(1, 0)
     copies[7].wait_recv()
     copies[9].wait_recv()
+    start_root(0, 1)
     spread(2)
-    start_root(1, 1)
-    pass_root(0, 1)
-    pass_root(0, 2)
-    start_root(1, 2)
-    for slot in range(SLOTS):
+    start_root(0, 2)
+    for slot in range(SLOTS):
+        pass_root(0, slot)
+    for slot in range(SLOTS):
+        start_root(1, slot)
         arrive(1, slot)
         block_copies[slot][0].start()
         arrive(2, slot)
         block_copies[slot][1].start()
-    for slot in range(SLOTS):
-        pass_root(1, slot)
+    pass_root(1, 0)
+    pass_root(1, 1)
 
     def target_of(place, count):
         target_sub = lax.rem(3 * count + 3 * sub + 2 * row, SUBS)
@@ -485,6 +482,10 @@
         grad = blocks[slot].reshape(BLK, BLK)
         precond[slot] = contract_last(grad, right_box[slot]).astype(bf16)
         direct(0, slot)
+    pass_root(1, 2)
+    for slot in range(SLOTS):
+        grad = blocks[slot].reshape(BLK, BLK)
+        powers.append(jnp.sum(jnp.square(grad.astype(f32))) / (BLK * BLK))
     pltpu.make_async_copy(inbox_0, inbox_0, back_recv.at[0]).wait()
     place_group(0)
     ring_group(0)
@@ -500,9 +501,6 @@
     ring_group(2)
     place_group(3)
     ring_group(3)
-    for slot in range(SLOTS):
-        grad = blocks[slot].reshape(BLK, BLK)
-        powers.append(jnp.sum(jnp.square(grad.astype(f32))) / (BLK * BLK))
     for copy in shares:
         copy.wait_recv()
     for slot in range(SLOTS):

time: 198 us -> 199 us (level)
  no operation moved by 1% of the time
where the time goes in v10:
time: 199 us; the launch traced here: 198 us
  Pallas kernels  198 us (99%)
    pallas_call x1, Pallas kernels, on_device(): pl.pallas_call(shampoo, in_specs=[smem] + [hbm] * 5, out_specs=[hbm] * 3,...  187 us
    pallas_call x1, Pallas kernels, on_device(): pl.pallas_call(deliver, in_specs=[hbm] * 3, out_specs=[hbm] * 3, out_shap...  10.6 us

profile of v10, /device:TPU:0, one launch (start us, length us, event | category | flops | bytes accessed | tf_op | source)
XLA Modules:
  0.0 198.4 jit_solution(17140604134288081594)
XLA Ops:
  0.6 187.1 %shampoo.1 = (f32[3,256,1024]{2,1,0:T(8,128)}, f32[3,256,1024]{2,1,0:T(8,128)}, bf16[1,1966080]{1,0:T(2,128)(2,1)}) custom-call(s32[3,32]{1,0:T(4,128)} %bitcast.15, bf16[1,1966080]{1,0:T(2,128)(2,1)} %grads.1, bf16[3,2,2,64,1024]{4,3,2,1,0:T(8,128)(2,1)} %bitcast.13, bf16[3,256,1024]{2,1,0:T(8,128)(2,1)} %bitcast.14, f32[3,256,1024]{2,1,0:T(8,128)} %bitcast.9, ...), custom_call_target="tpu_custom_call" | custom-call | tf_op jit(solution)/shard_map/shampoo/pallas_call | solution.py:552
  187.8 10.6 %deliver.1 = (bf16[1,1966080]{1,0:T(2,128)(2,1)}, f32[768,1024]{1,0:T(8,128)}, f32[768,1024]{1,0:T(8,128)}) custom-call(bf16[1,1966080]{1,0:T(2,128)(2,1)} %get-tuple-element.9.refs_0_, f32[768,1024]{1,0:T(8,128)} %bitcast.11, f32[768,1024]{1,0:T(8,128)} %bitcast.12), custom_call_target="tpu_custom_call" | custom-call | tf_op jit(solution)/shard_map/deliver/pallas_call | solution.py:621

commit v11 on v10

--- a/solution.py
+++ b/solution.py
@@ -31,7 +31,7 @@
 STEP = 9
 HALVES = 2
 HROWS = 64
-PARTS = 4
+PARTS = 8
 
 
 def deliver(*refs):
@@ -303,7 +303,8 @@
     for slot in range(SLOTS):
         pass_root(0, slot)
     for slot in range(SLOTS):
-        start_root(1, slot)
+        if slot < SLOTS - 1:
+            start_root(1, slot)
         arrive(1, slot)
         block_copies[slot][0].start()
         arrive(2, slot)
@@ -474,15 +475,20 @@
 
     keep.wait()
     fetch_right.wait()
+    fetch_left_fac.wait()
+    fetch_right_fac.wait()
     powers = []
     for slot in range(SLOTS):
         arrive(0, slot)
         for copy in block_copies[slot]:
             copy.wait_recv()
+        if slot == SLOTS - 1:
+            start_root(1, slot)
         grad = blocks[slot].reshape(BLK, BLK)
         precond[slot] = contract_last(grad, right_box[slot]).astype(bf16)
         direct(0, slot)
-    pass_root(1, 2)
+        if slot == 0:
+            statistics(0)
     for slot in range(SLOTS):
         grad = blocks[slot].reshape(BLK, BLK)
         powers.append(jnp.sum(jnp.square(grad.astype(f32))) / (BLK * BLK))
@@ -490,12 +496,15 @@
     place_group(0)
     ring_group(0)
     place_group(1)
-    for slot in range(SLOTS):
-        direct(1, slot)
+    pass_root(1, 2)
+    direct(1, 0)
+    direct(1, 1)
+    statistics(1)
+    forward(0)
+    direct(1, 2)
     ring_group(1)
     for slot in range(SLOTS):
         share(slot)
-    forward(0)
     pltpu.make_async_copy(inbox_1, inbox_1, back_recv.at[1]).wait()
     place_group(2)
     ring_group(2)
@@ -506,16 +515,12 @@
     for slot in range(SLOTS):
         graft(slot)
     forward(1)
-    fetch_left_fac.wait()
-    fetch_right_fac.wait()
-    statistics(0)
+    statistics(2)
     forward(2)
-    statistics(1)
     pltpu.make_async_copy(factor_box, factor_box, factor_recv).wait()
     flatten(0)
+    forward(3)
     flatten(1)
-    forward(3)
-    statistics(2)
     flatten(2)
     flatten(3)
     flat_copy(2).wait()

time: 199 us -> 196 us (0.985)
  Pallas kernels: 198 us -> 195 us
    pallas_call x1, Pallas kernels: 187 us -> 185 us  [on_device(): pl.pallas_call(shampoo, in_specs=[smem] + [hbm] * 5, out_specs=[hbm] * 3,...]
where the time goes in v11:
time: 196 us
  Pallas kernels  195 us (99%)
    pallas_call x1, Pallas kernels, on_device(): pl.pallas_call(shampoo, in_specs=[smem] + [hbm] * 5, out_specs=[hbm] * 3,...  185 us
    pallas_call x1, Pallas kernels, on_device(): pl.pallas_call(deliver, in_specs=[hbm] * 3, out_specs=[hbm] * 3, out_shap...  10.6 us

profile of v11, /device:TPU:0, one launch (start us, length us, event | category | flops | bytes accessed | tf_op | source)
XLA Modules:
  0.0 196.1 jit_solution(3873058688246065557)
XLA Ops:
  0.6 184.9 %shampoo.1 = (f32[3,256,1024]{2,1,0:T(8,128)}, f32[3,256,1024]{2,1,0:T(8,128)}, bf16[1,1966080]{1,0:T(2,128)(2,1)}) custom-call(s32[3,32]{1,0:T(4,128)} %bitcast.15, bf16[1,1966080]{1,0:T(2,128)(2,1)} %grads.1, bf16[3,2,2,64,1024]{4,3,2,1,0:T(8,128)(2,1)} %bitcast.13, bf16[3,256,1024]{2,1,0:T(8,128)(2,1)} %bitcast.14, f32[3,256,1024]{2,1,0:T(8,128)} %bitcast.9, ...), custom_call_target="tpu_custom_call" | custom-call | tf_op jit(solution)/shard_map/shampoo/pallas_call | solution.py:557
  185.5 10.6 %deliver.1 = (bf16[1,1966080]{1,0:T(2,128)(2,1)}, f32[768,1024]{1,0:T(8,128)}, f32[768,1024]{1,0:T(8,128)}) custom-call(bf16[1,1966080]{1,0:T(2,128)(2,1)} %get-tuple-element.9.refs_0_, f32[768,1024]{1,0:T(8,128)} %bitcast.11, f32[768,1024]{1,0:T(8,128)} %bitcast.12), custom_call_target="tpu_custom_call" | custom-call | tf_op jit(solution)/shard_map/deliver/pallas_call | solution.py:626

commit v12 on v11

--- a/solution.py
+++ b/solution.py
@@ -22,6 +22,7 @@
 QROWS = 32
 CUT = 8
 GROUPS = 4
+SPLIT = 5
 MESH = pl.DeviceIdType.MESH
 f32 = jnp.float32
 bf16 = jnp.bfloat16
@@ -81,7 +82,7 @@
 def shampoo(
     table, grads, left, right, left_fac, right_fac, new_left, new_right, update,
     flat, mid, tiles, fwd_a, fwd_b, part_a, part_b, from_p, from_m,
-    sum_own, sum_down, sum_up, outbox, blocks, roots, right_box, precond,
+    sum_own, sum_down, outbox, blocks, roots, right_box, precond,
     sums, sum_box, factors, factor_box, raw, inbox_0, inbox_1, gathered, left_box, right_fac_box, places,
     flat_sem, right_sem, keep_sem, out_sem, send, recv, root_send, root_recv,
     fac_sem, piece_send, piece_recv, block_send, block_recv, sum_send, sum_recv, factor_send, factor_recv,
@@ -111,9 +112,7 @@
         remote(part_a, from_p.at[low], 4, down),
         remote(part_b, from_m.at[high], 5, up),
         remote(sum_own.at[low], sum_down.at[low], 6, up),
-        remote(sum_own.at[high], sum_up.at[high], 7, down),
-        remote(sum_own.at[high], sum_down.at[high], 8, up),
-        remote(sum_own.at[low], sum_up.at[low], 9, down),
+        remote(sum_own.at[high], sum_down.at[high], 7, up),
     ]
     def root(slot, half):
         mine, there = left.at[slot], roots.at[slot, me_x]
@@ -183,8 +182,8 @@
         home = lambda: pltpu.make_async_copy(src, dst, recv_sem)
         return target, away, home
 
-    sums_of = (sum_own, sum_down, sum_up)
-    from_of = (me_x, down, up)
+    sums_of = (sum_own, sum_down)
+    from_of = (me_x, down)
 
     def piece(origin, place, count):
         holder = lax.rem(count + me_s // NBR, SUBS) * NBR + lax.rem(row + NBR - place, NBR)
@@ -218,7 +217,11 @@
             ref = blocks.at[slot, subs, x_from]
             return cross(ref, ref, block_send.at[slot, place], block_recv.at[slot, place], x)
 
-        return [one(0, pl.ds(0, 4), down, up), one(1, pl.ds(4, 4), up, down)]
+        return [
+            one(0, pl.ds(0, SUBS), me_x, down),
+            one(1, pl.ds(0, SPLIT), down, up),
+            one(2, pl.ds(SPLIT, SUBS - SPLIT), up, down),
+        ]
 
     block_copies = [gather_block(slot) for slot in range(SLOTS)]
 
@@ -283,31 +286,31 @@
     copies[4].wait_recv()
     lax.fori_loop(0, CUT, add_all, 0)
     copies[6].start()
-    copies[9].start()
     copies[2].wait_recv()
     copies[5].wait_recv()
     lax.fori_loop(CUT, NBC, add_all, 0)
     copies[7].start()
-    copies[8].start()
     spread(0)
+    start_root(0, 0)
     lax.fori_loop(0, NBC, locate, 0)
     copies[6].wait_recv()
-    copies[8].wait_recv()
-    start_root(0, 0)
+    copies[7].wait_recv()
     spread(1)
-    copies[7].wait_recv()
-    copies[9].wait_recv()
+    for slot in range(SLOTS):
+        arrive(0, slot)
+        block_copies[slot][0].start()
     start_root(0, 1)
-    spread(2)
     start_root(0, 2)
-    for slot in range(SLOTS):
-        pass_root(0, slot)
+    pass_root(0, 0)
+    for slot in range(SLOTS):
+        block_copies[slot][0].wait_recv()
+        block_copies[slot][2].start()
+    pass_root(0, 1)
+    pass_root(0, 2)
     for slot in range(SLOTS):
         if slot < SLOTS - 1:
             start_root(1, slot)
         arrive(1, slot)
-        block_copies[slot][0].start()
-        arrive(2, slot)
         block_copies[slot][1].start()
     pass_root(1, 0)
     pass_root(1, 1)
@@ -479,8 +482,7 @@
     fetch_right_fac.wait()
     powers = []
     for slot in range(SLOTS):
-        arrive(0, slot)
-        for copy in block_copies[slot]:
+        for copy in block_copies[slot][1:]:
             copy.wait_recv()
         if slot == SLOTS - 1:
             start_root(1, slot)
@@ -536,7 +538,7 @@
                 copy.wait_send()
             finish_all(functools.partial(back, slot, half))
         finish_all(functools.partial(tell, slot))
-        for origin in range(3):
+        for origin in range(2):
             finish_all(functools.partial(piece, origin, slot))
         for copy in block_copies[slot]:
             copy.wait_send()
@@ -572,9 +574,9 @@
             vmem((CUT, QROWS, BLK), bf16),
             vmem((NBC - CUT, QROWS, BLK), bf16),
         ]
-        + [vmem((NBC, QROWS, BLK), bf16)] * 5
+        + [vmem((NBC, QROWS, BLK), bf16)] * 4
         + [
-            vmem((3, SLOTS, SUBS, QROWS, BLK), bf16),
+            vmem((2, SLOTS, SUBS, QROWS, BLK), bf16),
             vmem((SLOTS, SUBS, N_X, QROWS, BLK), bf16),
             vmem((SLOTS, N_X, 2, HALVES, HROWS, BLK), bf16),
             vmem((SLOTS, 256, BLK), bf16),
@@ -594,15 +596,15 @@
             dma,
             dma,
             dma((SLOTS, 2)),
-            dma((10,)),
-            dma((10,)),
+            dma((8,)),
+            dma((8,)),
             dma((SLOTS, HALVES, 6)),
             dma((SLOTS, HALVES, 6)),
             dma((2,)),
-            dma((3, SLOTS, SUBS)),
-            dma((3, SLOTS)),
-            dma((SLOTS, 2)),
-            dma((SLOTS, 2)),
+            dma((2, SLOTS, SUBS)),
+            dma((2, SLOTS)),
+            dma((SLOTS, 3)),
+            dma((SLOTS, 3)),
             dma((SLOTS, 3)),
             dma((SLOTS, 3)),
             dma((SLOTS, SUBS)),

time: 196 us -> 218 us (1.11)
  Pallas kernels: 195 us -> 217 us
    pallas_call x1, Pallas kernels: 185 us -> 206 us  [on_device(): pl.pallas_call(shampoo, in_specs=[smem] + [hbm] * 5, out_specs=[hbm] * 3,...]
where the time goes in v12:
time: 218 us; the launch traced here: 217 us
  Pallas kernels  217 us (100%)
    pallas_call x1, Pallas kernels, on_device(): pl.pallas_call(shampoo, in_specs=[smem] + [hbm] * 5, out_specs=[hbm] * 3,...  206 us
    pallas_call x1, Pallas kernels, on_device(): pl.pallas_call(deliver, in_specs=[hbm] * 3, out_specs=[hbm] * 3, out_shap...  10.6 us

profile of v12, /device:TPU:0, one launch (start us, length us, event | category | flops | bytes accessed | tf_op | source)
XLA Modules:
  0.0 217.4 jit_solution(6597627703593514268)
XLA Ops:
  0.6 206.2 %shampoo.1 = (f32[3,256,1024]{2,1,0:T(8,128)}, f32[3,256,1024]{2,1,0:T(8,128)}, bf16[1,1966080]{1,0:T(2,128)(2,1)}) custom-call(s32[3,32]{1,0:T(4,128)} %bitcast.15, bf16[1,1966080]{1,0:T(2,128)(2,1)} %grads.1, bf16[3,2,2,64,1024]{4,3,2,1,0:T(8,128)(2,1)} %bitcast.13, bf16[3,256,1024]{2,1,0:T(8,128)(2,1)} %bitcast.14, f32[3,256,1024]{2,1,0:T(8,128)} %bitcast.9, ...), custom_call_target="tpu_custom_call" | custom-call | tf_op jit(solution)/shard_map/shampoo/pallas_call | solution.py:559
  206.8 10.6 %deliver.1 = (bf16[1,1966080]{1,0:T(2,128)(2,1)}, f32[768,1024]{1,0:T(8,128)}, f32[768,1024]{1,0:T(8,128)}) custom-call(bf16[1,1966080]{1,0:T(2,128)(2,1)} %get-tuple-element.9.refs_0_, f32[768,1024]{1,0:T(8,128)} %bitcast.11, f32[768,1024]{1,0:T(8,128)} %bitcast.12), custom_call_target="tpu_custom_call" | custom-call | tf_op jit(solution)/shard_map/deliver/pallas_call | solution.py:628

commit v13 on v11

--- a/solution.py
+++ b/solution.py
@@ -281,6 +281,7 @@
     unpack(OWN, 0, NBC)
     copies[3].wait_recv()
     copies[4].wait_recv()
+    start_root(0, 0)
     lax.fori_loop(0, CUT, add_all, 0)
     copies[6].start()
     copies[9].start()
@@ -290,16 +291,15 @@
     copies[7].start()
     copies[8].start()
     spread(0)
+    start_root(0, 1)
     lax.fori_loop(0, NBC, locate, 0)
     copies[6].wait_recv()
     copies[8].wait_recv()
-    start_root(0, 0)
     spread(1)
+    start_root(0, 2)
     copies[7].wait_recv()
     copies[9].wait_recv()
-    start_root(0, 1)
     spread(2)
-    start_root(0, 2)
     for slot in range(SLOTS):
         pass_root(0, slot)
     for slot in range(SLOTS):
@@ -497,12 +497,11 @@
     ring_group(0)
     place_group(1)
     pass_root(1, 2)
+    ring_group(1)
     direct(1, 0)
     direct(1, 1)
-    statistics(1)
     forward(0)
     direct(1, 2)
-    ring_group(1)
     for slot in range(SLOTS):
         share(slot)
     pltpu.make_async_copy(inbox_1, inbox_1, back_recv.at[1]).wait()
@@ -515,8 +514,9 @@
     for slot in range(SLOTS):
         graft(slot)
     forward(1)
+    statistics(1)
+    forward(2)
     statistics(2)
-    forward(2)
     pltpu.make_async_copy(factor_box, factor_box, factor_recv).wait()
     flatten(0)
     forward(3)

time: 196 us -> 200 us (1.020)
  Pallas kernels: 195 us -> 199 us
    pallas_call x1, Pallas kernels: 185 us -> 188 us  [on_device(): pl.pallas_call(shampoo, in_specs=[smem] + [hbm] * 5, out_specs=[hbm] * 3,...]
where the time goes in v13:
time: 200 us
  Pallas kernels  199 us (100%)
    pallas_call x1, Pallas kernels, on_device(): pl.pallas_call(shampoo, in_specs=[smem] + [hbm] * 5, out_specs=[hbm] * 3,...  188 us
    pallas_call x1, Pallas kernels, on_device(): pl.pallas_call(deliver, in_specs=[hbm] * 3, out_specs=[hbm] * 3, out_shap...  10.6 us

profile of v13, /device:TPU:0, one launch (start us, length us, event | category | flops | bytes accessed | tf_op | source)
XLA Modules:
  0.0 199.6 jit_solution(7705749115447964153)
XLA Ops:
  0.6 188.4 %shampoo.1 = (f32[3,256,1024]{2,1,0:T(8,128)}, f32[3,256,1024]{2,1,0:T(8,128)}, bf16[1,1966080]{1,0:T(2,128)(2,1)}) custom-call(s32[3,32]{1,0:T(4,128)} %bitcast.15, bf16[1,1966080]{1,0:T(2,128)(2,1)} %grads.1, bf16[3,2,2,64,1024]{4,3,2,1,0:T(8,128)(2,1)} %bitcast.13, bf16[3,256,1024]{2,1,0:T(8,128)(2,1)} %bitcast.14, f32[3,256,1024]{2,1,0:T(8,128)} %bitcast.9, ...), custom_call_target="tpu_custom_call" | custom-call | tf_op jit(solution)/shard_map/shampoo/pallas_call | solution.py:557
  189.1 10.6 %deliver.1 = (bf16[1,1966080]{1,0:T(2,128)(2,1)}, f32[768,1024]{1,0:T(8,128)}, f32[768,1024]{1,0:T(8,128)}) custom-call(bf16[1,1966080]{1,0:T(2,128)(2,1)} %get-tuple-element.9.refs_0_, f32[768,1024]{1,0:T(8,128)} %bitcast.11, f32[768,1024]{1,0:T(8,128)} %bitcast.12), custom_call_target="tpu_custom_call" | custom-call | tf_op jit(solution)/shard_map/deliver/pallas_call | solution.py:626

commit v14 on v11

--- a/solution.py
+++ b/solution.py
@@ -487,8 +487,8 @@
         grad = blocks[slot].reshape(BLK, BLK)
         precond[slot] = contract_last(grad, right_box[slot]).astype(bf16)
         direct(0, slot)
-        if slot == 0:
-            statistics(0)
+        if slot != 1:
+            statistics(slot)
     for slot in range(SLOTS):
         grad = blocks[slot].reshape(BLK, BLK)
         powers.append(jnp.sum(jnp.square(grad.astype(f32))) / (BLK * BLK))
@@ -497,14 +497,14 @@
     ring_group(0)
     place_group(1)
     pass_root(1, 2)
+    ring_group(1)
     direct(1, 0)
     direct(1, 1)
-    statistics(1)
     forward(0)
     direct(1, 2)
-    ring_group(1)
     for slot in range(SLOTS):
         share(slot)
+    statistics(1)
     pltpu.make_async_copy(inbox_1, inbox_1, back_recv.at[1]).wait()
     place_group(2)
     ring_group(2)
@@ -515,12 +515,11 @@
     for slot in range(SLOTS):
         graft(slot)
     forward(1)
-    statistics(2)
-    forward(2)
     pltpu.make_async_copy(factor_box, factor_box, factor_recv).wait()
     flatten(0)
+    forward(2)
+    flatten(1)
     forward(3)
-    flatten(1)
     flatten(2)
     flatten(3)
     flat_copy(2).wait()

time: 196 us -> 197 us (level)
  no operation moved by 1% of the time
where the time goes in v14:
time: 197 us
  Pallas kernels  196 us (99%)
    pallas_call x1, Pallas kernels, on_device(): pl.pallas_call(shampoo, in_specs=[smem] + [hbm] * 5, out_specs=[hbm] * 3,...  186 us
    pallas_call x1, Pallas kernels, on_device(): pl.pallas_call(deliver, in_specs=[hbm] * 3, out_specs=[hbm] * 3, out_shap...  10.6 us

profile of v14, /device:TPU:0, one launch (start us, length us, event | category | flops | bytes accessed | tf_op | source)
XLA Modules:
  0.0 197.1 jit_solution(8919552417930725100)
XLA Ops:
  0.6 185.9 %shampoo.1 = (f32[3,256,1024]{2,1,0:T(8,128)}, f32[3,256,1024]{2,1,0:T(8,128)}, bf16[1,1966080]{1,0:T(2,128)(2,1)}) custom-call(s32[3,32]{1,0:T(4,128)} %bitcast.15, bf16[1,1966080]{1,0:T(2,128)(2,1)} %grads.1, bf16[3,2,2,64,1024]{4,3,2,1,0:T(8,128)(2,1)} %bitcast.13, bf16[3,256,1024]{2,1,0:T(8,128)(2,1)} %bitcast.14, f32[3,256,1024]{2,1,0:T(8,128)} %bitcast.9, ...), custom_call_target="tpu_custom_call" | custom-call | tf_op jit(solution)/shard_map/shampoo/pallas_call | solution.py:556
  186.6 10.6 %deliver.1 = (bf16[1,1966080]{1,0:T(2,128)(2,1)}, f32[768,1024]{1,0:T(8,128)}, f32[768,1024]{1,0:T(8,128)}) custom-call(bf16[1,1966080]{1,0:T(2,128)(2,1)} %get-tuple-element.9.refs_0_, f32[768,1024]{1,0:T(8,128)} %bitcast.11, f32[768,1024]{1,0:T(8,128)} %bitcast.12), custom_call_target="tpu_custom_call" | custom-call | tf_op jit(solution)/shard_map/deliver/pallas_call | solution.py:625

commit v15 on v11

--- a/solution.py
+++ b/solution.py
@@ -91,6 +91,7 @@
     row, sub = me_s // SUBS, lax.rem(me_s, SUBS)
     up, down, over = lax.rem(me_x + 1, N_X), lax.rem(me_x + 3, N_X), lax.rem(me_x + 2, N_X)
     low, high = pl.ds(0, CUT), pl.ds(CUT, NBC - CUT)
+    top, bottom = pl.ds(0, 16), pl.ds(16, 16)
     inbox = (inbox_0, inbox_1)
     OVER, DOWN, UP, OWN = range(4)
 
@@ -110,10 +111,10 @@
         remote(tiles.at[UP, low], from_m.at[low], 3, up),
         remote(part_a, from_p.at[low], 4, down),
         remote(part_b, from_m.at[high], 5, up),
-        remote(sum_own.at[low], sum_down.at[low], 6, up),
-        remote(sum_own.at[high], sum_up.at[high], 7, down),
-        remote(sum_own.at[high], sum_down.at[high], 8, up),
-        remote(sum_own.at[low], sum_up.at[low], 9, down),
+        remote(sum_own.at[low, top], sum_down.at[low], 6, up),
+        remote(sum_own.at[high, top], sum_up.at[high], 7, down),
+        remote(sum_own.at[high, top], sum_down.at[high], 8, up),
+        remote(sum_own.at[low, top], sum_up.at[low], 9, down),
     ]
     def root(slot, half):
         mine, there = left.at[slot], roots.at[slot, me_x]
@@ -188,7 +189,9 @@
 
     def piece(origin, place, count):
         holder = lax.rem(count + me_s // NBR, SUBS) * NBR + lax.rem(row + NBR - place, NBR)
-        src, dst = outbox.at[origin, place, count], blocks.at[place, sub, from_of[origin]]
+        rows = pl.ds(0, QROWS) if origin == 0 else top
+        src = outbox.at[origin, place, count, rows]
+        dst = blocks.at[place, sub, from_of[origin], rows]
         return sender(
             src, dst, piece_send.at[origin, place, count], piece_recv.at[origin, place], holder
         )
@@ -199,7 +202,7 @@
             def step(count, carry):
                 holder, away, home = piece(origin, place, count)
                 block = table[place, holder]
-                outbox[origin, place, count] = sums_of[origin][lax.rem(jnp.maximum(block, 0), NBC)]
+                outbox[origin, place, count, : QROWS if origin == 0 else 16] = sums_of[origin][lax.rem(jnp.maximum(block, 0), NBC)]
 
                 @pl.when(holder != me_s)
                 def _():
@@ -214,16 +217,24 @@
             lax.fori_loop(0, SUBS, step, 0)
 
     def gather_block(slot):
-        def one(place, subs, x_from, x):
-            ref = blocks.at[slot, subs, x_from]
+        def one(place, subs, x_from, rows, x):
+            ref = blocks.at[slot, subs, x_from, rows]
             return cross(ref, ref, block_send.at[slot, place], block_recv.at[slot, place], x)
 
-        return [one(0, pl.ds(0, 4), down, up), one(1, pl.ds(4, 4), up, down)]
+        every_sub, first, second = pl.ds(0, 8), pl.ds(0, 4), pl.ds(4, 4)
+        return [
+            one(0, every_sub, me_x, bottom, up),
+            one(1, every_sub, me_x, bottom, down),
+            one(2, first, down, top, up),
+            one(3, second, up, top, down),
+            one(4, first, down, bottom, up),
+            one(5, second, up, bottom, down),
+        ]
 
     block_copies = [gather_block(slot) for slot in range(SLOTS)]
 
     def arrive(origin, slot):
-        pieces = blocks.at[slot, :, from_of[origin]]
+        pieces = blocks.at[slot, :, from_of[origin], pl.ds(0, QROWS) if origin == 0 else top]
         pltpu.make_async_copy(pieces, pieces, piece_recv.at[origin, slot]).wait()
 
     def locate(col, carry):
@@ -299,16 +310,25 @@
     copies[9].wait_recv()
     start_root(0, 1)
     spread(2)
+    for slot in range(SLOTS):
+        arrive(0, slot)
+        block_copies[slot][0].start()
+        block_copies[slot][1].start()
     start_root(0, 2)
-    for slot in range(SLOTS):
-        pass_root(0, slot)
+    pass_root(0, 0)
+    pass_root(0, 1)
+    for slot in range(SLOTS):
+        for place in range(2):
+            block_copies[slot][place].wait_recv()
+            block_copies[slot][place + 4].start()
+    pass_root(0, 2)
     for slot in range(SLOTS):
         if slot < SLOTS - 1:
             start_root(1, slot)
         arrive(1, slot)
-        block_copies[slot][0].start()
+        block_copies[slot][2].start()
         arrive(2, slot)
-        block_copies[slot][1].start()
+        block_copies[slot][3].start()
     pass_root(1, 0)
     pass_root(1, 1)
 
@@ -479,8 +499,7 @@
     fetch_right_fac.wait()
     powers = []
     for slot in range(SLOTS):
-        arrive(0, slot)
-        for copy in block_copies[slot]:
+        for copy in block_copies[slot][2:]:
             copy.wait_recv()
         if slot == SLOTS - 1:
             start_root(1, slot)
@@ -572,7 +591,8 @@
             vmem((CUT, QROWS, BLK), bf16),
             vmem((NBC - CUT, QROWS, BLK), bf16),
         ]
-        + [vmem((NBC, QROWS, BLK), bf16)] * 5
+        + [vmem((NBC, QROWS, BLK), bf16)] * 3
+        + [vmem((NBC, 16, BLK), bf16)] * 2
         + [
             vmem((3, SLOTS, SUBS, QROWS, BLK), bf16),
             vmem((SLOTS, SUBS, N_X, QROWS, BLK), bf16),
@@ -601,8 +621,8 @@
             dma((2,)),
             dma((3, SLOTS, SUBS)),
             dma((3, SLOTS)),
-            dma((SLOTS, 2)),
-            dma((SLOTS, 2)),
+            dma((SLOTS, 6)),
+            dma((SLOTS, 6)),
             dma((SLOTS, 3)),
             dma((SLOTS, 3)),
             dma((SLOTS, SUBS)),

time: 196 us -> 201 us (1.026)
  Pallas kernels: 195 us -> 201 us
    pallas_call x1, Pallas kernels: 185 us -> 190 us  [on_device(): pl.pallas_call(shampoo, in_specs=[smem] + [hbm] * 5, out_specs=[hbm] * 3,...]
where the time goes in v15:
time: 201 us
  Pallas kernels  201 us (100%)
    pallas_call x1, Pallas kernels, on_device(): pl.pallas_call(shampoo, in_specs=[smem] + [hbm] * 5, out_specs=[hbm] * 3,...  190 us
    pallas_call x1, Pallas kernels, on_device(): pl.pallas_call(deliver, in_specs=[hbm] * 3, out_specs=[hbm] * 3, out_shap...  10.6 us

profile of v15, /device:TPU:0, one launch (start us, length us, event | category | flops | bytes accessed | tf_op | source)
XLA Modules:
  0.0 201.1 jit_solution(6238600917141673240)
XLA Ops:
  0.6 189.9 %shampoo.1 = (f32[3,256,1024]{2,1,0:T(8,128)}, f32[3,256,1024]{2,1,0:T(8,128)}, bf16[1,1966080]{1,0:T(2,128)(2,1)}) custom-call(s32[3,32]{1,0:T(4,128)} %bitcast.15, bf16[1,1966080]{1,0:T(2,128)(2,1)} %grads.1, bf16[3,2,2,64,1024]{4,3,2,1,0:T(8,128)(2,1)} %bitcast.13, bf16[3,256,1024]{2,1,0:T(8,128)(2,1)} %bitcast.14, f32[3,256,1024]{2,1,0:T(8,128)} %bitcast.9, ...), custom_call_target="tpu_custom_call" | custom-call | tf_op jit(solution)/shard_map/shampoo/pallas_call | solution.py:576
  190.6 10.6 %deliver.1 = (bf16[1,1966080]{1,0:T(2,128)(2,1)}, f32[768,1024]{1,0:T(8,128)}, f32[768,1024]{1,0:T(8,128)}) custom-call(bf16[1,1966080]{1,0:T(2,128)(2,1)} %get-tuple-element.9.refs_0_, f32[768,1024]{1,0:T(8,128)} %bitcast.11, f32[768,1024]{1,0:T(8,128)} %bitcast.12), custom_call_target="tpu_custom_call" | custom-call | tf_op jit(solution)/shard_map/deliver/pallas_call | solution.py:646

commit v16 on v11

--- a/solution.py
+++ b/solution.py
@@ -292,8 +292,8 @@
     spread(0)
     lax.fori_loop(0, NBC, locate, 0)
     copies[6].wait_recv()
+    start_root(0, 0)
     copies[8].wait_recv()
-    start_root(0, 0)
     spread(1)
     copies[7].wait_recv()
     copies[9].wait_recv()

time: 196 us -> 197 us (level)
  no operation moved by 1% of the time
where the time goes in v16:
time: 197 us; the launch traced here: 196 us
  Pallas kernels  196 us (99%)
    pallas_call x1, Pallas kernels, on_device(): pl.pallas_call(shampoo, in_specs=[smem] + [hbm] * 5, out_specs=[hbm] * 3,...  185 us
    pallas_call x1, Pallas kernels, on_device(): pl.pallas_call(deliver, in_specs=[hbm] * 3, out_specs=[hbm] * 3, out_shap...  10.6 us

profile of v16, /device:TPU:0, one launch (start us, length us, event | category | flops | bytes accessed | tf_op | source)
XLA Modules:
  0.0 196.4 jit_solution(14635602449415017798)
XLA Ops:
  0.6 185.2 %shampoo.1 = (f32[3,256,1024]{2,1,0:T(8,128)}, f32[3,256,1024]{2,1,0:T(8,128)}, bf16[1,1966080]{1,0:T(2,128)(2,1)}) custom-call(s32[3,32]{1,0:T(4,128)} %bitcast.15, bf16[1,1966080]{1,0:T(2,128)(2,1)} %grads.1, bf16[3,2,2,64,1024]{4,3,2,1,0:T(8,128)(2,1)} %bitcast.13, bf16[3,256,1024]{2,1,0:T(8,128)(2,1)} %bitcast.14, f32[3,256,1024]{2,1,0:T(8,128)} %bitcast.9, ...), custom_call_target="tpu_custom_call" | custom-call | tf_op jit(solution)/shard_map/shampoo/pallas_call | solution.py:557
  185.8 10.6 %deliver.1 = (bf16[1,1966080]{1,0:T(2,128)(2,1)}, f32[768,1024]{1,0:T(8,128)}, f32[768,1024]{1,0:T(8,128)}) custom-call(bf16[1,1966080]{1,0:T(2,128)(2,1)} %get-tuple-element.9.refs_0_, f32[768,1024]{1,0:T(8,128)} %bitcast.11, f32[768,1024]{1,0:T(8,128)} %bitcast.12), custom_call_target="tpu_custom_call" | custom-call | tf_op jit(solution)/shard_map/deliver/pallas_call | solution.py:626
